TPU v7x, 128 devices: a whole 4x4x4 slice. The times are simulated.
128 devices in a mesh: dp: 16 (over y, x), expert: 8 (over z, core).
Axes of the slice: x: 4, y: 4, z: 4, core: 2. Of those that a mesh axis runs over, the one named last changes fastest.
Arguments:
- tokens: bfloat16 [16384, 1024], P(('dp', 'expert')), may hold values from -24 to 24
- segments: int32 [16, 1024], P('dp'), may hold values from 0 to 6, as said below
- routes: int32 [16384, 8], P(('dp', 'expert')), may hold values from 0 to 31, all different within a row; in each aligned block of 128 rows (0 to 127, 128 to 255, ...) at most 48 rows name the same one
- gain_attn: bfloat16 [1024], P(('dp', 'expert')), may hold values from 0.5 to 1.5
- gain_ffn: bfloat16 [1024], P(('dp', 'expert')), may hold values from 0.5 to 1.5
- w_query: bfloat16 [1024, 1024], P(('dp', 'expert')), may hold values from -0.1875 to 0.1875
- w_key: bfloat16 [1024, 512], P(('dp', 'expert')), may hold values from -0.1875 to 0.1875
- w_value: bfloat16 [1024, 512], P(('dp', 'expert')), may hold values from -0.1875 to 0.1875
- w_out: bfloat16 [1024, 1024], P(('dp', 'expert')), may hold values from -0.75 to 0.75
- w_router: bfloat16 [1024, 32], P(('dp', 'expert')), may hold values from -0.09375 to 0.09375
- w_gate: bfloat16 [32, 1024, 512], P('expert'), may hold values from -0.1875 to 0.1875
- w_up: bfloat16 [32, 1024, 512], P('expert'), may hold values from -0.1875 to 0.1875
- w_down: bfloat16 [32, 512, 1024], P('expert'), may hold values from -1 to 1
- cotangent: bfloat16 [16384, 1024], P(('dp', 'expert')), may hold values from -6 to 6
Outputs:
- output: bfloat16 [16384, 1024], P(('dp', 'expert'))
- input_grad: float32 [16384, 1024], P(('dp', 'expert'))
- gain_attn_grad: float32 [1024], P(('dp', 'expert'))
- gain_ffn_grad: float32 [1024], P(('dp', 'expert'))
- w_query_grad: float32 [1024, 1024], P(('dp', 'expert'))
- w_key_grad: float32 [1024, 512], P(('dp', 'expert'))
- w_value_grad: float32 [1024, 512], P(('dp', 'expert'))
- w_out_grad: float32 [1024, 1024], P(('dp', 'expert'))
- w_router_grad: float32 [1024, 32], P(('dp', 'expert'))
- w_gate_grad: float32 [32, 1024, 512], P('expert', 'dp')
- w_up_grad: float32 [32, 1024, 512], P('expert', 'dp')
- w_down_grad: float32 [32, 512, 1024], P('expert', 'dp')
Inputs may be any that keep to these rules, and one draw needn't show every extreme that they name: `segments`: along each row the numbers never fall and may skip values; one document covers at least positions 64 to 959, the others lie within the first and the last 64 positions. `routes`: each row names 8 different experts; within the rows of one device no expert is named more than 48 times, and in every draw some device's rows name some expert exactly 48 times.
All inputs are finite; a program needn't handle non-finite values.
Results may differ from a plain program's by a relative error of at most 0.02.
Values may be sent and summed in bfloat16 or wider, within the bound.
A program may use at most 128 MiB of HBM per device.

v0:
```python
import jax
import jax.numpy as jnp
from jax import lax
from jax.sharding import PartitionSpec as P

HEAD = 64


EPSILON = 1e-06


def rotary_tables(positions, half_width):
    inverse_freq = 10000.0 ** (-jnp.arange(half_width).astype(jnp.float32) / half_width)
    angles = positions.astype(jnp.float32)[:, None] * inverse_freq[None, :]
    return (jnp.cos(angles), jnp.sin(angles))


def rotate(values, cosine, sine_table):
    half_width = values.shape[-1] // 2
    first_half = values[..., :half_width]
    second_half = values[..., half_width:]
    cos_heads = cosine[:, None, :]
    sin_heads = sine_table[:, None, :]
    return jnp.concatenate(
        [
            first_half * cos_heads - second_half * sin_heads,
            second_half * cos_heads + first_half * sin_heads,
        ],
        axis=-1,
    )


def unrotate(values, cosine, sine_table):
    half_width = values.shape[-1] // 2
    first_half = values[..., :half_width]
    second_half = values[..., half_width:]
    cos_heads = cosine[:, None, :]
    sin_heads = sine_table[:, None, :]
    return jnp.concatenate(
        [
            first_half * cos_heads + second_half * sin_heads,
            second_half * cos_heads - first_half * sin_heads,
        ],
        axis=-1,
    )


def slot_tables(route_block, experts, capacity):
    entry_count = route_block.shape[0] * route_block.shape[1]
    flat_ids = route_block.reshape(-1)
    onehot = (flat_ids[:, None] == jnp.arange(experts, dtype=jnp.int32)[None, :]).astype(jnp.int32)
    slot_rank = jnp.sum(
        (jnp.cumsum(onehot, axis=0, dtype=jnp.int32) - 1) * onehot, axis=1, dtype=jnp.int32
    )
    entries = jnp.arange(entry_count, dtype=jnp.int32)
    slot_table = (
        jnp.full((experts, capacity), entry_count, jnp.int32).at[flat_ids, slot_rank].set(entries)
    )
    return (slot_table, slot_rank)


def lead_dot(factor_one, factor_two):
    return lax.dot_general(
        factor_one, factor_two, (((0,), (0,)), ((), ())), preferred_element_type=jnp.float32
    )


def tail_dot(factor_one, factor_two):
    return lax.dot_general(
        factor_one, factor_two, (((1,), (1,)), ((), ())), preferred_element_type=jnp.float32
    )


def norm_back(upstream, values, inverse, normed, norm_gain):
    gain_grad = jnp.sum(upstream * normed, axis=0)
    scaled = upstream * norm_gain
    inner_sum = jnp.mean(scaled * values, axis=-1, keepdims=True)
    return (scaled * inverse - values * inverse * inverse * inverse * inner_sum, gain_grad)


def masked_scores(rotated_query, key_per_head, row_mask):
    attention_scores = jnp.einsum(
        "oful,ifl->fuoi", rotated_query, key_per_head, preferred_element_type=jnp.float32
    ) * HEAD ** (-0.5)
    return jnp.where(row_mask[None, None], attention_scores, -1e30)


def shards(
    tokens,
    segments,
    routes,
    gain_attn,
    gain_ffn,
    w_query,
    w_key,
    w_value,
    w_out,
    w_router,
    w_gate,
    w_up,
    w_down,
    cotangent,
):
    local_rows, model_width = tokens.shape
    top_count = routes.shape[1]
    position_base = lax.axis_index("expert") * local_rows
    gains_a, gains_f, query_w, key_w, value_w, out_w, router_w = (
        lax.all_gather(gain_attn, ("dp", "expert"), axis=0, tiled=True),
        lax.all_gather(gain_ffn, ("dp", "expert"), axis=0, tiled=True),
        lax.all_gather(w_query, ("dp", "expert"), axis=0, tiled=True),
        lax.all_gather(w_key, ("dp", "expert"), axis=0, tiled=True),
        lax.all_gather(w_value, ("dp", "expert"), axis=0, tiled=True),
        lax.all_gather(w_out, ("dp", "expert"), axis=0, tiled=True),
        lax.all_gather(w_router, ("dp", "expert"), axis=0, tiled=True),
    )
    expert_total = router_w.shape[1]
    capacity = 3 * local_rows * top_count // (2 * expert_total)
    kv_heads = key_w.shape[1] // HEAD
    group_size = query_w.shape[1] // key_w.shape[1]
    score_scale = HEAD ** (-0.5)
    gain_one = gains_a.astype(jnp.float32)
    gain_two = gains_f.astype(jnp.float32)
    inputs = tokens.astype(jnp.float32)
    inverse_one = lax.rsqrt(jnp.mean(inputs * inputs, axis=-1, keepdims=True) + EPSILON)
    normed_one = inputs * inverse_one
    hidden_one = (normed_one * gain_one).astype(jnp.bfloat16)
    positions = position_base + jnp.arange(local_rows, dtype=jnp.int32)
    cosine, sine_table = rotary_tables(positions, HEAD // 2)
    query_full = jnp.dot(hidden_one, query_w, preferred_element_type=jnp.float32).reshape(
        local_rows, -1, HEAD
    )
    rotated_query = (
        rotate(query_full, cosine, sine_table)
        .astype(jnp.bfloat16)
        .reshape(local_rows, kv_heads, group_size, HEAD)
    )
    key_full = jnp.dot(hidden_one, key_w, preferred_element_type=jnp.float32).reshape(
        local_rows, kv_heads, HEAD
    )
    rotated_key = (
        rotate(key_full, cosine, sine_table)
        .astype(jnp.bfloat16)
        .reshape(local_rows, kv_heads * HEAD)
    )
    value_low = jnp.dot(hidden_one, value_w, preferred_element_type=jnp.float32).astype(
        jnp.bfloat16
    )
    keys_all, value_complete = (
        lax.all_gather(rotated_key, "expert", axis=0, tiled=True),
        lax.all_gather(value_low, "expert", axis=0, tiled=True),
    )
    seq_len = keys_all.shape[0]
    segment_row = segments[0]
    query_seg = lax.dynamic_slice_in_dim(segment_row, position_base, local_rows)
    key_pos = jnp.arange(seq_len, dtype=jnp.int32)
    row_mask = (segment_row[None, :] == query_seg[:, None]) & (
        key_pos[None, :] <= positions[:, None]
    )
    attention_scores = masked_scores(
        rotated_query, keys_all.reshape(seq_len, kv_heads, HEAD), row_mask
    )
    maxima = jnp.max(attention_scores, axis=-1, keepdims=True)
    numerators = jnp.exp(attention_scores - maxima)
    totals = jnp.sum(numerators, axis=-1, keepdims=True)
    weights_low = (numerators / totals).astype(jnp.bfloat16)
    log_total = maxima + jnp.log(totals)
    attended = (
        jnp.einsum(
            "iazd,diu->ziau",
            weights_low,
            value_complete.reshape(seq_len, kv_heads, HEAD),
            preferred_element_type=jnp.float32,
        )
        .reshape(local_rows, -1)
        .astype(jnp.bfloat16)
    )
    residual = inputs + jnp.dot(attended, out_w, preferred_element_type=jnp.float32)
    inverse_two = lax.rsqrt(jnp.mean(residual * residual, axis=-1, keepdims=True) + EPSILON)
    normed_two = residual * inverse_two
    hidden_two = (normed_two * gain_two).astype(jnp.bfloat16)
    logits = jnp.dot(hidden_two, router_w, preferred_element_type=jnp.float32)
    route_match = (
        routes[:, :, None] == jnp.arange(expert_total, dtype=jnp.int32)[None, None, :]
    ).astype(jnp.float32)
    chosen = jnp.sum(route_match * logits[:, None, :], axis=-1)
    gate_weights = jax.nn.softmax(chosen, axis=-1)
    slot_table, slot_rank = slot_tables(routes, expert_total, capacity)
    token_rows = slot_table // top_count
    padded = jnp.concatenate([hidden_two, jnp.zeros((1, model_width), jnp.bfloat16)], axis=0)
    send_rows = padded[token_rows]
    rows_in = lax.all_to_all(send_rows, "expert", split_axis=0, concat_axis=1, tiled=True)
    gate_pre = jnp.einsum("emd,edf->emf", rows_in, w_gate, preferred_element_type=jnp.float32)
    up_pre = jnp.einsum("emd,edf->emf", rows_in, w_up, preferred_element_type=jnp.float32)
    product = (jax.nn.silu(gate_pre) * up_pre).astype(jnp.bfloat16)
    expert_out = jnp.einsum(
        "emf,efd->emd", product, w_down, preferred_element_type=jnp.float32
    ).astype(jnp.bfloat16)
    returned = lax.all_to_all(expert_out, "expert", split_axis=1, concat_axis=0, tiled=True)
    route_index = routes * capacity + slot_rank.reshape(local_rows, top_count)
    route_rows = returned.reshape(expert_total * capacity, model_width)[route_index]
    output = residual + jnp.sum(gate_weights[:, :, None] * route_rows.astype(jnp.float32), axis=1)
    upstream = cotangent.astype(jnp.float32)
    route_grad = (gate_weights[:, :, None] * upstream[:, None, :]).astype(jnp.bfloat16)
    gate_grad = jnp.sum(upstream[:, None, :] * route_rows.astype(jnp.float32), axis=-1)
    chosen_grad = gate_weights * (
        gate_grad - jnp.sum(gate_weights * gate_grad, axis=-1, keepdims=True)
    )
    logit_grad = jnp.sum(route_match * chosen_grad[:, :, None], axis=1).astype(jnp.bfloat16)
    router_grad = lead_dot(hidden_two, logit_grad)
    hidden_grad = tail_dot(logit_grad, router_w)
    entry_count = local_rows * top_count
    grad_rows = jnp.concatenate(
        [route_grad.reshape(entry_count, model_width), jnp.zeros((1, model_width), jnp.bfloat16)],
        axis=0,
    )[slot_table]
    grad_in = lax.all_to_all(grad_rows, "expert", split_axis=0, concat_axis=1, tiled=True)
    rows_again, gate_back, up_back, product_back = (rows_in, gate_pre, up_pre, product)
    down_grad = jnp.einsum(
        "emf,emd->efd", product_back, grad_in, preferred_element_type=jnp.float32
    )
    product_grad = jnp.einsum("emd,efd->emf", grad_in, w_down, preferred_element_type=jnp.float32)
    sigmoid_gate = jax.nn.sigmoid(gate_back)
    gate_low = (
        product_grad * up_back * sigmoid_gate * (1.0 + gate_back * (1.0 - sigmoid_gate))
    ).astype(jnp.bfloat16)
    up_low = (product_grad * gate_back * sigmoid_gate).astype(jnp.bfloat16)
    gate_w_grad = jnp.einsum(
        "emd,emf->edf", rows_again, gate_low, preferred_element_type=jnp.float32
    )
    up_w_grad = jnp.einsum("emd,emf->edf", rows_again, up_low, preferred_element_type=jnp.float32)
    slot_grads = (
        jnp.einsum("emf,edf->emd", gate_low, w_gate, preferred_element_type=jnp.float32)
        + jnp.einsum("emf,edf->emd", up_low, w_up, preferred_element_type=jnp.float32)
    ).astype(jnp.bfloat16)
    grads_back = lax.all_to_all(slot_grads, "expert", split_axis=1, concat_axis=0, tiled=True)
    hidden_grad = hidden_grad + jnp.sum(
        grads_back.reshape(expert_total * capacity, model_width)[route_index].astype(jnp.float32),
        axis=1,
    )
    gate_sum, up_sum, down_sum = (
        lax.psum_scatter(
            gate_w_grad.astype(jnp.bfloat16), "dp", scatter_dimension=1, tiled=True
        ).astype(jnp.float32),
        lax.psum_scatter(
            up_w_grad.astype(jnp.bfloat16), "dp", scatter_dimension=1, tiled=True
        ).astype(jnp.float32),
        lax.psum_scatter(
            down_grad.astype(jnp.bfloat16), "dp", scatter_dimension=1, tiled=True
        ).astype(jnp.float32),
    )
    resid_grad, gain_two_grad = norm_back(hidden_grad, residual, inverse_two, normed_two, gain_two)
    resid_grad = resid_grad + upstream
    branch_grad = resid_grad.astype(jnp.bfloat16)
    out_grad = lead_dot(attended, branch_grad)
    attention_output_grad = (
        tail_dot(branch_grad, out_w)
        .astype(jnp.bfloat16)
        .reshape(local_rows, kv_heads, group_size, HEAD)
    )
    keys_back, values_back = (
        lax.all_gather(rotated_key, "expert", axis=0, tiled=True),
        lax.all_gather(value_low, "expert", axis=0, tiled=True),
    )
    key_per_head = keys_back.reshape(seq_len, kv_heads, HEAD)
    value_per_head = values_back.reshape(seq_len, kv_heads, HEAD)
    attention_scores = masked_scores(rotated_query, key_per_head, row_mask)
    probabilities = jnp.exp(attention_scores - log_total)
    probability_reduced = probabilities.astype(jnp.bfloat16)
    prob_grad = jnp.einsum(
        "oful,ifl->fuoi", attention_output_grad, value_per_head, preferred_element_type=jnp.float32
    )
    inner_sum = jnp.sum(probabilities * prob_grad, axis=-1, keepdims=True)
    attention_score_grad = (probabilities * (prob_grad - inner_sum)).astype(jnp.bfloat16)
    query_grad = (
        jnp.einsum(
            "iazd,diu->ziau", attention_score_grad, key_per_head, preferred_element_type=jnp.float32
        )
        * score_scale
    )
    key_grad = (
        jnp.einsum(
            "wlea,ewlk->awk",
            attention_score_grad,
            rotated_query,
            preferred_element_type=jnp.float32,
        )
        * score_scale
    )
    value_grad = jnp.einsum(
        "wlea,ewlk->awk",
        probability_reduced,
        attention_output_grad,
        preferred_element_type=jnp.float32,
    )
    key_mine, value_mine = (
        lax.psum_scatter(
            key_grad.reshape(seq_len, -1).astype(jnp.bfloat16),
            "expert",
            scatter_dimension=0,
            tiled=True,
        ).astype(jnp.float32),
        lax.psum_scatter(
            value_grad.reshape(seq_len, -1).astype(jnp.bfloat16),
            "expert",
            scatter_dimension=0,
            tiled=True,
        ).astype(jnp.float32),
    )
    query_pre = (
        unrotate(query_grad.reshape(local_rows, -1, HEAD), cosine, sine_table)
        .reshape(local_rows, -1)
        .astype(jnp.bfloat16)
    )
    key_pre = (
        unrotate(key_mine.reshape(local_rows, kv_heads, HEAD), cosine, sine_table)
        .reshape(local_rows, -1)
        .astype(jnp.bfloat16)
    )
    value_pre = value_mine.astype(jnp.bfloat16)
    query_w_grad = lead_dot(hidden_one, query_pre)
    key_w_grad = lead_dot(hidden_one, key_pre)
    value_w_grad = lead_dot(hidden_one, value_pre)
    hidden_one_grad = (
        tail_dot(query_pre, query_w) + tail_dot(key_pre, key_w) + tail_dot(value_pre, value_w)
    )
    input_grad, gain_one_grad = norm_back(
        hidden_one_grad, inputs, inverse_one, normed_one, gain_one
    )
    input_grad = input_grad + resid_grad
    dense_sums = (
        lax.psum_scatter(gain_one_grad, ("dp", "expert"), scatter_dimension=0, tiled=True),
        lax.psum_scatter(gain_two_grad, ("dp", "expert"), scatter_dimension=0, tiled=True),
        lax.psum_scatter(query_w_grad, ("dp", "expert"), scatter_dimension=0, tiled=True),
        lax.psum_scatter(key_w_grad, ("dp", "expert"), scatter_dimension=0, tiled=True),
        lax.psum_scatter(value_w_grad, ("dp", "expert"), scatter_dimension=0, tiled=True),
        lax.psum_scatter(out_grad, ("dp", "expert"), scatter_dimension=0, tiled=True),
        lax.psum_scatter(router_grad, ("dp", "expert"), scatter_dimension=0, tiled=True),
    )
    return (
        output.astype(jnp.bfloat16),
        input_grad,
        dense_sums[0],
        dense_sums[1],
        dense_sums[2],
        dense_sums[3],
        dense_sums[4],
        dense_sums[5],
        dense_sums[6],
        gate_sum,
        up_sum,
        down_sum,
    )


def solution(mesh):
    return jax.shard_map(
        shards,
        mesh=mesh,
        in_specs=(
            P(("dp", "expert"), None),
            P("dp", None),
            P(("dp", "expert"), None),
            P(("dp", "expert")),
            P(("dp", "expert")),
            P(("dp", "expert"), None),
            P(("dp", "expert"), None),
            P(("dp", "expert"), None),
            P(("dp", "expert"), None),
            P(("dp", "expert"), None),
            P("expert", None, None),
            P("expert", None, None),
            P("expert", None, None),
            P(("dp", "expert"), None),
        ),
        out_specs=(
            P(("dp", "expert"), None),
            P(("dp", "expert"), None),
            P(("dp", "expert")),
            P(("dp", "expert")),
            P(("dp", "expert"), None),
            P(("dp", "expert"), None),
            P(("dp", "expert"), None),
            P(("dp", "expert"), None),
            P(("dp", "expert"), None),
            P("expert", "dp", None),
            P("expert", "dp", None),
            P("expert", "dp", None),
        ),
        check_vma=False,
    )
```

profile of v0, /device:TPU:1, one launch (start us, length us, event | category | flops | bytes accessed | tf_op | source)
XLA Modules:
  0.0 3562.0 jit_solution(2261180904936219062)
XLA Ops:
  10.5 69.4 %all-reduce.8 = (bf16[1024]{0:T(1024)(128)(2,1)S(1)}, bf16[1024]{0:T(1024)(128)(2,1)S(1)}) all-reduce(bf16[1024]{0:T(1024)(128)(2,1)S(1)} %dynamic-update-slice, bf16[1024]{0:T(1024)(128)(2,1)S(1)} %dynamic-update-slice.1), channel_id=1, replica_groups=mesh['dp'=16,'expert'=8] {'dp','expert'}, use_global_device_ids=true, to_apply=%add.2 | all-reduce | flops 2048 | bytes 8192
  84.2 57.8 %all-gather.11.cloned.1.call-done = bf16[1024,512]{1,0:T(8,128)(2,1)} async-done(((bf16[8,512]{1,0:T(8,128)(2,1)}), bf16[1024,512]{1,0:T(8,128)(2,1)}) %all-gather.11.cloned.1.call-update) | async-done | bytes 1048592 | tf_op jit(solution)/shard_map/all_gather | solution.py:111
  145.7 9.0 reduce-window.6
  160.0 34.0 all_gather.37
  195.8 38.1 %all-gather.15.cloned.1.call-done = bf16[1024,1024]{1,0:T(8,128)(2,1)} async-done(((bf16[8,1024]{1,0:T(8,128)(2,1)}), bf16[1024,1024]{1,0:T(8,128)(2,1)}) %all-gather.15.cloned.1.call-update) | async-done | bytes 2097168 | tf_op jit(solution)/shard_map/all_gather | solution.py:110
  236.6 20.4 all-gather.13.cloned.1.call-done
  264.6 61.6 %all-gather.17.cloned.1.call-done = bf16[1024,1024]{1,0:T(8,128)(2,1)} async-done(((bf16[8,1024]{1,0:T(8,128)(2,1)}), bf16[1024,1024]{1,0:T(8,128)(2,1)}) %all-gather.17.cloned.1.call-update) | async-done | bytes 2097168 | tf_op jit(solution)/shard_map/all_gather | solution.py:113
  330.6 5.8 gather_fusion.2
  341.1 5.8 gather_fusion
  347.0 31.8 all-to-all-done.2
  386.4 35.3 all-to-all-done
  455.6 26.9 all-to-all-done.1
  504.1 23.0 all-to-all-done.3
  569.1 5.8 convolution_convert_fusion
  592.0 17.5 reduce-scatter.28.cloned.1.call-done
  625.8 135.9 %all-reduce.11.cloned.1.call-done = f32[1024,32]{1,0:T(8,128)} async-done(((f32[1024,32]{1,0:T(8,128)}), f32[1024,32]{1,0:T(8,128)}) %all-reduce.11.cloned.1.call-update) | async-done | bytes 131088
  766.7 64.8 %all-reduce.7 = (f32[1024]{0:T(1024)S(1)}, f32[1024]{0:T(1024)S(1)}) all-reduce(f32[1024]{0:T(1024)S(1)} %get-tuple-element.16, f32[1024]{0:T(1024)S(1)} %copy-done.47), channel_id=4, replica_groups=mesh['dp'=16,'expert'=8] {'dp','expert'}, use_global_device_ids=true, to_apply=%region_22.23.clone | all-reduce | flops 2048 | bytes 16384
  833.6 6.0 reduce-scatter.26.cloned.1.call-done
  841.4 78.6 %reduce-scatter.24.cloned.1.call-done = bf16[4,64,512]{2,1,0:T(8,128)(2,1)} async-done(((bf16[4,1024,512]{2,1,0:T(8,128)(2,1)}), bf16[4,64,512]{2,1,0:T(8,128)(2,1)}) %reduce-scatter.24.cloned.1.call-update) | async-done | bytes 262160 | tf_op jit(solution)/shard_map/reduce_scatter | solution.py:244
  921.8 78.7 %reduce-scatter.22.cloned.1.call-done = bf16[4,64,512]{2,1,0:T(8,128)(2,1)} async-done(((bf16[4,1024,512]{2,1,0:T(8,128)(2,1)}), bf16[4,64,512]{2,1,0:T(8,128)(2,1)}) %reduce-scatter.22.cloned.1.call-update) | async-done | bytes 262160 | tf_op jit(solution)/shard_map/reduce_scatter | solution.py:241
  1002.3 635.1 %reduce-scatter.18.cloned.1.call-done = f32[8,512]{1,0:T(8,128)} async-done(((f32[1024,512]{1,0:T(8,128)}), f32[8,512]{1,0:T(8,128)}) %reduce-scatter.18.cloned.1.call-update) | async-done | bytes 16400 | tf_op jit(solution)/shard_map/reduce_scatter | solution.py:335
  1637.4 636.2 %reduce-scatter.16.cloned.1.call-done = f32[8,512]{1,0:T(8,128)} async-done(((f32[1024,512]{1,0:T(8,128)}), f32[8,512]{1,0:T(8,128)}) %reduce-scatter.16.cloned.1.call-update) | async-done | bytes 16400 | tf_op jit(solution)/shard_map/reduce_scatter | solution.py:334
  2273.7 640.8 %reduce-scatter.20.cloned.1.call-done = f32[8,1024]{1,0:T(8,128)} async-done(((f32[1024,1024]{1,0:T(8,128)}), f32[8,1024]{1,0:T(8,128)}) %reduce-scatter.20.cloned.1.call-update) | async-done | bytes 32784 | tf_op jit(solution)/shard_map/reduce_scatter | solution.py:336
  2914.4 640.9 %reduce-scatter.14.cloned.1.call-done = f32[8,1024]{1,0:T(8,128)} async-done(((f32[1024,1024]{1,0:T(8,128)}), f32[8,1024]{1,0:T(8,128)}) %reduce-scatter.14.cloned.1.call-update) | async-done | bytes 32784 | tf_op jit(solution)/shard_map/reduce_scatter | solution.py:333
  (282 shorter events, 187.5 us)
Async XLA Ops:
  7.2 152.7 %copy-start.28 = (bf16[128,1024]{1,0:T(8,128)(2,1)S(1)}, bf16[128,1024]{1,0:T(8,128)(2,1)}, u32[]{:S(2)}) copy-start(bf16[128,1024]{1,0:T(8,128)(2,1)} %param.27) | copy-start | bytes 786436
  7.2 73.8 %all-gather.7.cloned.1.call-start = ((), (), s32[]{:S(2)}) async-start(), calls=%async_computation.13 | async-start | bytes 1056768 | tf_op jit(solution)/shard_map/all_gather | solution.py:112
  8.0 134.0 %all-gather.11.cloned.1.call-start = ((), (), s32[]{:S(2)}) async-start(), calls=%async_computation.15 | async-start | bytes 1056768 | tf_op jit(solution)/shard_map/all_gather | solution.py:111
  8.7 185.6 %all-gather.9.cloned.1.call-start = ((), (), s32[]{:S(2)}) async-start(), calls=%async_computation.14 | async-start | bytes 1179648 | tf_op jit(solution)/shard_map/all_gather | solution.py:150
  81.0 152.9 %copy-start.45 = (f32[128]{0:T(128)}, f32[128]{0:T(128)S(1)}, u32[]{:S(2)}) copy-start(f32[128]{0:T(128)S(1)} %add_rsqrt_fusion.1) | copy-start | bytes 1540
  83.4 150.5 %all-gather.15.cloned.1.call-start = ((), (), s32[]{:S(2)}) async-start(), calls=%async_computation.17 | async-start | bytes 2113536 | tf_op jit(solution)/shard_map/all_gather | solution.py:110
  84.0 173.1 %all-gather.13.cloned.1.call-start = ((), (), s32[]{:S(2)}) async-start(), calls=%async_computation.16 | async-start | bytes 1179648 | tf_op jit(solution)/shard_map/all_gather | solution.py:149
  144.7 181.5 %all-gather.17.cloned.1.call-start = ((), (), s32[]{:S(2)}) async-start(), calls=%async_computation.18 | async-start | bytes 2113536 | tf_op jit(solution)/shard_map/all_gather | solution.py:113
  145.6 182.7 %copy-start.40 = (f32[1024]{0:T(1024)}, f32[1024]{0:T(1024)S(1)}, u32[]{:S(2)}) copy-start(f32[1024]{0:T(1024)S(1)} %convert_element_type.162) | copy-start | bytes 12292
  160.0 169.8 %copy-start.19 = (f32[128,1024]{1,0:T(8,128)}, f32[128,1024]{1,0:T(8,128)S(1)}, u32[]{:S(2)}) copy-start(f32[128,1024]{1,0:T(8,128)S(1)} %convert_element_type.169) | copy-start | bytes 1572868
  336.4 42.3 %all-to-all-start.2 = ((bf16[32,48,1024]{2,1,0:T(8,128)(2,1)}), bf16[32,48,1024]{2,1,0:T(8,128)(2,1)}, u32[]{:S(2)}, u32[]{:S(2)}) async-start(bf16[32,48,1024]{2,1,0:T(8,128)(2,1)} %bitcast.160), calls=%async_computation.2 | async-start | bytes 6291456 | tf_op jit(solution)/shard_map/all_to_all | solution.py:216
  378.7 43.1 %all-to-all-start = ((bf16[32,48,1024]{2,1,0:T(8,128)(2,1)}), bf16[32,48,1024]{2,1,0:T(8,128)(2,1)}, u32[]{:S(2)}, u32[]{:S(2)}) async-start(bf16[32,48,1024]{2,1,0:T(8,128)(2,1)} %bitcast.161), calls=%async_computation | async-start | bytes 6291456 | tf_op jit(solution)/shard_map/all_to_all | solution.py:191
  440.3 42.2 %all-to-all-start.1 = ((bf16[4,384,1024]{2,0,1:T(4,128)(2,1)}), bf16[4,384,1024]{2,0,1:T(4,128)(2,1)S(1)}, u32[]{:S(2)}, u32[]{:S(2)}) async-start(bf16[4,384,1024]{2,0,1:T(4,128)(2,1)} %copy.162), calls=%async_computation.1 | async-start | bytes 6291456 | tf_op jit(solution)/shard_map/all_to_all | solution.py:198
  484.2 42.9 %all-to-all-start.3 = ((bf16[4,384,1024]{2,0,1:T(4,128)(2,1)}), bf16[4,384,1024]{2,0,1:T(4,128)(2,1)}, u32[]{:S(2)}, u32[]{:S(2)}) async-start(bf16[4,384,1024]{2,0,1:T(4,128)(2,1)} %copy.170), calls=%async_computation.3 | async-start | bytes 6291456 | tf_op jit(solution)/shard_map/all_to_all | solution.py:235
  489.4 99.2 %reduce-scatter.30.cloned.1.call-start = ((), (), s32[]{:S(2)}) async-start(), calls=%async_computation.27 | async-start | bytes 1179648
  549.8 59.7 %reduce-scatter.28.cloned.1.call-start = ((), (), s32[]{:S(2)}) async-start(), calls=%async_computation.26 | async-start | bytes 1179648
  567.0 194.7 %all-reduce.11.cloned.1.call-start = ((), (), s32[]{:S(2)}) async-start(), calls=%async_computation.28 | async-start | bytes 1048576
  569.1 270.6 %reduce-scatter.26.cloned.1.call-start = ((), (), s32[]{:S(2)}) async-start(), calls=%async_computation.25 | async-start | bytes 4456448 | tf_op jit(solution)/shard_map/reduce_scatter | solution.py:247
  575.0 345.0 %reduce-scatter.24.cloned.1.call-start = ((), (), s32[]{:S(2)}) async-start(), calls=%async_computation.24 | async-start | bytes 4456448 | tf_op jit(solution)/shard_map/reduce_scatter | solution.py:244
  582.6 417.9 %reduce-scatter.22.cloned.1.call-start = ((), (), s32[]{:S(2)}) async-start(), calls=%async_computation.23 | async-start | bytes 4456448 | tf_op jit(solution)/shard_map/reduce_scatter | solution.py:241
  588.5 1048.9 %reduce-scatter.18.cloned.1.call-start = ((), (), s32[]{:S(2)}) async-start(), calls=%async_computation.21 | async-start | bytes 2113536 | tf_op jit(solution)/shard_map/reduce_scatter | solution.py:335
  591.9 1681.7 %reduce-scatter.16.cloned.1.call-start = ((), (), s32[]{:S(2)}) async-start(), calls=%async_computation.20 | async-start | bytes 2113536 | tf_op jit(solution)/shard_map/reduce_scatter | solution.py:334
  612.6 2301.8 %reduce-scatter.20.cloned.1.call-start = ((), (), s32[]{:S(2)}) async-start(), calls=%async_computation.22 | async-start | bytes 4227072 | tf_op jit(solution)/shard_map/reduce_scatter | solution.py:336
  615.5 2939.8 %reduce-scatter.14.cloned.1.call-start = ((), (), s32[]{:S(2)}) async-start(), calls=%async_computation.19 | async-start | bytes 4227072 | tf_op jit(solution)/shard_map/reduce_scatter | solution.py:333
  (55 other events, 1842.7 us)
Sparse Core Ops, SparseCore 0:
  10.8 67.2 all-gather.6
  80.9 61.0 all-gather.10
  144.3 21.1 all-gather.8
  168.4 65.3 all-gather.14
  236.0 20.9 all-gather.12
  260.0 66.1 all-gather.16
  549.9 26.3 reduce-scatter.29
  578.7 30.7 reduce-scatter.27
  614.9 146.8 all-reduce.10
  765.2 74.3 reduce-scatter.25
  843.0 76.9 reduce-scatter.23
  923.5 76.9 reduce-scatter.21
  1003.4 633.9 reduce-scatter.17
  1640.3 633.2 reduce-scatter.15
  2276.4 637.9 reduce-scatter.19
  2917.3 637.9 reduce-scatter.13
where the time goes:
time: 3570 us; the launch traced here: 3560 us
  waiting for transfers between devices  3170 us (89%)
  blocking collectives  168 us (5%)
  matrix products  83 us (2%)
  local copies, waits for them, and re-layouts  72.9 us (2%)
    reduce_scatter x1, waiting for transfers between devices, shards(): lax.psum_scatter(query_w_grad, ('dp', 'expert'), scatter_dimension=0, til...  641 us
    reduce_scatter x1, waiting for transfers between devices, shards(): lax.psum_scatter(out_grad, ('dp', 'expert'), scatter_dimension=0, tiled=T...  641 us
    reduce_scatter x1, waiting for transfers between devices, shards(): lax.psum_scatter(key_w_grad, ('dp', 'expert'), scatter_dimension=0, tiled...  636 us
    reduce_scatter x1, waiting for transfers between devices, shards(): lax.psum_scatter(value_w_grad, ('dp', 'expert'), scatter_dimension=0, til...  635 us
    unnamed x19, waiting for transfers between devices  156 us
    unnamed x2, blocking collectives  134 us
    reduce_scatter x1, waiting for transfers between devices, shards(): lax.psum_scatter(gate_w_grad.astype(jnp.bfloat16), 'dp', scatter_dimensio...  78.7 us
    reduce_scatter x1, waiting for transfers between devices, shards(): lax.psum_scatter(up_w_grad.astype(jnp.bfloat16), 'dp', scatter_dimension=...  78.6 us
  transfers between devices with their start and end apart: 20, of which 17 were waited for; matrix products, arithmetic and copies ran while one was open for 4% of the time, Pallas kernels for 0%

commit v1 on v0

v1 whole, which is shorter than its diff:
```python
import functools
from types import SimpleNamespace

import jax
import jax.numpy as jnp
import numpy as np
from jax import lax
from jax.experimental import pallas as pl
from jax.experimental.pallas import tpu as pltpu
from jax.sharding import PartitionSpec as P

MESH = pl.DeviceIdType.MESH
LOW, WIDE = jnp.bfloat16, jnp.float32
EPSILON = 1e-06
SCALE = 64 ** (-0.5)
TOK, SEQ, D, SLOTS = 128, 1024, 1024, 384
Z_STEPS = (2, 1, 3)


def dot(one, two):
    return lax.dot_general(one, two, (((1,), (0,)), ((), ())), preferred_element_type=WIDE)


def tail_dot(one, two):
    return lax.dot_general(one, two, (((1,), (1,)), ((), ())), preferred_element_type=WIDE)


def lead_dot(one, two):
    return lax.dot_general(one, two, (((0,), (0,)), ((), ())), preferred_element_type=WIDE)


def place():
    i, j = lax.axis_index("dp"), lax.axis_index("expert")
    at = SimpleNamespace(i=i, j=j, x=lax.rem(i, 4), y=lax.div(i, 4), z=lax.div(j, 2), c=lax.rem(j, 2))
    at.sibling = (i, at.z * 2 + 1 - at.c)
    return at


def plus(value, step, size):
    return lax.rem(value + step, size)


def z_peer(at, step):
    return (at.i, plus(at.z, step, 4) * 2 + at.c)


def xy_peer(at, x_step, y_step):
    return (plus(at.y, y_step, 4) * 4 + plus(at.x, x_step, 4), at.j)


def send(source, target, sent, got, device):
    copy = pltpu.make_async_remote_copy(
        src_ref=source, dst_ref=target, send_sem=sent, recv_sem=got, device_id=device, device_id_type=MESH
    )
    copy.start()
    return copy


def rows(ref, block, size=TOK):
    return ref.at[pl.ds(pl.multiple_of(block * size, size), size)]


def columns(ref, block, size=128):
    return ref.at[:, pl.ds(pl.multiple_of(block * size, size), size)]


class Gather:
    def __init__(self, at, source, target, sent, got):
        self.at, self.source, self.target, self.sent, self.got = at, source, target, sent, got

    def start(self):
        at, mine = self.at, self.target(self.at.j)
        self.copies = [
            send(self.source, mine, self.sent.at[k], self.got.at[k], z_peer(at, step))
            for k, step in enumerate(Z_STEPS)
        ]
        self.copies.append(send(self.source, mine, self.sent.at[3], self.got.at[3], at.sibling))

    def forward(self):
        at = self.at
        for k, step in enumerate(Z_STEPS):
            self.copies[k].wait_recv()
            block = self.target(plus(at.z, 4 - step, 4) * 2 + at.c)
            self.copies.append(send(block, block, self.sent.at[4 + k], self.got.at[4 + k], at.sibling))

    def finish(self):
        for copy in self.copies[3:]:
            copy.wait_recv()
        for copy in self.copies:
            copy.wait_send()


def greet(devices):
    barrier = pltpu.get_barrier_semaphore()
    for device in devices:
        pl.semaphore_signal(barrier, inc=1, device_id=device, device_id_type=MESH)
    return lambda: pl.semaphore_wait(barrier, len(devices))


def expert_peers(at):
    return [(at.i, plus(at.j, step, 8)) for step in range(1, 8)]


def dp_peers(at):
    return [xy_peer(at, step % 4, step // 4) for step in range(1, 16)]


def lanes(shape):
    return lax.broadcasted_iota(jnp.int32, shape, len(shape) - 1)


def turn(values, cosine, signed_sine):
    lane = lanes(values.shape)
    swapped = jnp.where(
        lane % 64 < 32, pltpu.roll(values, 96, axis=1), pltpu.roll(values, 32, axis=1)
    )
    return values * cosine + swapped * signed_sine


def angles(r, here, shape):
    table = r.table[here, :]
    other, low_lanes = pltpu.roll(table, 64, axis=1), lanes(shape) < 64
    return jnp.where(low_lanes, table, other), jnp.where(low_lanes, other, table)


def both_heads(values, low_lanes):
    zero = jnp.zeros_like(values)
    return jnp.concatenate(
        [jnp.where(low_lanes, values, zero), jnp.where(low_lanes, zero, values)], axis=0
    )


def allowed_keys(r, token, start, length):
    query_segment, key_segment = r.seg_col[token, :], r.seg_row[:, 0:length].astype(WIDE)
    key_place = lax.broadcasted_iota(jnp.int32, (16, length), 1)
    query_place = lax.broadcasted_iota(jnp.int32, (16, length), 0) + start
    return (key_segment == query_segment) & (key_place <= query_place)


def front(r):
    at = place()
    ready = greet(expert_peers(at) + dp_peers(at))
    loads = []
    for n, (source, target) in enumerate(((r.gate_in, r.gate), (r.up_in, r.up), (r.down_in, r.down))):
        loads.append(pltpu.make_async_copy(source, target, r.load.at[n]))
        loads[-1].start()

    query_w, key_w = r.w_query[...].astype(WIDE), r.w_key[...].astype(WIDE)
    value_w, out_w, extra = r.w_value[...].astype(WIDE), r.w_out[...].astype(WIDE), r.extra[...]
    low_lanes = lanes((8, 128)) < 64
    for j in range(8):
        tile = slice(128 * (j // 2), 128 * (j // 2) + 128)
        key_part, value_part = key_w[:, tile], value_w[:, tile]
        if j % 2:
            key_part = pltpu.roll(key_part, 64, axis=1)
        else:
            value_part = pltpu.roll(value_part, 64, axis=1)
        head = slice(128 * j, 128 * j + 128)
        r.pack[j] = jnp.concatenate(
            [query_w[:, head], jnp.where(low_lanes, key_part, value_part), out_w[:, head], extra], axis=0
        ).astype(LOW)
    expert = lax.broadcasted_iota(jnp.int32, (128, TOK), 0)
    named = jnp.zeros((128, TOK), WIDE)
    for k in range(8):
        named = named + jnp.where(r.routes[k : k + 1, :] == expert, 1.0, 0.0)
    rows(r.named, at.j)[...] = jnp.transpose(named).astype(LOW)
    rows(r.hidden_one, at.j)[...] = r.tokens[...]
    r.stage[lax.div(at.j, 4), pl.ds(pl.multiple_of(lax.rem(at.j, 4) * 32, 32), 32)] = r.pack[at.j]
    for b in range(8):
        here = slice(TOK * b, TOK * (b + 1))
        across = jnp.broadcast_to(r.seg_row[:, here].astype(WIDE), (TOK, TOK))
        r.seg_col[here, :] = jnp.transpose(across)[:, 0:1]

    ready()
    tokens = Gather(at, r.tokens, lambda b: rows(r.hidden_one, b), r.x_sent, r.x_got)
    tokens.start()
    first = []
    place_in_stage = r.stage.at[lax.div(at.j, 4), pl.ds(pl.multiple_of(lax.rem(at.j, 4) * 32, 32), 32)]
    for step in range(1, 8):
        other = plus(at.j, step, 8)
        first.append(
            send(r.pack.at[other], place_in_stage, r.p_sent.at[step], r.p_got.at[step], (at.i, other))
        )
    marks = Gather(at, rows(r.named, at.j), lambda b: rows(r.named, b), r.n_sent, r.n_got)
    marks.start()
    for copy in first:
        copy.wait_recv()
    second = []
    for step in range(1, 16):
        second.append(
            send(
                r.stage, r.dense.at[:, at.y, at.x], r.w_sent.at[step], r.w_got.at[step],
                xy_peer(at, step % 4, step // 4),
            )
        )
    r.dense[:, at.y, at.x] = r.stage[...]
    tokens.forward()
    rows(r.upstream, at.j)[...] = r.cotangent[...]
    upstream = Gather(at, r.cotangent, lambda b: rows(r.upstream, b), r.g_sent, r.g_got)
    upstream.start()
    for copy in second:
        copy.wait_recv()

    def unpack(i, _):
        part = r.dense[:, lax.div(i, 4), lax.rem(i, 4)].reshape(8, 32, 128).astype(WIDE)
        here = pl.ds(pl.multiple_of(i * 64, 64), 64)
        r.w_qkv[here, 0:128] = part[:, 0:8, :].reshape(64, 128).astype(LOW)
        r.w_qkv[here, 128:256] = part[:, 8:16, :].reshape(64, 128).astype(LOW)
        r.w_out_part[here, :] = part[:, 16:24, :].reshape(64, 128).astype(LOW)
        r.extra_all[here, :] = part[:, 24:32, :].reshape(64, 128)
        return 0

    lax.fori_loop(0, 16, unpack, 0)
    out_weights = Gather(at, r.w_out_part, lambda b: columns(r.w_out_all, b), r.o_sent, r.o_got)
    out_weights.start()
    columns(r.w_out_all, at.j)[...] = r.w_out_part[...]
    r.gains[...] = extra_rows(r)
    r.router[...] = jnp.where(lanes((D, 128)) < 32, r.extra_all[...], 0.0).astype(LOW)
    tokens.finish()

    low_lanes = lanes((256, 128)) < 64

    def project(b, _):
        here = pl.ds(pl.multiple_of(b * 256, 256), 256)
        x = r.hidden_one[here, :].astype(WIDE)
        inverse = lax.rsqrt(jnp.mean(x * x, axis=-1, keepdims=True) + EPSILON)
        hidden = (x * inverse * r.gains[0:1, :]).astype(LOW)
        r.hidden_one[here, :] = hidden
        made = dot(hidden, r.w_qkv[...])
        cosine, sine = angles(r, here, (256, 128))
        r.queries[here, :] = turn(made[:, 0:128], cosine, sine).astype(LOW)
        pair = turn(
            made[:, 128:256], jnp.where(low_lanes, cosine, 1.0), jnp.where(low_lanes, sine, 0.0)
        )
        turned = pltpu.roll(pair, 64, axis=1)
        r.keys[here, :] = jnp.where(low_lanes, pair, turned).astype(LOW)
        r.values[here, :] = jnp.where(low_lanes, turned, pair).astype(LOW)
        return 0

    lax.fori_loop(0, 4, project, 0)
    marks.forward()
    hidden_save = pltpu.make_async_copy(r.hidden_one, r.hidden_far, r.load.at[3])
    hidden_save.start()

    low_lanes = lanes((TOK, 128)) < 64
    returned = []
    for b in range(8):
        length = TOK * (b + 1)
        both = both_heads(r.queries[TOK * b : TOK * (b + 1), :], low_lanes)
        r.scores[:, 0:length] = tail_dot(both, r.keys[0:length, :])

        def strip(t, _):
            token = pl.ds(pl.multiple_of(TOK * b + 16 * t, 16), 16)
            allowed = allowed_keys(r, token, TOK * b + 16 * t, length)
            logs = []
            for head in range(2):
                line = pl.ds(pl.multiple_of(TOK * head + 16 * t, 16), 16)
                scores = jnp.where(allowed, r.scores[line, 0:length] * SCALE, -1e30)
                top = jnp.max(scores, axis=-1, keepdims=True)
                powers = jnp.exp(scores - top)
                total = jnp.sum(powers, axis=-1, keepdims=True)
                r.probs[line, 0:length] = (powers * (1.0 / total)).astype(LOW)
                logs.append(top + jnp.log(total))
            lane = lanes((16, 128))
            r.log_total[token, :] = jnp.where(lane == 0, logs[0], jnp.where(lane == 1, logs[1], 0.0))
            return 0

        lax.fori_loop(0, 8, strip, 0)
        mixed = dot(r.probs[:, 0:length], r.values[0:length, :])
        r.attended_head[TOK * b : TOK * (b + 1), :] = jnp.where(low_lanes, mixed[0:TOK], mixed[TOK:]).astype(LOW)
        copy = pltpu.make_async_remote_copy(
            src_ref=r.attended_head.at[TOK * b : TOK * (b + 1)], dst_ref=columns(r.attended, at.j), send_sem=r.a_sent.at[b],
            recv_sem=r.a_got.at[at.j], device_id=(at.i, jnp.int32(b)), device_id_type=MESH,
        )
        returned.append(copy)

        @pl.when(at.j != b)
        def _():
            copy.start()

        @pl.when(at.j == b)
        def _():
            columns(r.attended, at.j)[...] = r.attended_head[TOK * b : TOK * (b + 1), :]

        if b == 3:
            upstream.forward()
        if b == 6:
            out_weights.forward()
    out_weights.finish()
    for b in range(8):

        @pl.when(at.j != b)
        def _():
            returned[b].wait_send()
            pltpu.make_async_remote_copy(
                src_ref=r.attended_head.at[TOK * b : TOK * (b + 1)], dst_ref=r.attended.at[:, 128 * b : 128 * b + 128],
                send_sem=r.a_sent.at[b], recv_sem=r.a_got.at[b], device_id=at.sibling, device_id_type=MESH,
            ).wait_recv()

    residual = r.tokens[...].astype(WIDE) + dot(r.attended[...], r.w_out_all[...])
    r.residual[...] = residual
    inverse = lax.rsqrt(jnp.mean(residual * residual, axis=-1, keepdims=True) + EPSILON)
    rows(r.hidden_two, at.j)[...] = (residual * inverse * r.gains[1:2, :]).astype(LOW)
    hidden = Gather(at, rows(r.hidden_two, at.j), lambda b: rows(r.hidden_two, b), r.h_sent, r.h_got)
    hidden.start()
    out_save = pltpu.make_async_copy(r.w_out_all, r.out_far, r.load.at[4])
    out_save.start()
    attended = Gather(at, r.attended, lambda b: rows(r.attended_all, b), r.t_sent, r.t_got)
    rows(r.attended_all, at.j)[...] = r.attended[...]
    for copy in first + second:
        copy.wait_send()
    upstream.finish()
    marks.finish()
    hidden_save.wait()
    out_save.wait()
    order_tokens(r, at)
    for copy in loads:
        copy.wait()
    lax.fori_loop(0, 4, lambda e, _: pick_upstream(r, at, e), 0)
    hidden.forward()
    hidden.finish()
    attended.start()
    return attended


def extra_rows(r):
    picked = [jnp.transpose(r.extra_all[TOK * b : TOK * (b + 1), :])[32:40, :] for b in range(8)]
    return jnp.concatenate(picked, axis=1)


def got(ref, semaphore, at):
    pltpu.make_async_remote_copy(
        src_ref=ref, dst_ref=ref, send_sem=semaphore, recv_sem=semaphore, device_id=at.sibling, device_id_type=MESH
    ).wait_recv()


def gone(ref, semaphore, at):
    pltpu.make_async_remote_copy(
        src_ref=ref, dst_ref=ref, send_sem=semaphore, recv_sem=semaphore, device_id=at.sibling, device_id_type=MESH
    ).wait_send()


class SumXY:
    def __init__(self, at, source, ways, sent, got_sems, x_first, height):
        self.at, self.source, self.ways, self.sent, self.got_sems = at, source, ways, sent, got_sems
        self.x_first, self.height = x_first, height
        self.f, self.s = (at.x, at.y) if x_first else (at.y, at.x)

    def block(self, first, second):
        return self.source.at[second, first] if self.x_first else self.source.at[first, second]

    def neighbour(self, along_first, step):
        return xy_peer(self.at, step, 0) if along_first == self.x_first else xy_peer(self.at, 0, step)

    def out(self, k, ref, target, along_first, step):
        send(ref, target, self.sent.at[k], self.got_sems.at[k], self.neighbour(along_first, step))

    def take(self, k, ref):
        got(ref, self.got_sems.at[k], self.at)

    def step1(self):
        far = plus(self.f, 2, 4)
        self.out(0, self.block(far, pl.ds(0, 2)), self.ways[0].at[0], True, 1)
        self.out(1, self.block(far, pl.ds(2, 2)), self.ways[0].at[1], True, 3)

    def step2(self):
        for k, step in enumerate((1, 3)):
            self.take(k, self.ways[0].at[k])
            near = plus(self.f, step, 4)
            part = self.block(near, pl.ds(2 * k, 2))
            part[...] = part[...] + self.ways[0][k]
            self.out(2 + k, self.block(near, pl.ds(0, 4)), self.ways[1].at[k], True, step)

    def step3(self):
        for k in range(2):
            self.take(2 + k, self.ways[1].at[k])
        mine = self.block(self.f, pl.ds(0, 4))
        mine[...] = mine[...] + (self.ways[1][0] + self.ways[1][1])
        half, far = self.height // 2, self.block(self.f, plus(self.s, 2, 4))
        self.out(4, far.at[pl.ds(0, half)], self.ways[2].at[0], False, 1)
        self.out(5, far.at[pl.ds(half, half)], self.ways[2].at[1], False, 3)

    def step4(self):
        half = self.height // 2
        for k, step in enumerate((1, 3)):
            self.take(4 + k, self.ways[2].at[k])
            near = self.block(self.f, plus(self.s, step, 4))
            part = near.at[pl.ds(half * k, half)]
            part[...] = part[...] + self.ways[2][k]
            self.out(6 + k, near, self.ways[3].at[k], False, step)

    def step5(self):
        for k in range(2):
            self.take(6 + k, self.ways[3].at[k])
        mine = self.block(self.f, self.s)
        return mine[...].astype(WIDE) + self.ways[3][0].astype(WIDE) + self.ways[3][1].astype(WIDE)

    def finish(self):
        far = plus(self.f, 2, 4)
        gone(self.block(far, pl.ds(0, 2)), self.sent.at[0], self.at)
        gone(self.block(far, pl.ds(2, 2)), self.sent.at[1], self.at)
        for k, step in enumerate((1, 3)):
            gone(self.block(plus(self.f, step, 4), pl.ds(0, 4)), self.sent.at[2 + k], self.at)
            part = self.block(self.f, plus(self.s, 2, 4)).at[pl.ds(self.height // 2 * k, self.height // 2)]
            gone(part, self.sent.at[4 + k], self.at)
            gone(self.block(self.f, plus(self.s, step, 4)), self.sent.at[6 + k], self.at)


class SumExpert:
    def __init__(self, at, r, pair_in, line_in, mine, sent, got_sems):
        self.at, self.r, self.pair_in, self.line_in = at, r, pair_in, line_in
        self.mine, self.sent, self.got_sems = mine, sent, got_sems

    def start(self, tiles):
        at, partial = self.at, self.r.partial

        def to_sibling(p, _):
            steps = (2 + p, 1 - p)
            blocks = [plus(at.z, step, 4) * 2 + 1 - at.c for step in steps]
            for n in range(4):
                part = slice(256 * n, 256 * (n + 1))
                made = tiles(*blocks, part)
                for k, step in enumerate(steps):
                    partial[step, :, part] = made[TOK * k : TOK * (k + 1)].astype(LOW)
            for step in steps:
                send(partial.at[step], self.pair_in.at[step], self.sent.at[step], self.got_sems.at[step], at.sibling)
            return 0

        lax.fori_loop(0, 2, to_sibling, 0)

        def along_z(p, _):
            steps = (2 + p, 1 - p)
            blocks = [plus(at.z, step, 4) * 2 + at.c for step in steps]
            for step in steps:
                got(self.pair_in.at[step], self.got_sems.at[step], at)
            for n in range(4):
                part = slice(256 * n, 256 * (n + 1))
                made = tiles(*blocks, part)
                first = made[0:TOK] + self.pair_in[steps[0], :, part].astype(WIDE)
                second = made[TOK:] + self.pair_in[steps[1], :, part].astype(WIDE)
                partial[3 + steps[0], :, part] = first.astype(LOW)

                @pl.when(p == 0)
                def _():
                    partial[3 + steps[1], :, part] = second.astype(LOW)

                @pl.when(p == 1)
                def _():
                    self.mine[:, part] = second

            def away(step):
                send(
                    partial.at[3 + step], self.line_in.at[step - 1], self.sent.at[3 + step],
                    self.got_sems.at[3 + step], z_peer(at, step),
                )

            away(steps[0])
            pl.when(p == 0)(lambda: away(steps[1]))
            return 0

        lax.fori_loop(0, 2, along_z, 0)

    def sent_all(self):
        for k in range(7):
            gone(self.r.partial.at[k], self.sent.at[k], self.at)

    def total(self):
        value = self.mine[...]
        for k in range(3):
            got(self.line_in.at[k], self.got_sems.at[4 + k], self.at)
            value = value + self.line_in[k].astype(WIDE)
        return value


def order_tokens(r, at):
    before = (
        lax.broadcasted_iota(jnp.int32, (TOK, TOK), 0) > lax.broadcasted_iota(jnp.int32, (TOK, TOK), 1)
    )
    before = jnp.where(before, 1.0, 0.0).astype(LOW)

    def block(b, earlier):
        here = pl.ds(pl.multiple_of(b * TOK, TOK), TOK)
        named = r.named[here, :]
        flags = named.astype(WIDE)
        order = jnp.where(flags > 0.0, dot(before, named) + earlier, -1.0)
        r.order_row[:, here] = jnp.transpose(order)[0:32]
        for e in range(4):
            mine = jnp.where(lanes((TOK, 128)) == 4 * at.j + e, order, 0.0)
            column = jnp.sum(mine, axis=-1, keepdims=True).astype(jnp.int32)
            r.places[here, SLOTS * e : SLOTS * (e + 1)] = jnp.where(
                column == lanes((TOK, SLOTS)), 1.0, 0.0
            ).astype(LOW)
        return earlier + jnp.sum(flags, axis=0, keepdims=True)

    lax.fori_loop(0, 8, block, jnp.zeros((1, 128), WIDE))


def share_tokens(r, at):
    def block(b, _):
        here = pl.ds(pl.multiple_of(b * TOK, TOK), TOK)
        named = r.named[here, :].astype(WIDE) > 0.0
        logits = jnp.where(named, dot(r.hidden_two[here, :], r.router[...]), -1e30)
        powers = jnp.where(named, jnp.exp(logits - jnp.max(logits, axis=-1, keepdims=True)), 0.0)
        shares = powers / jnp.sum(powers, axis=-1, keepdims=True)

        @pl.when(b == at.j)
        def _():
            r.shares[...] = shares

        r.shares_row[:, here] = jnp.transpose(shares)[0:32]
        return 0

    lax.fori_loop(0, 8, block, 0)


def hits(r, at, e, t):
    slot = lax.broadcasted_iota(jnp.int32, (TOK, SEQ), 0) + TOK * t
    return slot == r.order_row[pl.ds(4 * at.j + e, 1), :].astype(jnp.int32)


def pick_rows(r, at, e):
    def pick(t, _):
        r.partial[t] = jnp.where(hits(r, at, e, t), 1.0, 0.0).astype(LOW)
        return 0

    lax.fori_loop(0, 3, pick, 0)


def pick_upstream(r, at, e):
    pick_rows(r, at, e)
    here = pl.ds(pl.multiple_of(e * SLOTS, SLOTS), SLOTS)
    for n in range(4):
        part = slice(256 * n, 256 * (n + 1))
        r.slot_grad[here, part] = dot(r.partial[0:3].reshape(SLOTS, SEQ), r.upstream[:, part]).astype(LOW)
    return 0


def expert(r, at, e):
    row = pl.ds(4 * at.j + e, 1)
    here = pl.ds(pl.multiple_of(e * SLOTS, SLOTS), SLOTS)
    quarters = [slice(256 * n, 256 * (n + 1)) for n in range(4)]

    def strip(t):
        return pl.ds(pl.multiple_of(t * 32, 32), 32)

    def slot_strip(t):
        return pl.ds(pl.multiple_of(e * SLOTS + t * 32, 32), 32)

    def shares(t, _):
        share = jnp.sum(jnp.where(hits(r, at, e, t), r.shares_row[row, :], 0.0), axis=-1, keepdims=True)
        r.share[pl.ds(pl.multiple_of(t * TOK, TOK), TOK), :] = share
        return 0

    pick_rows(r, at, e)
    lax.fori_loop(0, 3, shares, 0)
    for n in quarters:
        r.rows[:, n] = dot(r.partial[0:3].reshape(SLOTS, SEQ), r.hidden_two[:, n]).astype(LOW)
    r.wide_a[:, 0:512] = dot(r.rows[...], r.gate[e].reshape(D, 512))
    r.wide_a[:, 512:1024] = dot(r.rows[...], r.up[e].reshape(D, 512))

    def activate(t, _):
        gate_pre = r.wide_a[strip(t), 0:512]
        silu = gate_pre / (1.0 + jnp.exp(-gate_pre))
        r.product[strip(t), :] = (silu * r.wide_a[strip(t), 512:1024]).astype(LOW)
        return 0

    lax.fori_loop(0, 12, activate, 0)
    for n in quarters:
        r.made[:, n] = dot(r.product[...], r.down[e, :, :, :, n].reshape(512, 256)).astype(LOW)

    def weigh(t, _):
        upstream = r.slot_grad[slot_strip(t), :].astype(WIDE)
        made, share = r.made[strip(t), :].astype(WIDE), r.share[strip(t), :]
        r.gate_dot[strip(t), :] = jnp.sum(upstream * made, axis=-1, keepdims=True)
        r.made[strip(t), :] = (share * made).astype(LOW)
        r.route_grad[strip(t), :] = (share * upstream).astype(LOW)
        return 0

    lax.fori_loop(0, 12, weigh, 0)
    keep = pltpu.make_async_copy(r.made, r.made_far.at[here], r.load.at[3])
    keep.start()
    r.wide_b[:, 0:512] = tail_dot(r.route_grad[...], r.down[e].reshape(512, D))
    for n in quarters:
        down_grad = lead_dot(r.product[...], r.route_grad[:, n])
        r.down[e, :, :, :, n] = down_grad.astype(LOW).reshape(4, 4, 32, 256)

    def activate_back(t, _):
        gate_pre, product_grad = r.wide_a[strip(t), 0:512], r.wide_b[strip(t), 0:512]
        sigmoid = 1.0 / (1.0 + jnp.exp(-gate_pre))
        slope = sigmoid * (1.0 + gate_pre * (1.0 - sigmoid))
        r.gate_low[strip(t), :] = (product_grad * r.wide_a[strip(t), 512:1024] * slope).astype(LOW)
        r.up_low[strip(t), :] = (product_grad * (gate_pre * sigmoid)).astype(LOW)
        return 0

    lax.fori_loop(0, 12, activate_back, 0)
    for m, n in enumerate(quarters):
        slot_grad = tail_dot(r.gate_low[...], r.gate[e, m].reshape(256, 512)) + tail_dot(
            r.up_low[...], r.up[e, m].reshape(256, 512)
        )
        r.slot_grad[here, n] = slot_grad.astype(LOW)
        r.gate[e, m] = lead_dot(r.rows[:, n], r.gate_low[...]).astype(LOW).reshape(4, 64, 512)
        r.up[e, m] = lead_dot(r.rows[:, n], r.up_low[...]).astype(LOW).reshape(4, 64, 512)

    def gate_rows(t, total):
        grads = r.gate_dot[pl.ds(pl.multiple_of(t * TOK, TOK), TOK), :]
        return total + jnp.sum(jnp.where(hits(r, at, e, t), grads, 0.0), axis=0, keepdims=True)

    gate_row = lax.fori_loop(0, 3, gate_rows, jnp.zeros((1, SEQ), WIDE))
    for b in range(8):
        r.gate_grad[b, pl.ds(e, 1), :] = gate_row[:, TOK * b : TOK * (b + 1)]
    keep.wait()


def expert_sums(r, at, e):
    left, right = pl.ds(0, 512), pl.ds(512, 512)
    made = []
    for n, (source, x_first, height) in enumerate(
        (
            (r.gate.at[e], True, 64),
            (r.up.at[e], False, 64),
            (r.down.at[e, :, :, :, left], True, 32),
            (r.down.at[e, :, :, :, right], False, 32),
        )
    ):
        ways = [
            (r.wide_ways if n < 2 else r.half_ways)[k].at[e, n % 2] for k in range(4)
        ]
        made.append(SumXY(at, source, ways, r.e_sent.at[e, n], r.e_got.at[e, n], x_first, height))
    return made


def back(r, attended):
    at = place()
    r.wide_ways = (r.wide1, r.wide2, r.wide3, r.wide4)
    r.half_ways = (r.half1, r.half2, r.half3, r.half4)
    r.gate_grad[...] = jnp.zeros((8, 8, 128), WIDE)
    share_tokens(r, at)

    def sums(e, name):
        for unit in expert_sums(r, at, e):
            getattr(unit, name)()

    def one(e, _):
        expert(r, at, e)
        sums(e, "step1")

        @pl.when(e > 0)
        def _():
            sums(e - 1, "step2")

        return 0

    lax.fori_loop(0, 4, one, 0)

    def share_out(source, target, sent, got_sems):
        copies = []
        for step in range(1, 8):
            other = plus(at.j, step, 8)
            copies.append(send(source(other), target, sent.at[step], got_sems.at[step], (at.i, other)))
        return copies

    gate_copies = share_out(lambda b: r.gate_grad.at[b], r.gate_back.at[at.j], r.c_sent, r.c_got)
    r.gate_back[pl.ds(at.j, 1)] = r.gate_grad[pl.ds(at.j, 1)]

    def two_blocks(ref, a, b):
        return jnp.concatenate([rows(ref, a)[...], rows(ref, b)[...]], axis=0)

    hidden_sum = SumExpert(at, r, r.pair1, r.line1, r.mine1, r.s1_sent, r.s1_got)
    hidden_sum.start(lambda a, b, n: dot(two_blocks(r.places, a, b), r.slot_grad[:, n]))
    made_load = pltpu.make_async_copy(r.made_far, r.slot_grad, r.load.at[3])
    made_load.start()
    own = pl.ds(pl.multiple_of(at.j * TOK, TOK), TOK)
    r.hidden_own[...] = r.hidden_two[own, :]
    out_load = pltpu.make_async_copy(r.out_far, r.hidden_two, r.load.at[0])
    out_load.start()
    hidden_load = pltpu.make_async_copy(r.hidden_far, r.upstream, r.load.at[1])
    hidden_load.start()
    sums(3, "step2")
    attended.forward()
    for copy in gate_copies:
        copy.wait_recv()
    gate_grad = jnp.concatenate(
        [r.gate_back[b][0:4] for b in range(8)] + [jnp.zeros((96, 128), WIDE)], axis=0
    )
    gate_grad = jnp.transpose(gate_grad)
    shares = r.shares[...]
    logit_grad = shares * (gate_grad - jnp.sum(shares * gate_grad, axis=-1, keepdims=True))
    logit_grad = logit_grad.astype(LOW)
    router_grad = lead_dot(r.hidden_own[...], logit_grad)
    hidden_grad = tail_dot(logit_grad, r.router[...])
    hidden_grad = hidden_grad + hidden_sum.total()
    residual, upstream = r.residual[...], r.cotangent[...].astype(WIDE)
    inverse = lax.rsqrt(jnp.mean(residual * residual, axis=-1, keepdims=True) + EPSILON)
    gain_two_grad = jnp.sum(hidden_grad * (residual * inverse), axis=0, keepdims=True)
    scaled = hidden_grad * r.gains[1:2, :]
    mean = jnp.mean(scaled * residual, axis=-1, keepdims=True)
    residual_grad = upstream + scaled * inverse - residual * (inverse * inverse * inverse * mean)
    r.residual_grad[...] = residual_grad
    r.branch[...] = residual_grad.astype(LOW)
    branch_copies = share_out(lambda b: columns(r.branch, b), rows(r.branch_part, at.j), r.b_sent, r.b_got)
    out_load.wait()
    for n in range(4):
        part = slice(256 * n, 256 * (n + 1))
        r.attended_grad[:, part] = tail_dot(r.branch[...], r.hidden_two[part, :]).astype(LOW)
    grad_copies = share_out(
        lambda b: columns(r.attended_grad, b), rows(r.attended_back, at.j), r.d_sent, r.d_got
    )
    rows(r.branch_part, at.j)[...] = columns(r.branch, at.j)[...]
    rows(r.attended_back, at.j)[...] = columns(r.attended_grad, at.j)[...]
    hidden_sum.sent_all()

    output_sum = SumExpert(at, r, r.pair2, r.line2, r.mine2, r.s2_sent, r.s2_got)
    made_load.wait()
    output_sum.start(lambda a, b, n: dot(two_blocks(r.places, a, b), r.slot_grad[:, n]))
    sums(0, "step3")
    sums(1, "step3")
    for copy in grad_copies:
        copy.wait_recv()

    low_lanes = lanes((TOK, 128)) < 64
    r.key_grad[...] = jnp.zeros((SEQ, 128), WIDE)
    r.value_grad[...] = jnp.zeros((SEQ, 128), WIDE)
    for b in range(8):
        length, here = TOK * (b + 1), slice(TOK * b, TOK * (b + 1))
        both = both_heads(r.queries[here, :], low_lanes)
        both_grad = both_heads(r.attended_back[here, :], low_lanes)
        r.wide_a[0:256, 0:length] = tail_dot(both, r.keys[0:length, :])
        r.wide_b[0:256, 0:length] = tail_dot(both_grad, r.values[0:length, :])
        for head in range(2):

            def strip(t, _):
                token = pl.ds(pl.multiple_of(TOK * b + 16 * t, 16), 16)
                line = pl.ds(pl.multiple_of(TOK * head + 16 * t, 16), 16)
                allowed = allowed_keys(r, token, TOK * b + 16 * t, length)
                powers = jnp.exp(r.wide_a[line, 0:length] * SCALE - r.log_total[token, head : head + 1])
                probs = jnp.where(allowed, powers, 0.0)
                prob_grad = r.wide_b[line, 0:length]
                inner = jnp.sum(probs * prob_grad, axis=-1, keepdims=True)
                r.rows[line, 0:length] = (probs * (prob_grad - inner)).astype(LOW)
                r.route_grad[line, 0:length] = probs.astype(LOW)
                return 0

            lax.fori_loop(0, 8, strip, 0, unroll=2)
        score_grad, probs = r.rows[0:256, 0:length], r.route_grad[0:256, 0:length]
        query_grad = dot(score_grad, r.keys[0:length, :]) * SCALE
        query_grad = jnp.where(low_lanes, query_grad[0:TOK], query_grad[TOK:])
        cosine, sine = angles(r, here, (TOK, 128))
        r.qkv_grad[here, 0:128] = turn(query_grad, cosine, -sine).astype(LOW)
        r.key_grad[0:length, :] += lead_dot(score_grad, both)
        r.value_grad[0:length, :] += lead_dot(probs, both_grad)
        if b == 4:
            sums(2, "step3")
            sums(0, "step4")
        if b == 6:
            sums(1, "step4")

    def finish_keys(b, _):
        here = pl.ds(pl.multiple_of(b * TOK, TOK), TOK)
        key_grad, value_grad = r.key_grad[here, :], r.value_grad[here, :]
        key_grad = (key_grad + pltpu.roll(key_grad, 64, axis=1)) * SCALE
        value_grad = value_grad + pltpu.roll(value_grad, 64, axis=1)
        cosine, sine = angles(r, here, (TOK, 128))
        key_grad = turn(key_grad, cosine, -sine)
        r.qkv_grad[here, 128:256] = jnp.where(low_lanes, key_grad, value_grad).astype(LOW)
        return 0

    lax.fori_loop(0, 8, finish_keys, 0)

    output_sum.sent_all()
    r.gain_sum[...] = jnp.zeros((8, D), WIDE)

    hidden_load.wait()

    def hidden_one_tile(a, b, n):
        made = tail_dot(two_blocks(r.qkv_grad, a, b), r.w_qkv[n, :])
        hidden = jnp.concatenate([rows(r.upstream, k).at[:, n][...] for k in (a, b)], axis=0)
        r.gain_sum[0:1, n] += jnp.sum(made * hidden.astype(WIDE), axis=0, keepdims=True)
        return made

    input_sum = SumExpert(at, r, r.pair3, r.line3, r.mine1, r.s3_sent, r.s3_got)
    input_sum.start(hidden_one_tile)

    for copy in branch_copies:
        copy.wait()
    attended.finish()
    gain_rows = jnp.concatenate(
        [
            jnp.zeros((32, D), WIDE), r.gain_sum[0:1, :] / r.gains[0:1, :], gain_two_grad, jnp.zeros((94, D), WIDE),
        ],
        axis=0,
    )
    for m in range(4):
        here = slice(256 * m, 256 * (m + 1))
        grads = lead_dot(r.upstream[:, here], r.qkv_grad[...]).astype(LOW)
        out_grads = lead_dot(r.attended_all[:, here], r.branch_part[...]).astype(LOW)
        others = [jnp.transpose(gain_rows[:, 256 * m + 128 * t : 256 * m + 128 * (t + 1)]) for t in range(2)]
        others = (router_grad[here] + jnp.concatenate(others, axis=0)).astype(LOW)
        for x in range(4):
            part = slice(64 * x, 64 * (x + 1))
            r.dense[0, m, x, 0:64] = grads[part, 0:128]
            r.dense[0, m, x, 64:128] = grads[part, 128:256]
            r.dense[1, m, x, 0:64] = out_grads[part]
            r.dense[1, m, x, 64:128] = others[part]
    dense_sums = [
        SumXY(
            at, r.dense.at[n], [r.dense1.at[n], r.dense2.at[n], r.dense3.at[n], r.dense4.at[n]],
            r.f_sent.at[n], r.f_got.at[n], n == 0, 128,
        )
        for n in range(2)
    ]
    for unit in dense_sums:
        unit.step1()
    sums(3, "step3")
    sums(2, "step4")
    for unit in dense_sums:
        unit.step2()

    def stores(e):
        high = pl.ds(pl.multiple_of(e * 64, 64), 64)
        low = pl.ds(pl.multiple_of(e * 32, 32), 32)
        return [
            pltpu.make_async_copy(r.wide_a.at[high, 0:512], r.gate_out.at[e], r.store.at[e, 0]),
            pltpu.make_async_copy(r.wide_a.at[high, 512:1024], r.up_out.at[e], r.store.at[e, 1]),
            pltpu.make_async_copy(r.wide_b.at[low], r.down_out.at[e], r.store.at[e, 2]),
        ]

    def finish_expert(e, _):
        gate, up, left, right = expert_sums(r, at, e)
        high = pl.ds(pl.multiple_of(e * 64, 64), 64)
        r.wide_a[high, 0:512] = gate.step5()
        r.wide_a[high, 512:1024] = up.step5()
        low = pl.ds(pl.multiple_of(e * 32, 32), 32)
        r.wide_b[low, 0:512] = left.step5()
        r.wide_b[low, 512:1024] = right.step5()
        for copy in stores(e):
            copy.start()
        return 0

    lax.fori_loop(0, 3, finish_expert, 0)
    sums(3, "step4")
    for unit in dense_sums:
        unit.step3()
    r.branch[...] = (r.residual[...] + output_sum.total()).astype(LOW)
    output_store = pltpu.make_async_copy(r.branch, r.output, r.load.at[0])
    output_store.start()
    finish_expert(3, 0)
    for unit in dense_sums:
        unit.step4()

    hidden_grad = input_sum.total()
    inputs = r.tokens[...].astype(WIDE)
    inverse = lax.rsqrt(jnp.mean(inputs * inputs, axis=-1, keepdims=True) + EPSILON)
    scaled = hidden_grad * r.gains[0:1, :]
    mean = jnp.mean(scaled * inputs, axis=-1, keepdims=True)
    r.residual_grad[...] = (
        r.residual_grad[...] + scaled * inverse - inputs * (inverse * inverse * inverse * mean)
    )
    input_store = pltpu.make_async_copy(r.residual_grad, r.input_grad, r.load.at[1])
    input_store.start()
    for n, unit in enumerate(dense_sums):
        r.dense_total[n] = unit.step5().reshape(2, 8, 8, 128)
    last_copies = share_out(lambda b: r.dense_total.at[:, :, b], r.dense_back.at[at.j], r.l_sent, r.l_got)
    r.dense_back[pl.ds(at.j, 1)] = r.dense_total[:, :, pl.ds(at.j, 1)].reshape(1, 2, 2, 8, 128)
    for copy in last_copies:
        copy.wait_recv()
    low_lanes = lanes((8, 128)) < 64
    others = jnp.zeros((8, 128), WIDE)
    for b in range(8):
        head = slice(128 * b, 128 * (b + 1))
        r.query_out[:, head] = r.dense_back[b, 0, 0]
        r.out_out[:, head] = r.dense_back[b, 1, 0]
        others = others + r.dense_back[b, 1, 1]
    for t in range(4):
        head = slice(128 * t, 128 * (t + 1))
        even, odd = r.dense_back[2 * t, 0, 1], r.dense_back[2 * t + 1, 0, 1]
        r.key_out[:, head] = jnp.where(low_lanes, even, pltpu.roll(odd, 64, axis=1))
        r.value_out[:, head] = jnp.where(low_lanes, pltpu.roll(even, 64, axis=1), odd)
    r.others_out[...] = others

    input_sum.sent_all()
    for copy in gate_copies + grad_copies + last_copies:
        copy.wait_send()
    output_store.wait()
    input_store.wait()

    def ended(e, _):
        for copy in stores(e):
            copy.wait()
        for unit in expert_sums(r, at, e):
            unit.finish()
        return 0

    lax.fori_loop(0, 4, ended, 0)
    for unit in dense_sums:
        unit.finish()

DMA = pltpu.SemaphoreType.DMA


def low(*shape):
    return pltpu.VMEM(shape, LOW)


def wide(*shape):
    return pltpu.VMEM(shape, WIDE)


def far(*shape, kind=WIDE):
    return pltpu.HBM(shape, kind)


OUTS = dict(
    output=far(TOK, D, kind=LOW), input_grad=far(TOK, D), query_out=wide(8, D), key_out=wide(8, 512),
    value_out=wide(8, 512), out_out=wide(8, D), others_out=wide(8, 128), gate_out=far(4, 64, 512),
    up_out=far(4, 64, 512), down_out=far(4, 32, D), made_far=far(4 * SLOTS, D, kind=LOW),
    hidden_far=far(SEQ, D, kind=LOW), out_far=far(D, D, kind=LOW),
)
SCRATCH = dict(
    w_qkv=low(D, 256), router=low(D, 128), gains=wide(8, D), queries=low(SEQ, 128), keys=low(SEQ, 128),
    values=low(SEQ, 128), log_total=wide(SEQ, 128), attended=low(TOK, D), residual=wide(TOK, D),
    hidden_two=low(SEQ, D), upstream=low(SEQ, D), named=low(SEQ, 128), seg_col=wide(SEQ, 1),
    pack=low(8, 32, 128), stage=low(2, 128, 128),
    gate=low(4, 4, 4, 64, 512), up=low(4, 4, 4, 64, 512), down=low(4, 4, 4, 32, D),
    shares=wide(TOK, 128), shares_row=wide(32, SEQ), order_row=wide(32, SEQ), places=low(SEQ, 4 * SLOTS),
    rows=low(SLOTS, D), route_grad=low(SLOTS, D), made=low(SLOTS, D), slot_grad=low(4 * SLOTS, D),
    gate_grad=wide(8, 8, 128), gate_back=wide(8, 8, 128), wide_a=wide(SLOTS, D), wide_b=wide(SLOTS, D),
    product=low(SLOTS, 512), gate_low=low(SLOTS, 512), up_low=low(SLOTS, 512), share=wide(SLOTS, 1),
    gate_dot=wide(SLOTS, 1), hidden_own=low(TOK, D),
    wide1=low(4, 2, 2, 2, 64, 512), wide2=low(4, 2, 2, 4, 64, 512), wide3=low(4, 2, 2, 32, 512),
    wide4=low(4, 2, 2, 64, 512), half1=low(4, 2, 2, 2, 32, 512), half2=low(4, 2, 2, 4, 32, 512),
    half3=low(4, 2, 2, 16, 512), half4=low(4, 2, 2, 32, 512), dense=low(2, 4, 4, 128, 128),
    dense1=low(2, 2, 2, 128, 128), dense2=low(2, 2, 4, 128, 128), dense3=low(2, 2, 64, 128),
    dense4=low(2, 2, 128, 128), dense_total=wide(2, 2, 8, 8, 128), dense_back=wide(8, 2, 2, 8, 128),
    partial=low(7, TOK, D), pair1=low(4, TOK, D), line1=low(3, TOK, D), mine1=wide(TOK, D),
    pair2=low(4, TOK, D), line2=low(3, TOK, D), mine2=wide(TOK, D), pair3=low(4, TOK, D), line3=low(3, TOK, D),
    residual_grad=wide(TOK, D), branch=low(TOK, D), branch_part=low(SEQ, 128), attended_grad=low(TOK, D),
    attended_back=low(SEQ, 128), attended_all=low(SEQ, D), key_grad=wide(SEQ, 128), value_grad=wide(SEQ, 128),
    qkv_grad=low(SEQ, 256), gain_sum=wide(8, D),
    x_sent=DMA((7,)), x_got=DMA((7,)), n_sent=DMA((7,)), n_got=DMA((7,)), g_sent=DMA((7,)), g_got=DMA((7,)),
    o_sent=DMA((7,)), o_got=DMA((7,)), h_sent=DMA((7,)), h_got=DMA((7,)), t_sent=DMA((7,)), t_got=DMA((7,)),
    p_sent=DMA((8,)), p_got=DMA((8,)), w_sent=DMA((16,)), w_got=DMA((16,)), a_sent=DMA((8,)), a_got=DMA((8,)),
    e_sent=DMA((4, 4, 8)), e_got=DMA((4, 4, 8)), f_sent=DMA((2, 8)), f_got=DMA((2, 8)), c_sent=DMA((8,)),
    c_got=DMA((8,)), b_sent=DMA((8,)), b_got=DMA((8,)), d_sent=DMA((8,)), d_got=DMA((8,)), l_sent=DMA((8,)),
    l_got=DMA((8,)), s1_sent=DMA((7,)), s1_got=DMA((7,)), s2_sent=DMA((7,)), s2_got=DMA((7,)),
    s3_sent=DMA((7,)), s3_got=DMA((7,)), load=DMA((5,)), store=DMA((4, 3)),
)


def is_far(name):
    return name in OUTS and OUTS[name].memory_space != pltpu.VMEM or name in ("gate_in", "up_in", "down_in")


def spec(name):
    return pl.BlockSpec(memory_space=pl.ANY if is_far(name) else pltpu.VMEM)


def layer(**arrays):
    names = list(arrays) + list(OUTS) + list(SCRATCH)

    def kernel(*refs):
        r = SimpleNamespace(**dict(zip(names, refs)))
        r.hidden_one, r.w_out_all = r.slot_grad.at[0:SEQ], r.places.at[:, 0:D]
        r.scores, r.probs = r.wide_a.at[0:256], r.rows.at[0:256]
        r.w_out_part, r.attended_head = r.qkv_grad.at[:, 0:128], r.qkv_grad.at[:, 128:256]
        r.extra_all = r.key_grad
        back(r, front(r))

    outs = pl.pallas_call(
        kernel,
        out_shape=[jax.ShapeDtypeStruct(OUTS[n].shape, OUTS[n].dtype) for n in OUTS],
        in_specs=[spec(n) for n in arrays],
        out_specs=[spec(n) for n in OUTS],
        scratch_shapes=list(SCRATCH.values()),
        name="layer",
        compiler_params=pltpu.CompilerParams(
            collective_id=0, has_side_effects=True, vmem_limit_bytes=510 << 17
        ),
    )(*arrays.values())
    return dict(zip(OUTS, outs))


def hand_on(*refs):
    come, go = refs[-2:]
    loads = [pltpu.make_async_copy(refs[n], refs[18 + n], come.at[n]) for n in range(9)]
    stores = [pltpu.make_async_copy(refs[18 + n], refs[9 + n], go.at[n]) for n in range(9)]
    for copy in loads:
        copy.start()
    for load, store in zip(loads, stores):
        load.wait()
        store.start()
    for copy in stores:
        copy.wait()


def handed_on(*arrays):
    return pl.pallas_call(
        hand_on,
        out_shape=[jax.ShapeDtypeStruct(a.shape, a.dtype) for a in arrays],
        in_specs=[pl.BlockSpec(memory_space=pl.ANY)] * 9,
        out_specs=[pl.BlockSpec(memory_space=pl.ANY)] * 9,
        scratch_shapes=[pltpu.VMEM(a.shape, a.dtype) for a in arrays] + [DMA((9,)), DMA((9,))],
        name="hand_on",
    )(*arrays)


def shards(
    tokens, segments, routes, gain_attn, gain_ffn, w_query, w_key, w_value, w_out, w_router, w_gate, w_up,
    w_down, cotangent,
):
    extra = jnp.concatenate(
        [w_router, gain_attn[:, None], gain_ffn[:, None], jnp.zeros((8, 94), LOW)], axis=1
    ).astype(WIDE)
    angle = np.arange(SEQ, dtype=np.float32)[:, None] * (
        np.float32(10000.0) ** (-np.arange(32, dtype=np.float32) / np.float32(32))
    )
    waves = np.concatenate([np.cos(angle), np.cos(angle), -np.sin(angle), np.sin(angle)], axis=1)
    made = layer(
        tokens=tokens, routes=routes.T, w_query=w_query, w_key=w_key, w_value=w_value, w_out=w_out,
        extra=extra, seg_row=segments, table=jnp.asarray(waves.astype(np.float32)), cotangent=cotangent,
        gate_in=w_gate.reshape(4, 4, 4, 64, 512), up_in=w_up.reshape(4, 4, 4, 64, 512),
        down_in=w_down.reshape(4, 4, 4, 32, D),
    )
    others = made["others_out"]
    output, input_grad, query, key, value, out, gate, up, down = handed_on(
        made["output"], made["input_grad"], made["query_out"], made["key_out"], made["value_out"],
        made["out_out"], made["gate_out"], made["up_out"], made["down_out"],
    )
    return (
        output, input_grad, others[:, 32], others[:, 33], query, key, value, out, others[:, 0:32], gate, up, down,
    )


def solution(mesh):
    line, dense = P(("dp", "expert")), P(("dp", "expert"), None)
    copied, summed = P("expert", None, None), P("expert", "dp", None)
    return jax.shard_map(
        shards,
        mesh=mesh,
        in_specs=(dense, P("dp", None), dense, line, line) + (dense,) * 5 + (copied,) * 3 + (dense,),
        out_specs=(dense, dense, line, line) + (dense,) * 5 + (summed,) * 3,
        check_vma=False,
    )
```

time: 3570 us -> 218 us (0.06)
  waiting for transfers between devices: 3170 us -> 0 us
  Pallas kernels: 0 us -> 211 us
  blocking collectives: 168 us -> 0 us
  matrix products: 83 us -> 0 us
  local copies, waits for them, and re-layouts: 72.9 us -> 4.31 us
    reduce_scatter x7 -> x0, waiting for transfers between devices: 2720 us -> none  [the longest x1 641 us: shards(): lax.psum_scatter(query_w_grad, ('dp', 'expert'), scatter_dimension=0, til...]
    pallas_call x0 -> x2, Pallas kernels: none -> 211 us  [the longest x1 208 us: layer(): pl.pallas_call(kernel, out_shape=[jax.ShapeDtypeStruct(OUTS[n].shape, OUT...]
    all_gather x6 -> x0, waiting for transfers between devices: 178 us -> none  [the longest x1 61.6 us: shards(): lax.all_gather(w_out, ('dp', 'expert'), axis=0, tiled=True)]
    unnamed x19 -> x0, waiting for transfers between devices: 156 us -> none
    unnamed x2 -> x0, blocking collectives: 134 us -> none
    all_to_all x4 -> x0, waiting for transfers between devices: 117 us -> none  [the longest x1 35.3 us: shards(): lax.all_to_all(send_rows, 'expert', split_axis=0, concat_axis=1, tiled=True)]
    dot_general x30 -> x0, matrix products: 83 us -> none  [the longest x5 12.1 us: lead_dot(): lax.dot_general(factor_one, factor_two, (((0,), (0,)), ((), ())), preferr...]
  transfers between devices with their start and end apart: 20 -> 0, of which waited for: 17 -> 0; matrix products, arithmetic and copies ran while one was open for 4% -> 0% of each run, Pallas kernels for 0% -> 0%
where the time goes in v1:
time: 218 us; the launch traced here: 217 us
  Pallas kernels  211 us (97%)
  local copies, waits for them, and re-layouts  4.31 us (2%)
    pallas_call x1, Pallas kernels, layer(): pl.pallas_call(kernel, out_shape=[jax.ShapeDtypeStruct(OUTS[n].shape, OUT...  208 us

profile of v1, /device:TPU:1, one launch (start us, length us, event | category | flops | bytes accessed | tf_op | source)
XLA Modules:
  0.0 217.3 jit_solution(9659860932229611797)
XLA Ops:
  0.7 0.1 pad.3.clone
  0.7 0.7 copy.29
  1.5 0.7 copy.30
  2.2 1.3 maximum_convert_fusion.refs_6_
  3.6 208.3 %layer.1 = (bf16[128,1024]{1,0:T(8,128)(2,1)}, f32[128,1024]{1,0:T(8,128)}, f32[8,1024]{1,0:T(8,128)}, f32[8,512]{1,0:T(8,128)}, f32[8,512]{1,0:T(8,128)}, /*ind...) custom-call(bf16[128,1024]{1,0:T(8,128)(2,1)} %refs_0_.1, ...), custom_call_target="tpu_custom_call" | custom-call | tf_op jit(solution)/shard_map/layer/pallas_call | solution.py:968
  211.9 2.6 %hand_on.1 = (bf16[128,1024]{1,0:T(8,128)(2,1)}, f32[128,1024]{1,0:T(8,128)}, f32[8,1024]{1,0:T(8,128)}, f32[8,512]{1,0:T(8,128)}, f32[8,512]{1,0:T(8,128)}, /*i...) custom-call(bf16[128,1024]{1,0:T(8,128)(2,1)} %get-tuple-element.31.refs_0_, ...), custom_call_target="tpu_custom_call" | custom-call | tf_op jit(solution)/shard_map/hand_on/pallas_call | solution.py:996
  214.6 1.5 slice_reduce_fusion
  216.0 1.3 copy.32
  (1 shorter events, 0.0 us)

commit v2 on v1

--- a/solution.py
+++ b/solution.py
@@ -64,30 +64,70 @@
     return ref.at[:, pl.ds(pl.multiple_of(block * size, size), size)]
 
 
+def got(ref, semaphore, at):
+    pltpu.make_async_remote_copy(
+        src_ref=ref, dst_ref=ref, send_sem=semaphore, recv_sem=semaphore, device_id=at.sibling, device_id_type=MESH
+    ).wait_recv()
+
+
+def gone(ref, semaphore, at):
+    pltpu.make_async_remote_copy(
+        src_ref=ref, dst_ref=ref, send_sem=semaphore, recv_sem=semaphore, device_id=at.sibling, device_id_type=MESH
+    ).wait_send()
+
+
 class Gather:
-    def __init__(self, at, source, target, sent, got):
-        self.at, self.source, self.target, self.sent, self.got = at, source, target, sent, got
+    def __init__(self, at, source, target, sems):
+        self.at, self.source, self.target, self.sems = at, source, target, sems
 
     def start(self):
-        at, mine = self.at, self.target(self.at.j)
-        self.copies = [
-            send(self.source, mine, self.sent.at[k], self.got.at[k], z_peer(at, step))
-            for k, step in enumerate(Z_STEPS)
-        ]
-        self.copies.append(send(self.source, mine, self.sent.at[3], self.got.at[3], at.sibling))
+        at, mine = self.at, rows(self.target, self.at.j)
+        for k, step in enumerate(Z_STEPS):
+            send(self.source, mine, self.sems.at[0], self.sems.at[1 + k], z_peer(at, step))
+        send(self.source, mine, self.sems.at[0], self.sems.at[4], at.sibling)
 
     def forward(self):
         at = self.at
         for k, step in enumerate(Z_STEPS):
-            self.copies[k].wait_recv()
-            block = self.target(plus(at.z, 4 - step, 4) * 2 + at.c)
-            self.copies.append(send(block, block, self.sent.at[4 + k], self.got.at[4 + k], at.sibling))
+            block = rows(self.target, plus(at.z, 4 - step, 4) * 2 + at.c)
+            got(block, self.sems.at[1 + k], at)
+            send(block, block, self.sems.at[0], self.sems.at[4], at.sibling)
 
     def finish(self):
-        for copy in self.copies[3:]:
-            copy.wait_recv()
-        for copy in self.copies:
-            copy.wait_send()
+        got(self.target.at[0 : 4 * TOK], self.sems.at[4], self.at)
+        gone(self.target.at[0 : 7 * TOK], self.sems.at[0], self.at)
+
+
+class Shares:
+    def __init__(self, at, source, target, seven, sems):
+        self.at, self.seven, self.sems = at, seven, sems
+        for step in range(1, 8):
+            other = plus(at.j, step, 8)
+            send(source(other), target, sems.at[0], sems.at[1], (at.i, other))
+
+    def wait_recv(self):
+        got(self.seven, self.sems.at[1], self.at)
+
+    def wait_send(self):
+        gone(self.seven, self.sems.at[0], self.at)
+
+
+class Spread:
+    def __init__(self, at, source, target, four, three, sems):
+        self.at, self.four, self.three, self.sems = at, four, three, sems
+        for step in range(1, 16):
+            y = step // 4
+            send(source, target, sems.at[0, y], sems.at[1, y], xy_peer(at, step % 4, y))
+
+    def wait_recv(self):
+        got(self.three, self.sems.at[1, 0], self.at)
+        for step in range(1, 4):
+            got(self.four(plus(self.at.y, 4 - step, 4)), self.sems.at[1, step], self.at)
+
+    def wait_send(self):
+        gone(self.three, self.sems.at[0, 0], self.at)
+        for step in range(1, 4):
+            gone(self.four(plus(self.at.y, 4 - step, 4)), self.sems.at[0, step], self.at)
 
 
 def greet(devices):
@@ -123,30 +163,26 @@
     return jnp.where(low_lanes, table, other), jnp.where(low_lanes, other, table)
 
 
-def both_heads(values, low_lanes):
-    zero = jnp.zeros_like(values)
-    return jnp.concatenate(
-        [jnp.where(low_lanes, values, zero), jnp.where(low_lanes, zero, values)], axis=0
-    )
-
-
-def allowed_keys(r, token, start, length):
-    query_segment, key_segment = r.seg_col[token, :], r.seg_row[:, 0:length].astype(WIDE)
-    key_place = lax.broadcasted_iota(jnp.int32, (16, length), 1)
-    query_place = lax.broadcasted_iota(jnp.int32, (16, length), 0) + start
-    return (key_segment == query_segment) & (key_place <= query_place)
+def allowed(r, b, c):
+    keep = None
+    if c == 0 or b == 3:
+        keep = r.log_total[256 * b : 256 * (b + 1), 2:3] == r.seg_row[:, 256 * c : 256 * (c + 1)].astype(WIDE)
+    if b == c:
+        below = lanes((256, 256)) <= lax.broadcasted_iota(jnp.int32, (256, 256), 0)
+        keep = below if keep is None else keep & below
+    return keep
+
+
+def one_head(values, head):
+    return jnp.where((lanes(values.shape) < 64) == (head == 0), values, jnp.zeros_like(values))
 
 
 def front(r):
     at = place()
     ready = greet(expert_peers(at) + dp_peers(at))
-    loads = []
-    for n, (source, target) in enumerate(((r.gate_in, r.gate), (r.up_in, r.up), (r.down_in, r.down))):
-        loads.append(pltpu.make_async_copy(source, target, r.load.at[n]))
-        loads[-1].start()
 
     query_w, key_w = r.w_query[...].astype(WIDE), r.w_key[...].astype(WIDE)
-    value_w, out_w, extra = r.w_value[...].astype(WIDE), r.w_out[...].astype(WIDE), r.extra[...]
+    value_w = r.w_value[...].astype(WIDE)
     low_lanes = lanes((8, 128)) < 64
     for j in range(8):
         tile = slice(128 * (j // 2), 128 * (j // 2) + 128)
@@ -157,63 +193,76 @@
             value_part = pltpu.roll(value_part, 64, axis=1)
         head = slice(128 * j, 128 * j + 128)
         r.pack[j] = jnp.concatenate(
-            [query_w[:, head], jnp.where(low_lanes, key_part, value_part), out_w[:, head], extra], axis=0
-        ).astype(LOW)
+            [query_w[:, head], jnp.where(low_lanes, key_part, value_part), r.extra[...]], axis=0
+        )
+    r.out_mine[...] = r.w_out[...].astype(WIDE)
+    r.near[at.j] = r.pack[at.j]
     expert = lax.broadcasted_iota(jnp.int32, (128, TOK), 0)
     named = jnp.zeros((128, TOK), WIDE)
     for k in range(8):
         named = named + jnp.where(r.routes[k : k + 1, :] == expert, 1.0, 0.0)
     rows(r.named, at.j)[...] = jnp.transpose(named).astype(LOW)
     rows(r.hidden_one, at.j)[...] = r.tokens[...]
-    r.stage[lax.div(at.j, 4), pl.ds(pl.multiple_of(lax.rem(at.j, 4) * 32, 32), 32)] = r.pack[at.j]
     for b in range(8):
         here = slice(TOK * b, TOK * (b + 1))
         across = jnp.broadcast_to(r.seg_row[:, here].astype(WIDE), (TOK, TOK))
-        r.seg_col[here, :] = jnp.transpose(across)[:, 0:1]
+        r.log_total[here, :] = jnp.transpose(across)
 
     ready()
-    tokens = Gather(at, r.tokens, lambda b: rows(r.hidden_one, b), r.x_sent, r.x_got)
+    pair = send(r.out_mine, r.out_other, r.q_sems.at[0], r.q_sems.at[1], at.sibling)
+    first = Shares(at, lambda b: r.pack.at[b], r.near.at[at.j], r.near.at[0:7], r.p_sems)
+    tokens = Gather(at, r.tokens, r.hidden_one, r.x_sems)
     tokens.start()
-    first = []
-    place_in_stage = r.stage.at[lax.div(at.j, 4), pl.ds(pl.multiple_of(lax.rem(at.j, 4) * 32, 32), 32)]
-    for step in range(1, 8):
-        other = plus(at.j, step, 8)
-        first.append(
-            send(r.pack.at[other], place_in_stage, r.p_sent.at[step], r.p_got.at[step], (at.i, other))
-        )
-    marks = Gather(at, rows(r.named, at.j), lambda b: rows(r.named, b), r.n_sent, r.n_got)
+    pair.wait_recv()
+    mine, other = r.out_mine[...], r.out_other[...]
+    both = jnp.where(
+        at.c == 0,
+        jnp.concatenate([mine[:, 0:512], other[:, 0:512]], axis=0),
+        jnp.concatenate([other[:, 512:1024], mine[:, 512:1024]], axis=0),
+    )
+    line = rows(r.out_rows, at.z, 16)
+    line[...] = both.astype(LOW)
+    for step in Z_STEPS:
+        send(line, line, r.q_sems.at[2], r.q_sems.at[3], z_peer(at, step))
+    marks = Gather(at, rows(r.named, at.j), r.named, r.n_sems)
     marks.start()
-    for copy in first:
-        copy.wait_recv()
-    second = []
-    for step in range(1, 16):
-        second.append(
-            send(
-                r.stage, r.dense.at[:, at.y, at.x], r.w_sent.at[step], r.w_got.at[step],
-                xy_peer(at, step % 4, step // 4),
-            )
-        )
-    r.dense[:, at.y, at.x] = r.stage[...]
+    loads = []
+    for n, (source, target) in enumerate(((r.gate_in, r.gate), (r.up_in, r.up), (r.down_in, r.down))):
+        loads.append(pltpu.make_async_copy(source, target, r.load.at[n]))
+        loads[-1].start()
+    first.wait_recv()
+    for b in range(8):
+        r.stage[16 * b : 16 * (b + 1)] = r.near[b, 0:16].astype(LOW)
+    r.stage[128:192] = jnp.concatenate([r.near[b, 16:24] for b in range(8)], axis=0).astype(LOW)
+    second = Spread(
+        at, r.stage, r.dense.at[at.y, at.x, 0:192], lambda y: r.dense.at[y, :, 0:192], r.dense.at[0, 0:3, 0:192],
+        r.w_sems,
+    )
+    r.dense[at.y, at.x, 0:192] = r.stage[...]
+    half = pl.ds(pl.multiple_of(at.c * 512, 512), 512)
+    out_half = r.w_out_all.at[pl.ds(pl.multiple_of(at.i * 64, 64), 64), half]
+    got(r.out_rows.at[0:48], r.q_sems.at[3], at)
+    third = Spread(
+        at, r.out_rows, out_half, lambda y: r.w_out_all.at[pl.ds(pl.multiple_of(y * 256, 256), 256), half],
+        r.w_out_all.at[0:192, half], r.o_sems,
+    )
+    out_half[...] = r.out_rows[...]
     tokens.forward()
     rows(r.upstream, at.j)[...] = r.cotangent[...]
-    upstream = Gather(at, r.cotangent, lambda b: rows(r.upstream, b), r.g_sent, r.g_got)
+    upstream = Gather(at, r.cotangent, r.upstream, r.g_sems)
     upstream.start()
-    for copy in second:
-        copy.wait_recv()
+    second.wait_recv()
 
     def unpack(i, _):
-        part = r.dense[:, lax.div(i, 4), lax.rem(i, 4)].reshape(8, 32, 128).astype(WIDE)
+        part = r.dense[lax.div(i, 4), lax.rem(i, 4), 0:192].astype(WIDE)
         here = pl.ds(pl.multiple_of(i * 64, 64), 64)
-        r.w_qkv[here, 0:128] = part[:, 0:8, :].reshape(64, 128).astype(LOW)
-        r.w_qkv[here, 128:256] = part[:, 8:16, :].reshape(64, 128).astype(LOW)
-        r.w_out_part[here, :] = part[:, 16:24, :].reshape(64, 128).astype(LOW)
-        r.extra_all[here, :] = part[:, 24:32, :].reshape(64, 128)
+        heads = part[0:128].reshape(8, 16, 128)
+        r.w_qkv[here, 0:128] = heads[:, 0:8, :].reshape(64, 128).astype(LOW)
+        r.w_qkv[here, 128:256] = heads[:, 8:16, :].reshape(64, 128).astype(LOW)
+        r.extra_all[here, :] = part[128:192]
         return 0
 
     lax.fori_loop(0, 16, unpack, 0)
-    out_weights = Gather(at, r.w_out_part, lambda b: columns(r.w_out_all, b), r.o_sent, r.o_got)
-    out_weights.start()
-    columns(r.w_out_all, at.j)[...] = r.w_out_part[...]
     r.gains[...] = extra_rows(r)
     r.router[...] = jnp.where(lanes((D, 128)) < 32, r.extra_all[...], 0.0).astype(LOW)
     tokens.finish()
@@ -242,73 +291,70 @@
     hidden_save = pltpu.make_async_copy(r.hidden_one, r.hidden_far, r.load.at[3])
     hidden_save.start()
 
-    low_lanes = lanes((TOK, 128)) < 64
-    returned = []
-    for b in range(8):
-        length = TOK * (b + 1)
-        both = both_heads(r.queries[TOK * b : TOK * (b + 1), :], low_lanes)
-        r.scores[:, 0:length] = tail_dot(both, r.keys[0:length, :])
-
-        def strip(t, _):
-            token = pl.ds(pl.multiple_of(TOK * b + 16 * t, 16), 16)
-            allowed = allowed_keys(r, token, TOK * b + 16 * t, length)
-            logs = []
-            for head in range(2):
-                line = pl.ds(pl.multiple_of(TOK * head + 16 * t, 16), 16)
-                scores = jnp.where(allowed, r.scores[line, 0:length] * SCALE, -1e30)
-                top = jnp.max(scores, axis=-1, keepdims=True)
-                powers = jnp.exp(scores - top)
-                total = jnp.sum(powers, axis=-1, keepdims=True)
-                r.probs[line, 0:length] = (powers * (1.0 / total)).astype(LOW)
-                logs.append(top + jnp.log(total))
-            lane = lanes((16, 128))
-            r.log_total[token, :] = jnp.where(lane == 0, logs[0], jnp.where(lane == 1, logs[1], 0.0))
-            return 0
-
-        lax.fori_loop(0, 8, strip, 0)
-        mixed = dot(r.probs[:, 0:length], r.values[0:length, :])
-        r.attended_head[TOK * b : TOK * (b + 1), :] = jnp.where(low_lanes, mixed[0:TOK], mixed[TOK:]).astype(LOW)
-        copy = pltpu.make_async_remote_copy(
-            src_ref=r.attended_head.at[TOK * b : TOK * (b + 1)], dst_ref=columns(r.attended, at.j), send_sem=r.a_sent.at[b],
-            recv_sem=r.a_got.at[at.j], device_id=(at.i, jnp.int32(b)), device_id_type=MESH,
+    low_lanes = lanes((256, 128)) < 64
+    scores = (r.wide_a, r.wide_b)
+    for b in range(4):
+        here = slice(256 * b, 256 * (b + 1))
+        logs, heads = [], []
+        for head in range(2):
+            query = one_head(r.queries[here, :], head) * SCALE
+            top = jnp.full((256, 256), -1e30, WIDE)
+            for c in range(b + 1):
+                part = slice(256 * c, 256 * (c + 1))
+                score, keep = tail_dot(query, r.keys[part, :]), allowed(r, b, c)
+                if keep is not None:
+                    score = jnp.where(keep, score, -1e30)
+                scores[head][0:256, part] = score
+                top = jnp.maximum(top, score)
+            top = jnp.max(top, axis=-1, keepdims=True)
+            mixed = jnp.zeros((256, 128), WIDE)
+            for c in range(b + 1):
+                part = slice(256 * c, 256 * (c + 1))
+                powers = jnp.exp(scores[head][0:256, part] - top).astype(LOW)
+                value = r.values[part, :]
+                mixed = mixed + dot(powers, jnp.where(low_lanes == (head == 0), value, jnp.ones_like(value)))
+            total = mixed[:, 64:65] if head == 0 else mixed[:, 0:1]
+            heads.append(mixed / total)
+            logs.append(top + jnp.log(total))
+        r.attended_head[here, :] = jnp.where(low_lanes, heads[0], heads[1]).astype(LOW)
+        lane = lanes((256, 128))
+        r.log_total[here, :] = jnp.where(
+            lane == 0, logs[0], jnp.where(lane == 1, logs[1], r.log_total[here, :])
         )
-        returned.append(copy)
-
-        @pl.when(at.j != b)
-        def _():
-            copy.start()
-
-        @pl.when(at.j == b)
-        def _():
-            columns(r.attended, at.j)[...] = r.attended_head[TOK * b : TOK * (b + 1), :]
-
-        if b == 3:
-            upstream.forward()
-        if b == 6:
-            out_weights.forward()
-    out_weights.finish()
-    for b in range(8):
-
-        @pl.when(at.j != b)
-        def _():
-            returned[b].wait_send()
-            pltpu.make_async_remote_copy(
-                src_ref=r.attended_head.at[TOK * b : TOK * (b + 1)], dst_ref=r.attended.at[:, 128 * b : 128 * b + 128],
-                send_sem=r.a_sent.at[b], recv_sem=r.a_got.at[b], device_id=at.sibling, device_id_type=MESH,
-            ).wait_recv()
+        for n in (2 * b, 2 * b + 1):
+
+            @pl.when(at.j != n)
+            def _():
+                send(
+                    r.attended_head.at[TOK * n : TOK * (n + 1)], columns(r.attended, at.j), r.a_sems.at[0],
+                    r.a_sems.at[1], (at.i, jnp.int32(n)),
+                )
+
+            @pl.when(at.j == n)
+            def _():
+                columns(r.attended, at.j)[...] = r.attended_head[TOK * n : TOK * (n + 1), :]
+
+    third.wait_recv()
+    out_mine = columns(r.w_out_all, at.c, 512)
+    whole = send(out_mine, out_mine, r.q_sems.at[4], r.q_sems.at[5], at.sibling)
+    upstream.forward()
+    got(r.attended.at[:, 0 : 7 * 128], r.a_sems.at[1], at)
+    whole.wait_recv()
 
     residual = r.tokens[...].astype(WIDE) + dot(r.attended[...], r.w_out_all[...])
     r.residual[...] = residual
     inverse = lax.rsqrt(jnp.mean(residual * residual, axis=-1, keepdims=True) + EPSILON)
     rows(r.hidden_two, at.j)[...] = (residual * inverse * r.gains[1:2, :]).astype(LOW)
-    hidden = Gather(at, rows(r.hidden_two, at.j), lambda b: rows(r.hidden_two, b), r.h_sent, r.h_got)
+    hidden = Gather(at, rows(r.hidden_two, at.j), r.hidden_two, r.h_sems)
     hidden.start()
     out_save = pltpu.make_async_copy(r.w_out_all, r.out_far, r.load.at[4])
     out_save.start()
-    attended = Gather(at, r.attended, lambda b: rows(r.attended_all, b), r.t_sent, r.t_got)
+    attended = Gather(at, r.attended, r.attended_all, r.t_sems)
     rows(r.attended_all, at.j)[...] = r.attended[...]
-    for copy in first + second:
+    for copy in (first, second, third, pair, whole):
         copy.wait_send()
+    gone(r.out_rows.at[0:48], r.q_sems.at[2], at)
+    gone(r.attended_head.at[0 : 7 * TOK], r.a_sems.at[0], at)
     upstream.finish()
     marks.finish()
     hidden_save.wait()
@@ -328,88 +374,76 @@
     return jnp.concatenate(picked, axis=1)
 
 
-def got(ref, semaphore, at):
-    pltpu.make_async_remote_copy(
-        src_ref=ref, dst_ref=ref, send_sem=semaphore, recv_sem=semaphore, device_id=at.sibling, device_id_type=MESH
-    ).wait_recv()
-
-
-def gone(ref, semaphore, at):
-    pltpu.make_async_remote_copy(
-        src_ref=ref, dst_ref=ref, send_sem=semaphore, recv_sem=semaphore, device_id=at.sibling, device_id_type=MESH
-    ).wait_send()
-
-
 class SumXY:
-    def __init__(self, at, source, ways, sent, got_sems, x_first, height):
-        self.at, self.source, self.ways, self.sent, self.got_sems = at, source, ways, sent, got_sems
-        self.x_first, self.height = x_first, height
-        self.f, self.s = (at.x, at.y) if x_first else (at.y, at.x)
-
-    def block(self, first, second):
-        return self.source.at[second, first] if self.x_first else self.source.at[first, second]
-
-    def neighbour(self, along_first, step):
-        return xy_peer(self.at, step, 0) if along_first == self.x_first else xy_peer(self.at, 0, step)
-
-    def out(self, k, ref, target, along_first, step):
-        send(ref, target, self.sent.at[k], self.got_sems.at[k], self.neighbour(along_first, step))
-
-    def take(self, k, ref):
-        got(ref, self.got_sems.at[k], self.at)
+    def __init__(self, at, sources, ways, sems, height):
+        self.at, self.sources, self.ways, self.sems, self.height = at, sources, ways, sems, height
+
+    def place(self, n):
+        return (self.at.x, self.at.y) if n == 0 else (self.at.y, self.at.x)
+
+    def block(self, n, first, second):
+        return self.sources[n].at[second, first] if n == 0 else self.sources[n].at[first, second]
+
+    def out(self, n, k, way, ref, second, step):
+        device = xy_peer(self.at, step, 0) if (n == 0) != second else xy_peer(self.at, 0, step)
+        send(ref, self.ways[k].at[n, way], self.sems.at[k, 0], self.sems.at[k, 1], device)
+
+    def take(self, k):
+        got(self.ways[k], self.sems.at[k, 1], self.at)
 
     def step1(self):
-        far = plus(self.f, 2, 4)
-        self.out(0, self.block(far, pl.ds(0, 2)), self.ways[0].at[0], True, 1)
-        self.out(1, self.block(far, pl.ds(2, 2)), self.ways[0].at[1], True, 3)
+        for n in range(2):
+            far = plus(self.place(n)[0], 2, 4)
+            self.out(n, 0, 0, self.block(n, far, pl.ds(0, 2)), False, 1)
+            self.out(n, 0, 1, self.block(n, far, pl.ds(2, 2)), False, 3)
 
     def step2(self):
-        for k, step in enumerate((1, 3)):
-            self.take(k, self.ways[0].at[k])
-            near = plus(self.f, step, 4)
-            part = self.block(near, pl.ds(2 * k, 2))
-            part[...] = part[...] + self.ways[0][k]
-            self.out(2 + k, self.block(near, pl.ds(0, 4)), self.ways[1].at[k], True, step)
+        self.take(0)
+        for n in range(2):
+            for k, step in enumerate((1, 3)):
+                near = plus(self.place(n)[0], step, 4)
+                part = self.block(n, near, pl.ds(2 * k, 2))
+                part[...] = part[...] + self.ways[0][n, k]
+                self.out(n, 1, k, self.block(n, near, pl.ds(0, 4)), False, step)
 
     def step3(self):
-        for k in range(2):
-            self.take(2 + k, self.ways[1].at[k])
-        mine = self.block(self.f, pl.ds(0, 4))
-        mine[...] = mine[...] + (self.ways[1][0] + self.ways[1][1])
-        half, far = self.height // 2, self.block(self.f, plus(self.s, 2, 4))
-        self.out(4, far.at[pl.ds(0, half)], self.ways[2].at[0], False, 1)
-        self.out(5, far.at[pl.ds(half, half)], self.ways[2].at[1], False, 3)
+        self.take(1)
+        half = self.height // 2
+        for n in range(2):
+            first, second = self.place(n)
+            mine = self.block(n, first, pl.ds(0, 4))
+            mine[...] = mine[...] + (self.ways[1][n, 0] + self.ways[1][n, 1])
+            far = self.block(n, first, plus(second, 2, 4))
+            self.out(n, 2, 0, far.at[pl.ds(0, half)], True, 1)
+            self.out(n, 2, 1, far.at[pl.ds(half, half)], True, 3)
 
     def step4(self):
+        self.take(2)
         half = self.height // 2
-        for k, step in enumerate((1, 3)):
-            self.take(4 + k, self.ways[2].at[k])
-            near = self.block(self.f, plus(self.s, step, 4))
-            part = near.at[pl.ds(half * k, half)]
-            part[...] = part[...] + self.ways[2][k]
-            self.out(6 + k, near, self.ways[3].at[k], False, step)
+        for n in range(2):
+            first, second = self.place(n)
+            for k, step in enumerate((1, 3)):
+                near = self.block(n, first, plus(second, step, 4))
+                part = near.at[pl.ds(half * k, half)]
+                part[...] = part[...] + self.ways[2][n, k]
+                self.out(n, 3, k, near, True, step)
 
     def step5(self):
-        for k in range(2):
-            self.take(6 + k, self.ways[3].at[k])
-        mine = self.block(self.f, self.s)
-        return mine[...].astype(WIDE) + self.ways[3][0].astype(WIDE) + self.ways[3][1].astype(WIDE)
+        self.take(3)
+        totals = []
+        for n in range(2):
+            mine = self.block(n, *self.place(n))[...].astype(WIDE)
+            totals.append(mine + self.ways[3][n, 0].astype(WIDE) + self.ways[3][n, 1].astype(WIDE))
+        return totals
 
     def finish(self):
-        far = plus(self.f, 2, 4)
-        gone(self.block(far, pl.ds(0, 2)), self.sent.at[0], self.at)
-        gone(self.block(far, pl.ds(2, 2)), self.sent.at[1], self.at)
-        for k, step in enumerate((1, 3)):
-            gone(self.block(plus(self.f, step, 4), pl.ds(0, 4)), self.sent.at[2 + k], self.at)
-            part = self.block(self.f, plus(self.s, 2, 4)).at[pl.ds(self.height // 2 * k, self.height // 2)]
-            gone(part, self.sent.at[4 + k], self.at)
-            gone(self.block(self.f, plus(self.s, step, 4)), self.sent.at[6 + k], self.at)
+        for k in range(4):
+            gone(self.ways[k], self.sems.at[k, 0], self.at)
 
 
 class SumExpert:
-    def __init__(self, at, r, pair_in, line_in, mine, sent, got_sems):
-        self.at, self.r, self.pair_in, self.line_in = at, r, pair_in, line_in
-        self.mine, self.sent, self.got_sems = mine, sent, got_sems
+    def __init__(self, at, r, pair_in, line_in, mine, sems):
+        self.at, self.r, self.pair_in, self.line_in, self.mine, self.sems = at, r, pair_in, line_in, mine, sems
 
     def start(self, tiles):
         at, partial = self.at, self.r.partial
@@ -423,7 +457,7 @@
                 for k, step in enumerate(steps):
                     partial[step, :, part] = made[TOK * k : TOK * (k + 1)].astype(LOW)
             for step in steps:
-                send(partial.at[step], self.pair_in.at[step], self.sent.at[step], self.got_sems.at[step], at.sibling)
+                send(partial.at[step], self.pair_in.at[step], self.sems.at[0], self.sems.at[1 + step], at.sibling)
             return 0
 
         lax.fori_loop(0, 2, to_sibling, 0)
@@ -432,7 +466,7 @@
             steps = (2 + p, 1 - p)
             blocks = [plus(at.z, step, 4) * 2 + at.c for step in steps]
             for step in steps:
-                got(self.pair_in.at[step], self.got_sems.at[step], at)
+                got(self.pair_in.at[step], self.sems.at[1 + step], at)
             for n in range(4):
                 part = slice(256 * n, 256 * (n + 1))
                 made = tiles(*blocks, part)
@@ -450,8 +484,8 @@
 
             def away(step):
                 send(
-                    partial.at[3 + step], self.line_in.at[step - 1], self.sent.at[3 + step],
-                    self.got_sems.at[3 + step], z_peer(at, step),
+                    partial.at[3 + step], self.line_in.at[step - 1], self.sems.at[0], self.sems.at[5],
+                    z_peer(at, step),
                 )
 
             away(steps[0])
@@ -461,13 +495,12 @@
         lax.fori_loop(0, 2, along_z, 0)
 
     def sent_all(self):
-        for k in range(7):
-            gone(self.r.partial.at[k], self.sent.at[k], self.at)
+        gone(self.r.partial, self.sems.at[0], self.at)
 
     def total(self):
         value = self.mine[...]
+        got(self.line_in, self.sems.at[5], self.at)
         for k in range(3):
-            got(self.line_in.at[k], self.got_sems.at[4 + k], self.at)
             value = value + self.line_in[k].astype(WIDE)
         return value
 
@@ -612,21 +645,11 @@
 
 
 def expert_sums(r, at, e):
-    left, right = pl.ds(0, 512), pl.ds(512, 512)
-    made = []
-    for n, (source, x_first, height) in enumerate(
-        (
-            (r.gate.at[e], True, 64),
-            (r.up.at[e], False, 64),
-            (r.down.at[e, :, :, :, left], True, 32),
-            (r.down.at[e, :, :, :, right], False, 32),
-        )
-    ):
-        ways = [
-            (r.wide_ways if n < 2 else r.half_ways)[k].at[e, n % 2] for k in range(4)
-        ]
-        made.append(SumXY(at, source, ways, r.e_sent.at[e, n], r.e_got.at[e, n], x_first, height))
-    return made
+    halves = [r.down.at[e, :, :, :, pl.ds(512 * n, 512)] for n in range(2)]
+    return (
+        SumXY(at, [r.gate.at[e], r.up.at[e]], [way.at[e] for way in r.wide_ways], r.e_sems.at[e, 0], 64),
+        SumXY(at, halves, [way.at[e] for way in r.half_ways], r.e_sems.at[e, 1], 32),
+    )
 
 
 def back(r, attended):
@@ -652,20 +675,13 @@
 
     lax.fori_loop(0, 4, one, 0)
 
-    def share_out(source, target, sent, got_sems):
-        copies = []
-        for step in range(1, 8):
-            other = plus(at.j, step, 8)
-            copies.append(send(source(other), target, sent.at[step], got_sems.at[step], (at.i, other)))
-        return copies
-
-    gate_copies = share_out(lambda b: r.gate_grad.at[b], r.gate_back.at[at.j], r.c_sent, r.c_got)
+    gate_copies = Shares(at, lambda b: r.gate_grad.at[b], r.gate_back.at[at.j], r.gate_back.at[0:7], r.c_sems)
     r.gate_back[pl.ds(at.j, 1)] = r.gate_grad[pl.ds(at.j, 1)]
 
     def two_blocks(ref, a, b):
         return jnp.concatenate([rows(ref, a)[...], rows(ref, b)[...]], axis=0)
 
-    hidden_sum = SumExpert(at, r, r.pair1, r.line1, r.mine1, r.s1_sent, r.s1_got)
+    hidden_sum = SumExpert(at, r, r.pair1, r.line1, r.mine1, r.s_sems.at[0])
     hidden_sum.start(lambda a, b, n: dot(two_blocks(r.places, a, b), r.slot_grad[:, n]))
     made_load = pltpu.make_async_copy(r.made_far, r.slot_grad, r.load.at[3])
     made_load.start()
@@ -677,8 +693,7 @@
     hidden_load.start()
     sums(3, "step2")
     attended.forward()
-    for copy in gate_copies:
-        copy.wait_recv()
+    gate_copies.wait_recv()
     gate_grad = jnp.concatenate(
         [r.gate_back[b][0:4] for b in range(8)] + [jnp.zeros((96, 128), WIDE)], axis=0
     )
@@ -697,67 +712,66 @@
     residual_grad = upstream + scaled * inverse - residual * (inverse * inverse * inverse * mean)
     r.residual_grad[...] = residual_grad
     r.branch[...] = residual_grad.astype(LOW)
-    branch_copies = share_out(lambda b: columns(r.branch, b), rows(r.branch_part, at.j), r.b_sent, r.b_got)
+    branch_copies = Shares(
+        at, lambda b: columns(r.branch, b), rows(r.branch_part, at.j), r.branch_part.at[0 : 7 * TOK], r.b_sems
+    )
     out_load.wait()
     for n in range(4):
         part = slice(256 * n, 256 * (n + 1))
         r.attended_grad[:, part] = tail_dot(r.branch[...], r.hidden_two[part, :]).astype(LOW)
-    grad_copies = share_out(
-        lambda b: columns(r.attended_grad, b), rows(r.attended_back, at.j), r.d_sent, r.d_got
+    grad_copies = Shares(
+        at, lambda b: columns(r.attended_grad, b), rows(r.attended_back, at.j), r.attended_back.at[0 : 7 * TOK],
+        r.d_sems,
     )
     rows(r.branch_part, at.j)[...] = columns(r.branch, at.j)[...]
     rows(r.attended_back, at.j)[...] = columns(r.attended_grad, at.j)[...]
     hidden_sum.sent_all()
 
-    output_sum = SumExpert(at, r, r.pair2, r.line2, r.mine2, r.s2_sent, r.s2_got)
+    output_sum = SumExpert(at, r, r.pair2, r.line2, r.mine2, r.s_sems.at[1])
     made_load.wait()
     output_sum.start(lambda a, b, n: dot(two_blocks(r.places, a, b), r.slot_grad[:, n]))
     sums(0, "step3")
     sums(1, "step3")
-    for copy in grad_copies:
-        copy.wait_recv()
-
-    low_lanes = lanes((TOK, 128)) < 64
+    grad_copies.wait_recv()
+
+    low_lanes = lanes((256, 128)) < 64
     r.key_grad[...] = jnp.zeros((SEQ, 128), WIDE)
     r.value_grad[...] = jnp.zeros((SEQ, 128), WIDE)
-    for b in range(8):
-        length, here = TOK * (b + 1), slice(TOK * b, TOK * (b + 1))
-        both = both_heads(r.queries[here, :], low_lanes)
-        both_grad = both_heads(r.attended_back[here, :], low_lanes)
-        r.wide_a[0:256, 0:length] = tail_dot(both, r.keys[0:length, :])
-        r.wide_b[0:256, 0:length] = tail_dot(both_grad, r.values[0:length, :])
+    for b in range(4):
+        here = slice(256 * b, 256 * (b + 1))
+        heads = []
         for head in range(2):
-
-            def strip(t, _):
-                token = pl.ds(pl.multiple_of(TOK * b + 16 * t, 16), 16)
-                line = pl.ds(pl.multiple_of(TOK * head + 16 * t, 16), 16)
-                allowed = allowed_keys(r, token, TOK * b + 16 * t, length)
-                powers = jnp.exp(r.wide_a[line, 0:length] * SCALE - r.log_total[token, head : head + 1])
-                probs = jnp.where(allowed, powers, 0.0)
-                prob_grad = r.wide_b[line, 0:length]
-                inner = jnp.sum(probs * prob_grad, axis=-1, keepdims=True)
-                r.rows[line, 0:length] = (probs * (prob_grad - inner)).astype(LOW)
-                r.route_grad[line, 0:length] = probs.astype(LOW)
-                return 0
-
-            lax.fori_loop(0, 8, strip, 0, unroll=2)
-        score_grad, probs = r.rows[0:256, 0:length], r.route_grad[0:256, 0:length]
-        query_grad = dot(score_grad, r.keys[0:length, :]) * SCALE
-        query_grad = jnp.where(low_lanes, query_grad[0:TOK], query_grad[TOK:])
-        cosine, sine = angles(r, here, (TOK, 128))
+            query = one_head(r.queries[here, :], head) * SCALE
+            grad = one_head(r.attended_back[here, :], head)
+            inner = grad.astype(WIDE) * r.attended_head[here, :].astype(WIDE)
+            inner = jnp.sum(inner, axis=-1, keepdims=True)
+            log_total = r.log_total[here, head : head + 1]
+            query_grad = jnp.zeros((256, 128), WIDE)
+            for c in range(b + 1):
+                part = slice(256 * c, 256 * (c + 1))
+                probs = jnp.exp(tail_dot(query, r.keys[part, :]) - log_total)
+                keep = allowed(r, b, c)
+                if keep is not None:
+                    probs = jnp.where(keep, probs, 0.0)
+                prob_grad = tail_dot(grad, r.values[part, :])
+                score_grad = (probs * (prob_grad - inner)).astype(LOW)
+                query_grad = query_grad + dot(score_grad, r.keys[part, :])
+                r.key_grad[part, :] += lead_dot(score_grad, query)
+                r.value_grad[part, :] += lead_dot(probs.astype(LOW), grad)
+            heads.append(query_grad)
+        query_grad = jnp.where(low_lanes, heads[0], heads[1]) * SCALE
+        cosine, sine = angles(r, here, (256, 128))
         r.qkv_grad[here, 0:128] = turn(query_grad, cosine, -sine).astype(LOW)
-        r.key_grad[0:length, :] += lead_dot(score_grad, both)
-        r.value_grad[0:length, :] += lead_dot(probs, both_grad)
-        if b == 4:
+        if b == 2:
             sums(2, "step3")
             sums(0, "step4")
-        if b == 6:
-            sums(1, "step4")
+    sums(1, "step4")
+    low_lanes = lanes((TOK, 128)) < 64
 
     def finish_keys(b, _):
         here = pl.ds(pl.multiple_of(b * TOK, TOK), TOK)
         key_grad, value_grad = r.key_grad[here, :], r.value_grad[here, :]
-        key_grad = (key_grad + pltpu.roll(key_grad, 64, axis=1)) * SCALE
+        key_grad = key_grad + pltpu.roll(key_grad, 64, axis=1)
         value_grad = value_grad + pltpu.roll(value_grad, 64, axis=1)
         cosine, sine = angles(r, here, (TOK, 128))
         key_grad = turn(key_grad, cosine, -sine)
@@ -777,11 +791,11 @@
         r.gain_sum[0:1, n] += jnp.sum(made * hidden.astype(WIDE), axis=0, keepdims=True)
         return made
 
-    input_sum = SumExpert(at, r, r.pair3, r.line3, r.mine1, r.s3_sent, r.s3_got)
+    input_sum = SumExpert(at, r, r.pair3, r.line3, r.mine1, r.s_sems.at[2])
     input_sum.start(hidden_one_tile)
 
-    for copy in branch_copies:
-        copy.wait()
+    branch_copies.wait_recv()
+    branch_copies.wait_send()
     attended.finish()
     gain_rows = jnp.concatenate(
         [
@@ -797,23 +811,18 @@
         others = (router_grad[here] + jnp.concatenate(others, axis=0)).astype(LOW)
         for x in range(4):
             part = slice(64 * x, 64 * (x + 1))
-            r.dense[0, m, x, 0:64] = grads[part, 0:128]
-            r.dense[0, m, x, 64:128] = grads[part, 128:256]
-            r.dense[1, m, x, 0:64] = out_grads[part]
-            r.dense[1, m, x, 64:128] = others[part]
-    dense_sums = [
-        SumXY(
-            at, r.dense.at[n], [r.dense1.at[n], r.dense2.at[n], r.dense3.at[n], r.dense4.at[n]],
-            r.f_sent.at[n], r.f_got.at[n], n == 0, 128,
-        )
-        for n in range(2)
-    ]
-    for unit in dense_sums:
-        unit.step1()
+            r.dense[m, x, 0:64] = grads[part, 0:128]
+            r.dense[m, x, 64:128] = grads[part, 128:256]
+            r.dense[m, x, 128:192] = out_grads[part]
+            r.dense[m, x, 192:256] = others[part]
+    dense_sum = SumXY(
+        at, [r.dense.at[:, :, pl.ds(128 * n, 128)] for n in range(2)], (r.dense1, r.dense2, r.dense3, r.dense4),
+        r.f_sems, 128,
+    )
+    dense_sum.step1()
     sums(3, "step3")
     sums(2, "step4")
-    for unit in dense_sums:
-        unit.step2()
+    dense_sum.step2()
 
     def stores(e):
         high = pl.ds(pl.multiple_of(e * 64, 64), 64)
@@ -825,27 +834,27 @@
         ]
 
     def finish_expert(e, _):
-        gate, up, left, right = expert_sums(r, at, e)
+        wide_sum, half_sum = expert_sums(r, at, e)
+        gate, up = wide_sum.step5()
+        left, right = half_sum.step5()
         high = pl.ds(pl.multiple_of(e * 64, 64), 64)
-        r.wide_a[high, 0:512] = gate.step5()
-        r.wide_a[high, 512:1024] = up.step5()
+        r.wide_a[high, 0:512] = gate
+        r.wide_a[high, 512:1024] = up
         low = pl.ds(pl.multiple_of(e * 32, 32), 32)
-        r.wide_b[low, 0:512] = left.step5()
-        r.wide_b[low, 512:1024] = right.step5()
+        r.wide_b[low, 0:512] = left
+        r.wide_b[low, 512:1024] = right
         for copy in stores(e):
             copy.start()
         return 0
 
     lax.fori_loop(0, 3, finish_expert, 0)
     sums(3, "step4")
-    for unit in dense_sums:
-        unit.step3()
+    dense_sum.step3()
     r.branch[...] = (r.residual[...] + output_sum.total()).astype(LOW)
     output_store = pltpu.make_async_copy(r.branch, r.output, r.load.at[0])
     output_store.start()
     finish_expert(3, 0)
-    for unit in dense_sums:
-        unit.step4()
+    dense_sum.step4()
 
     hidden_grad = input_sum.total()
     inputs = r.tokens[...].astype(WIDE)
@@ -857,12 +866,13 @@
     )
     input_store = pltpu.make_async_copy(r.residual_grad, r.input_grad, r.load.at[1])
     input_store.start()
-    for n, unit in enumerate(dense_sums):
-        r.dense_total[n] = unit.step5().reshape(2, 8, 8, 128)
-    last_copies = share_out(lambda b: r.dense_total.at[:, :, b], r.dense_back.at[at.j], r.l_sent, r.l_got)
+    for n, total in enumerate(dense_sum.step5()):
+        r.dense_total[n] = total.reshape(2, 8, 8, 128)
+    last_copies = Shares(
+        at, lambda b: r.dense_total.at[:, :, b], r.dense_back.at[at.j], r.dense_back.at[0:7], r.l_sems
+    )
     r.dense_back[pl.ds(at.j, 1)] = r.dense_total[:, :, pl.ds(at.j, 1)].reshape(1, 2, 2, 8, 128)
-    for copy in last_copies:
-        copy.wait_recv()
+    last_copies.wait_recv()
     low_lanes = lanes((8, 128)) < 64
     others = jnp.zeros((8, 128), WIDE)
     for b in range(8):
@@ -878,7 +888,7 @@
     r.others_out[...] = others
 
     input_sum.sent_all()
-    for copy in gate_copies + grad_copies + last_copies:
+    for copy in (gate_copies, grad_copies, last_copies):
         copy.wait_send()
     output_store.wait()
     input_store.wait()
@@ -891,8 +901,7 @@
         return 0
 
     lax.fori_loop(0, 4, ended, 0)
-    for unit in dense_sums:
-        unit.finish()
+    dense_sum.finish()
 
 DMA = pltpu.SemaphoreType.DMA
 
@@ -918,8 +927,9 @@
 SCRATCH = dict(
     w_qkv=low(D, 256), router=low(D, 128), gains=wide(8, D), queries=low(SEQ, 128), keys=low(SEQ, 128),
     values=low(SEQ, 128), log_total=wide(SEQ, 128), attended=low(TOK, D), residual=wide(TOK, D),
-    hidden_two=low(SEQ, D), upstream=low(SEQ, D), named=low(SEQ, 128), seg_col=wide(SEQ, 1),
-    pack=low(8, 32, 128), stage=low(2, 128, 128),
+    hidden_two=low(SEQ, D), upstream=low(SEQ, D), named=low(SEQ, 128),
+    pack=wide(8, 24, 128), near=wide(8, 24, 128), stage=low(192, 128),
+    out_mine=wide(8, D), out_other=wide(8, D), out_rows=low(64, 512),
     gate=low(4, 4, 4, 64, 512), up=low(4, 4, 4, 64, 512), down=low(4, 4, 4, 32, D),
     shares=wide(TOK, 128), shares_row=wide(32, SEQ), order_row=wide(32, SEQ), places=low(SEQ, 4 * SLOTS),
     rows=low(SLOTS, D), route_grad=low(SLOTS, D), made=low(SLOTS, D), slot_grad=low(4 * SLOTS, D),
@@ -928,7 +938,7 @@
     gate_dot=wide(SLOTS, 1), hidden_own=low(TOK, D),
     wide1=low(4, 2, 2, 2, 64, 512), wide2=low(4, 2, 2, 4, 64, 512), wide3=low(4, 2, 2, 32, 512),
     wide4=low(4, 2, 2, 64, 512), half1=low(4, 2, 2, 2, 32, 512), half2=low(4, 2, 2, 4, 32, 512),
-    half3=low(4, 2, 2, 16, 512), half4=low(4, 2, 2, 32, 512), dense=low(2, 4, 4, 128, 128),
+    half3=low(4, 2, 2, 16, 512), half4=low(4, 2, 2, 32, 512), dense=low(4, 4, 256, 128),
     dense1=low(2, 2, 2, 128, 128), dense2=low(2, 2, 4, 128, 128), dense3=low(2, 2, 64, 128),
     dense4=low(2, 2, 128, 128), dense_total=wide(2, 2, 8, 8, 128), dense_back=wide(8, 2, 2, 8, 128),
     partial=low(7, TOK, D), pair1=low(4, TOK, D), line1=low(3, TOK, D), mine1=wide(TOK, D),
@@ -936,13 +946,10 @@
     residual_grad=wide(TOK, D), branch=low(TOK, D), branch_part=low(SEQ, 128), attended_grad=low(TOK, D),
     attended_back=low(SEQ, 128), attended_all=low(SEQ, D), key_grad=wide(SEQ, 128), value_grad=wide(SEQ, 128),
     qkv_grad=low(SEQ, 256), gain_sum=wide(8, D),
-    x_sent=DMA((7,)), x_got=DMA((7,)), n_sent=DMA((7,)), n_got=DMA((7,)), g_sent=DMA((7,)), g_got=DMA((7,)),
-    o_sent=DMA((7,)), o_got=DMA((7,)), h_sent=DMA((7,)), h_got=DMA((7,)), t_sent=DMA((7,)), t_got=DMA((7,)),
-    p_sent=DMA((8,)), p_got=DMA((8,)), w_sent=DMA((16,)), w_got=DMA((16,)), a_sent=DMA((8,)), a_got=DMA((8,)),
-    e_sent=DMA((4, 4, 8)), e_got=DMA((4, 4, 8)), f_sent=DMA((2, 8)), f_got=DMA((2, 8)), c_sent=DMA((8,)),
-    c_got=DMA((8,)), b_sent=DMA((8,)), b_got=DMA((8,)), d_sent=DMA((8,)), d_got=DMA((8,)), l_sent=DMA((8,)),
-    l_got=DMA((8,)), s1_sent=DMA((7,)), s1_got=DMA((7,)), s2_sent=DMA((7,)), s2_got=DMA((7,)),
-    s3_sent=DMA((7,)), s3_got=DMA((7,)), load=DMA((5,)), store=DMA((4, 3)),
+    x_sems=DMA((5,)), n_sems=DMA((5,)), g_sems=DMA((5,)), h_sems=DMA((5,)), t_sems=DMA((5,)), p_sems=DMA((2,)),
+    c_sems=DMA((2,)), b_sems=DMA((2,)), d_sems=DMA((2,)), l_sems=DMA((2,)), w_sems=DMA((2, 4)),
+    o_sems=DMA((2, 4)), a_sems=DMA((2,)), q_sems=DMA((6,)), e_sems=DMA((4, 2, 4, 2)), f_sems=DMA((4, 2)),
+    s_sems=DMA((3, 6)), load=DMA((5,)), store=DMA((4, 3)),
 )
 
 
@@ -960,8 +967,7 @@
     def kernel(*refs):
         r = SimpleNamespace(**dict(zip(names, refs)))
         r.hidden_one, r.w_out_all = r.slot_grad.at[0:SEQ], r.places.at[:, 0:D]
-        r.scores, r.probs = r.wide_a.at[0:256], r.rows.at[0:256]
-        r.w_out_part, r.attended_head = r.qkv_grad.at[:, 0:128], r.qkv_grad.at[:, 128:256]
+        r.attended_head = r.qkv_grad.at[:, 128:256]
         r.extra_all = r.key_grad
         back(r, front(r))
 

time: 218 us -> 181 us (0.83)
  Pallas kernels: 211 us -> 175 us
    pallas_call x1, Pallas kernels: 208 us -> 172 us  [layer(): pl.pallas_call(kernel, out_shape=[jax.ShapeDtypeStruct(OUTS[n].shape, OUT...]
where the time goes in v2:
time: 181 us
  Pallas kernels  175 us (97%)
  local copies, waits for them, and re-layouts  4.31 us (2%)
    pallas_call x1, Pallas kernels, layer(): pl.pallas_call(kernel, out_shape=[jax.ShapeDtypeStruct(OUTS[n].shape, OUT...  172 us

profile of v2, /device:TPU:1, one launch (start us, length us, event | category | flops | bytes accessed | tf_op | source)
XLA Modules:
  0.0 181.2 jit_solution(16991514891011823662)
XLA Ops:
  0.7 0.1 pad.3.clone
  0.7 0.7 copy.29
  1.5 0.7 copy.30
  2.2 1.3 maximum_convert_fusion.refs_6_
  3.6 172.2 %layer.1 = (bf16[128,1024]{1,0:T(8,128)(2,1)}, f32[128,1024]{1,0:T(8,128)}, f32[8,1024]{1,0:T(8,128)}, f32[8,512]{1,0:T(8,128)}, f32[8,512]{1,0:T(8,128)}, /*ind...) custom-call(bf16[128,1024]{1,0:T(8,128)(2,1)} %refs_0_.1, ...), custom_call_target="tpu_custom_call" | custom-call | tf_op jit(solution)/shard_map/layer/pallas_call | solution.py:974
  175.7 2.6 %hand_on.1 = (bf16[128,1024]{1,0:T(8,128)(2,1)}, f32[128,1024]{1,0:T(8,128)}, f32[8,1024]{1,0:T(8,128)}, f32[8,512]{1,0:T(8,128)}, f32[8,512]{1,0:T(8,128)}, /*i...) custom-call(bf16[128,1024]{1,0:T(8,128)(2,1)} %get-tuple-element.31.refs_0_, ...), custom_call_target="tpu_custom_call" | custom-call | tf_op jit(solution)/shard_map/hand_on/pallas_call | solution.py:1002
  178.4 1.5 slice_reduce_fusion
  179.9 1.3 copy.32
  (1 shorter events, 0.0 us)

commit v3 on v2

--- a/solution.py
+++ b/solution.py
@@ -183,6 +183,11 @@
 
     query_w, key_w = r.w_query[...].astype(WIDE), r.w_key[...].astype(WIDE)
     value_w = r.w_value[...].astype(WIDE)
+    r.corner[...] = jnp.zeros((128, 128), WIDE)
+    r.corner[32:33, 0:8] = r.gain_attn[...].astype(WIDE)
+    r.corner[33:34, 0:8] = r.gain_ffn[...].astype(WIDE)
+    r.extra[...] = jnp.transpose(r.corner[...])[0:8]
+    r.extra[:, 0:32] = r.w_router[...].astype(WIDE)
     low_lanes = lanes((8, 128)) < 64
     for j in range(8):
         tile = slice(128 * (j // 2), 128 * (j // 2) + 128)
@@ -264,7 +269,7 @@
 
     lax.fori_loop(0, 16, unpack, 0)
     r.gains[...] = extra_rows(r)
-    r.router[...] = jnp.where(lanes((D, 128)) < 32, r.extra_all[...], 0.0).astype(LOW)
+    r.router[...] = r.extra_all[...].astype(LOW)
     tokens.finish()
 
     low_lanes = lanes((256, 128)) < 64
@@ -292,7 +297,7 @@
     hidden_save.start()
 
     low_lanes = lanes((256, 128)) < 64
-    scores = (r.wide_a, r.wide_b)
+    scores = ((r.mine1, r.mine2), (r.residual, r.residual_grad))
     for b in range(4):
         here = slice(256 * b, 256 * (b + 1))
         logs, heads = [], []
@@ -304,13 +309,14 @@
                 score, keep = tail_dot(query, r.keys[part, :]), allowed(r, b, c)
                 if keep is not None:
                     score = jnp.where(keep, score, -1e30)
-                scores[head][0:256, part] = score
+                scores[head][0][:, part], scores[head][1][:, part] = score[0:TOK], score[TOK:256]
                 top = jnp.maximum(top, score)
             top = jnp.max(top, axis=-1, keepdims=True)
             mixed = jnp.zeros((256, 128), WIDE)
             for c in range(b + 1):
                 part = slice(256 * c, 256 * (c + 1))
-                powers = jnp.exp(scores[head][0:256, part] - top).astype(LOW)
+                score = jnp.concatenate([scores[head][0][:, part], scores[head][1][:, part]], axis=0)
+                powers = jnp.exp(score - top).astype(LOW)
                 value = r.values[part, :]
                 mixed = mixed + dot(powers, jnp.where(low_lanes == (head == 0), value, jnp.ones_like(value)))
             total = mixed[:, 64:65] if head == 0 else mixed[:, 0:1]
@@ -442,66 +448,62 @@
 
 
 class SumExpert:
-    def __init__(self, at, r, pair_in, line_in, mine, sems):
-        self.at, self.r, self.pair_in, self.line_in, self.mine, self.sems = at, r, pair_in, line_in, mine, sems
-
-    def start(self, tiles):
-        at, partial = self.at, self.r.partial
-
-        def to_sibling(p, _):
+    def __init__(self, at, partial, seven, pair_in, line_in, mine, sems):
+        self.at, self.partial, self.seven = at, partial, seven
+        self.pair_in, self.line_in, self.mine, self.sems = pair_in, line_in, mine, sems
+
+    def across(self, tiles, n):
+        at, part = self.at, slice(256 * n, 256 * (n + 1))
+
+        def one(p, _):
             steps = (2 + p, 1 - p)
-            blocks = [plus(at.z, step, 4) * 2 + 1 - at.c for step in steps]
-            for n in range(4):
-                part = slice(256 * n, 256 * (n + 1))
-                made = tiles(*blocks, part)
-                for k, step in enumerate(steps):
-                    partial[step, :, part] = made[TOK * k : TOK * (k + 1)].astype(LOW)
-            for step in steps:
-                send(partial.at[step], self.pair_in.at[step], self.sems.at[0], self.sems.at[1 + step], at.sibling)
+            made = tiles(*[plus(at.z, step, 4) * 2 + 1 - at.c for step in steps], part)
+            for k, step in enumerate(steps):
+                ref = self.partial(step).at[:, part]
+                ref[...] = made[TOK * k : TOK * (k + 1)].astype(LOW)
+                send(ref, self.pair_in.at[step, :, part], self.sems.at[0], self.sems.at[1 + n], at.sibling)
             return 0
 
-        lax.fori_loop(0, 2, to_sibling, 0)
-
-        def along_z(p, _):
+        lax.fori_loop(0, 2, one, 0)
+
+    def along(self, tiles, n):
+        at, part = self.at, slice(256 * n, 256 * (n + 1))
+
+        def away(step, total):
+            ref = self.partial(3 + step).at[:, part]
+            ref[...] = total.astype(LOW)
+            send(ref, self.line_in.at[step - 1, :, part], self.sems.at[0], self.sems.at[5], z_peer(at, step))
+
+        def one(p, _):
             steps = (2 + p, 1 - p)
-            blocks = [plus(at.z, step, 4) * 2 + at.c for step in steps]
-            for step in steps:
-                got(self.pair_in.at[step], self.sems.at[1 + step], at)
-            for n in range(4):
-                part = slice(256 * n, 256 * (n + 1))
-                made = tiles(*blocks, part)
-                first = made[0:TOK] + self.pair_in[steps[0], :, part].astype(WIDE)
-                second = made[TOK:] + self.pair_in[steps[1], :, part].astype(WIDE)
-                partial[3 + steps[0], :, part] = first.astype(LOW)
-
-                @pl.when(p == 0)
-                def _():
-                    partial[3 + steps[1], :, part] = second.astype(LOW)
-
-                @pl.when(p == 1)
-                def _():
-                    self.mine[:, part] = second
-
-            def away(step):
-                send(
-                    partial.at[3 + step], self.line_in.at[step - 1], self.sems.at[0], self.sems.at[5],
-                    z_peer(at, step),
-                )
-
-            away(steps[0])
-            pl.when(p == 0)(lambda: away(steps[1]))
+            made = tiles(*[plus(at.z, step, 4) * 2 + at.c for step in steps], part)
+            first = made[0:TOK] + self.pair_in[steps[0], :, part].astype(WIDE)
+            second = made[TOK:] + self.pair_in[steps[1], :, part].astype(WIDE)
+            away(steps[0], first)
+
+            @pl.when(p == 0)
+            def _():
+                away(steps[1], second)
+
+            @pl.when(p == 1)
+            def _():
+                self.mine[:, part] = second
+
             return 0
 
-        lax.fori_loop(0, 2, along_z, 0)
+        got(self.pair_in.at[:, :, part], self.sems.at[1 + n], at)
+        lax.fori_loop(0, 2, one, 0)
 
     def sent_all(self):
-        gone(self.r.partial, self.sems.at[0], self.at)
-
-    def total(self):
-        value = self.mine[...]
+        gone(self.seven, self.sems.at[0], self.at)
+
+    def arrived(self):
         got(self.line_in, self.sems.at[5], self.at)
+
+    def total(self, here):
+        value = self.mine[here, :]
         for k in range(3):
-            value = value + self.line_in[k].astype(WIDE)
+            value = value + self.line_in[k, here, :].astype(WIDE)
         return value
 
 
@@ -530,20 +532,28 @@
 
 def share_tokens(r, at):
     def block(b, _):
-        here = pl.ds(pl.multiple_of(b * TOK, TOK), TOK)
+        here = pl.ds(pl.multiple_of(b * 256, 256), 256)
         named = r.named[here, :].astype(WIDE) > 0.0
         logits = jnp.where(named, dot(r.hidden_two[here, :], r.router[...]), -1e30)
         powers = jnp.where(named, jnp.exp(logits - jnp.max(logits, axis=-1, keepdims=True)), 0.0)
         shares = powers / jnp.sum(powers, axis=-1, keepdims=True)
-
-        @pl.when(b == at.j)
+        high, middle, lowest = three_parts(shares)
+        parts = high + pltpu.roll(middle, 32, axis=1) + pltpu.roll(lowest, 64, axis=1)
+        r.share_parts[here, :] = parts.astype(LOW)
+
+        @pl.when(b == at.z)
         def _():
-            r.shares[...] = shares
-
-        r.shares_row[:, here] = jnp.transpose(shares)[0:32]
+            r.shares[...] = jnp.where(at.c == 0, shares[0:TOK], shares[TOK:])
+
         return 0
 
-    lax.fori_loop(0, 8, block, 0)
+    lax.fori_loop(0, 4, block, 0)
+
+
+def three_parts(values):
+    high = values.astype(LOW).astype(WIDE)
+    middle = (values - high).astype(LOW).astype(WIDE)
+    return high, middle, (values - high - middle).astype(LOW).astype(WIDE)
 
 
 def hits(r, at, e, t):
@@ -565,83 +575,67 @@
     for n in range(4):
         part = slice(256 * n, 256 * (n + 1))
         r.slot_grad[here, part] = dot(r.partial[0:3].reshape(SLOTS, SEQ), r.upstream[:, part]).astype(LOW)
+    r.low_grad[here, 512:1024] = tail_dot(r.slot_grad[here, :], r.down[e].reshape(512, D)).astype(LOW)
     return 0
 
 
 def expert(r, at, e):
-    row = pl.ds(4 * at.j + e, 1)
     here = pl.ds(pl.multiple_of(e * SLOTS, SLOTS), SLOTS)
     quarters = [slice(256 * n, 256 * (n + 1)) for n in range(4)]
-
-    def strip(t):
-        return pl.ds(pl.multiple_of(t * 32, 32), 32)
-
-    def slot_strip(t):
-        return pl.ds(pl.multiple_of(e * SLOTS + t * 32, 32), 32)
-
-    def shares(t, _):
-        share = jnp.sum(jnp.where(hits(r, at, e, t), r.shares_row[row, :], 0.0), axis=-1, keepdims=True)
-        r.share[pl.ds(pl.multiple_of(t * TOK, TOK), TOK), :] = share
-        return 0
-
     pick_rows(r, at, e)
-    lax.fori_loop(0, 3, shares, 0)
+    lane = lanes((SLOTS, 128))
+    share = dot(r.partial[0:3].reshape(SLOTS, SEQ), r.share_parts[...])
+    share = jnp.where((lane % 32 == 4 * at.j + e) & (lane < 96), share, 0.0)
+    share = jnp.sum(share, axis=-1, keepdims=True)
     for n in quarters:
-        r.rows[:, n] = dot(r.partial[0:3].reshape(SLOTS, SEQ), r.hidden_two[:, n]).astype(LOW)
-    r.wide_a[:, 0:512] = dot(r.rows[...], r.gate[e].reshape(D, 512))
-    r.wide_a[:, 512:1024] = dot(r.rows[...], r.up[e].reshape(D, 512))
-
-    def activate(t, _):
-        gate_pre = r.wide_a[strip(t), 0:512]
-        silu = gate_pre / (1.0 + jnp.exp(-gate_pre))
-        r.product[strip(t), :] = (silu * r.wide_a[strip(t), 512:1024]).astype(LOW)
-        return 0
-
-    lax.fori_loop(0, 12, activate, 0)
+        r.rows[here, n] = dot(r.partial[0:3].reshape(SLOTS, SEQ), r.hidden_two[:, n]).astype(LOW)
+    gate_dot = jnp.zeros((SLOTS, 1), WIDE)
+    for n in range(2):
+        part = slice(256 * n, 256 * (n + 1))
+        gate_pre = dot(r.rows[here, :], r.gate[e, :, :, :, part].reshape(D, 256))
+        up_pre = dot(r.rows[here, :], r.up[e, :, :, :, part].reshape(D, 256))
+        later = slice(512 + 256 * n, 768 + 256 * n)
+        product_grad = r.low_grad[here, later].astype(WIDE)
+        sigmoid = 1.0 / (1.0 + jnp.exp(-gate_pre))
+        silu = gate_pre * sigmoid
+        product = silu * up_pre
+        gate_dot = gate_dot + jnp.sum(product * product_grad, axis=-1, keepdims=True)
+        product_grad = share * product_grad
+        r.product[:, part] = (share * product).astype(LOW)
+        r.low_grad[here, part] = (product_grad * up_pre * (sigmoid + silu * (1.0 - sigmoid))).astype(LOW)
+        r.low_grad[here, later] = (product_grad * silu).astype(LOW)
     for n in quarters:
         r.made[:, n] = dot(r.product[...], r.down[e, :, :, :, n].reshape(512, 256)).astype(LOW)
-
-    def weigh(t, _):
-        upstream = r.slot_grad[slot_strip(t), :].astype(WIDE)
-        made, share = r.made[strip(t), :].astype(WIDE), r.share[strip(t), :]
-        r.gate_dot[strip(t), :] = jnp.sum(upstream * made, axis=-1, keepdims=True)
-        r.made[strip(t), :] = (share * made).astype(LOW)
-        r.route_grad[strip(t), :] = (share * upstream).astype(LOW)
-        return 0
-
-    lax.fori_loop(0, 12, weigh, 0)
     keep = pltpu.make_async_copy(r.made, r.made_far.at[here], r.load.at[3])
     keep.start()
-    r.wide_b[:, 0:512] = tail_dot(r.route_grad[...], r.down[e].reshape(512, D))
     for n in quarters:
-        down_grad = lead_dot(r.product[...], r.route_grad[:, n])
+        down_grad = lead_dot(r.product[...], r.slot_grad[here, n])
         r.down[e, :, :, :, n] = down_grad.astype(LOW).reshape(4, 4, 32, 256)
-
-    def activate_back(t, _):
-        gate_pre, product_grad = r.wide_a[strip(t), 0:512], r.wide_b[strip(t), 0:512]
-        sigmoid = 1.0 / (1.0 + jnp.exp(-gate_pre))
-        slope = sigmoid * (1.0 + gate_pre * (1.0 - sigmoid))
-        r.gate_low[strip(t), :] = (product_grad * r.wide_a[strip(t), 512:1024] * slope).astype(LOW)
-        r.up_low[strip(t), :] = (product_grad * (gate_pre * sigmoid)).astype(LOW)
-        return 0
-
-    lax.fori_loop(0, 12, activate_back, 0)
-    for m, n in enumerate(quarters):
-        slot_grad = tail_dot(r.gate_low[...], r.gate[e, m].reshape(256, 512)) + tail_dot(
-            r.up_low[...], r.up[e, m].reshape(256, 512)
-        )
-        r.slot_grad[here, n] = slot_grad.astype(LOW)
-        r.gate[e, m] = lead_dot(r.rows[:, n], r.gate_low[...]).astype(LOW).reshape(4, 64, 512)
-        r.up[e, m] = lead_dot(r.rows[:, n], r.up_low[...]).astype(LOW).reshape(4, 64, 512)
-
-    def gate_rows(t, total):
-        grads = r.gate_dot[pl.ds(pl.multiple_of(t * TOK, TOK), TOK), :]
-        return total + jnp.sum(jnp.where(hits(r, at, e, t), grads, 0.0), axis=0, keepdims=True)
-
-    gate_row = lax.fori_loop(0, 3, gate_rows, jnp.zeros((1, SEQ), WIDE))
+    high, middle, lowest = three_parts(gate_dot)
+    parts = jnp.where(lane == 0, high, jnp.where(lane == 1, middle, jnp.where(lane == 2, lowest, 0.0)))
+    gate_rows = lead_dot(parts.astype(LOW), r.partial[0:3].reshape(SLOTS, SEQ))
+    gate_row = gate_rows[0:1] + gate_rows[1:2] + gate_rows[2:3]
     for b in range(8):
         r.gate_grad[b, pl.ds(e, 1), :] = gate_row[:, TOK * b : TOK * (b + 1)]
     keep.wait()
+
+
+def slot_grads(r, m):
+    def one(e, _):
+        here = pl.ds(pl.multiple_of(e * SLOTS, SLOTS), SLOTS)
+        gate, up = r.gate[e, m].reshape(256, 512), r.up[e, m].reshape(256, 512)
+        slot_grad = tail_dot(r.low_grad[here, 0:512], gate) + tail_dot(r.low_grad[here, 512:1024], up)
+        r.slot_grad[here, 256 * m : 256 * (m + 1)] = slot_grad.astype(LOW)
+        return 0
+
+    lax.fori_loop(0, 4, one, 0)
+
+
+def gate_up_grads(r, e):
+    here = pl.ds(pl.multiple_of(e * SLOTS, SLOTS), SLOTS)
+    for m in range(4):
+        grads = lead_dot(r.rows[here, 256 * m : 256 * (m + 1)], r.low_grad[here, :]).astype(LOW)
+        r.gate[e, m], r.up[e, m] = grads[:, 0:512].reshape(4, 64, 512), grads[:, 512:1024].reshape(4, 64, 512)
 
 
 def expert_sums(r, at, e):
@@ -659,17 +653,21 @@
     r.gate_grad[...] = jnp.zeros((8, 8, 128), WIDE)
     share_tokens(r, at)
 
-    def sums(e, name):
-        for unit in expert_sums(r, at, e):
-            getattr(unit, name)()
+    def wide(name, *experts):
+        for e in experts:
+            getattr(expert_sums(r, at, e)[0], name)()
+
+    def half(name, *experts):
+        for e in experts:
+            getattr(expert_sums(r, at, e)[1], name)()
 
     def one(e, _):
         expert(r, at, e)
-        sums(e, "step1")
+        half("step1", e)
 
         @pl.when(e > 0)
         def _():
-            sums(e - 1, "step2")
+            half("step2", e - 1)
 
         return 0
 
@@ -681,17 +679,36 @@
     def two_blocks(ref, a, b):
         return jnp.concatenate([rows(ref, a)[...], rows(ref, b)[...]], axis=0)
 
-    hidden_sum = SumExpert(at, r, r.pair1, r.line1, r.mine1, r.s_sems.at[0])
-    hidden_sum.start(lambda a, b, n: dot(two_blocks(r.places, a, b), r.slot_grad[:, n]))
+    def partial(k):
+        return r.partial.at[k]
+
+    def slot_sums(a, b, n):
+        return dot(two_blocks(r.places, a, b), r.slot_grad[:, n])
+
+    hidden_sum = SumExpert(at, partial, r.partial, r.pair1, r.line1, r.mine1, r.s_sems.at[0])
+    for n in range(4):
+        slot_grads(r, n)
+        hidden_sum.across(slot_sums, n)
+        if n > 0:
+            hidden_sum.along(slot_sums, n - 1)
+        if n == 1:
+            half("step2", 3)
+            half("step3", 0)
+    hidden_sum.along(slot_sums, 3)
     made_load = pltpu.make_async_copy(r.made_far, r.slot_grad, r.load.at[3])
     made_load.start()
     own = pl.ds(pl.multiple_of(at.j * TOK, TOK), TOK)
     r.hidden_own[...] = r.hidden_two[own, :]
     out_load = pltpu.make_async_copy(r.out_far, r.hidden_two, r.load.at[0])
     out_load.start()
-    hidden_load = pltpu.make_async_copy(r.hidden_far, r.upstream, r.load.at[1])
-    hidden_load.start()
-    sums(3, "step2")
+
+    def two(e, _):
+        gate_up_grads(r, e)
+        wide("step1", e)
+        return 0
+
+    lax.fori_loop(0, 4, two, 0)
+    half("step3", 1, 2, 3)
     attended.forward()
     gate_copies.wait_recv()
     gate_grad = jnp.concatenate(
@@ -701,17 +718,37 @@
     shares = r.shares[...]
     logit_grad = shares * (gate_grad - jnp.sum(shares * gate_grad, axis=-1, keepdims=True))
     logit_grad = logit_grad.astype(LOW)
-    router_grad = lead_dot(r.hidden_own[...], logit_grad)
-    hidden_grad = tail_dot(logit_grad, r.router[...])
-    hidden_grad = hidden_grad + hidden_sum.total()
-    residual, upstream = r.residual[...], r.cotangent[...].astype(WIDE)
-    inverse = lax.rsqrt(jnp.mean(residual * residual, axis=-1, keepdims=True) + EPSILON)
-    gain_two_grad = jnp.sum(hidden_grad * (residual * inverse), axis=0, keepdims=True)
-    scaled = hidden_grad * r.gains[1:2, :]
-    mean = jnp.mean(scaled * residual, axis=-1, keepdims=True)
-    residual_grad = upstream + scaled * inverse - residual * (inverse * inverse * inverse * mean)
-    r.residual_grad[...] = residual_grad
-    r.branch[...] = residual_grad.astype(LOW)
+    for m in range(4):
+        router_grad = lead_dot(r.hidden_own[:, 256 * m : 256 * (m + 1)], logit_grad).astype(LOW)
+        for x in range(4):
+            r.dense[m, x, 192:256] = router_grad[64 * x : 64 * (x + 1)]
+    for n in range(4):
+        part = slice(256 * n, 256 * (n + 1))
+        r.mine1[:, part] += tail_dot(logit_grad, r.router[part, :])
+    made_load.wait()
+    output_sum = SumExpert(
+        at, lambda k: rows(r.upstream, k), r.upstream.at[0 : 7 * TOK], r.pair2, r.line2, r.mine2, r.s_sems.at[1]
+    )
+    for n in range(4):
+        output_sum.across(slot_sums, n)
+    hidden_sum.arrived()
+
+    def norm_back(values, hidden_grad, gain):
+        inverse = lax.rsqrt(jnp.mean(values * values, axis=-1, keepdims=True) + EPSILON)
+        scaled = hidden_grad * gain
+        mean = jnp.mean(scaled * values, axis=-1, keepdims=True)
+        return inverse, scaled * inverse - values * (inverse * inverse * inverse * mean)
+
+    def strip_back(t, gain_grad):
+        here = pl.ds(pl.multiple_of(t * 32, 32), 32)
+        residual, hidden_grad = r.residual[here, :], hidden_sum.total(here)
+        inverse, residual_grad = norm_back(residual, hidden_grad, r.gains[1:2, :])
+        residual_grad = residual_grad + r.cotangent[here, :].astype(WIDE)
+        r.residual_grad[here, :] = residual_grad
+        r.branch[here, :] = residual_grad.astype(LOW)
+        return gain_grad + jnp.sum(hidden_grad * (residual * inverse), axis=0, keepdims=True)
+
+    r.gains[2:3, :] = lax.fori_loop(0, 4, strip_back, jnp.zeros((1, D), WIDE))
     branch_copies = Shares(
         at, lambda b: columns(r.branch, b), rows(r.branch_part, at.j), r.branch_part.at[0 : 7 * TOK], r.b_sems
     )
@@ -727,11 +764,21 @@
     rows(r.attended_back, at.j)[...] = columns(r.attended_grad, at.j)[...]
     hidden_sum.sent_all()
 
-    output_sum = SumExpert(at, r, r.pair2, r.line2, r.mine2, r.s_sems.at[1])
-    made_load.wait()
-    output_sum.start(lambda a, b, n: dot(two_blocks(r.places, a, b), r.slot_grad[:, n]))
-    sums(0, "step3")
-    sums(1, "step3")
+    wide("step2", 0)
+    half("step4", 0, 1)
+    for n in range(4):
+        output_sum.along(slot_sums, n)
+    for b in range(8):
+        here = slice(TOK * b, TOK * (b + 1))
+        gain_grad = jnp.concatenate(
+            [jnp.zeros((33, TOK), WIDE), r.gains[2:3, here], jnp.zeros((94, TOK), WIDE)], axis=0
+        )
+        gain_grad = jnp.transpose(gain_grad)
+        for t in range(2):
+            m, x = b // 2, 2 * (b % 2) + t
+            others = r.dense[m, x, 192:256].astype(WIDE) + gain_grad[64 * t : 64 * (t + 1)]
+            r.dense[m, x, 192:256] = others.astype(LOW)
+    half("step4", 2, 3)
     grad_copies.wait_recv()
 
     low_lanes = lanes((256, 128)) < 64
@@ -762,10 +809,8 @@
         query_grad = jnp.where(low_lanes, heads[0], heads[1]) * SCALE
         cosine, sine = angles(r, here, (256, 128))
         r.qkv_grad[here, 0:128] = turn(query_grad, cosine, -sine).astype(LOW)
-        if b == 2:
-            sums(2, "step3")
-            sums(0, "step4")
-    sums(1, "step4")
+        if b > 0:
+            wide("step2", b)
     low_lanes = lanes((TOK, 128)) < 64
 
     def finish_keys(b, _):
@@ -781,97 +826,101 @@
     lax.fori_loop(0, 8, finish_keys, 0)
 
     output_sum.sent_all()
-    r.gain_sum[...] = jnp.zeros((8, D), WIDE)
-
+    hidden_load = pltpu.make_async_copy(r.hidden_far, r.upstream, r.load.at[1])
+    hidden_load.start()
+
+    branch_copies.wait_recv()
+    attended.finish()
     hidden_load.wait()
-
-    def hidden_one_tile(a, b, n):
-        made = tail_dot(two_blocks(r.qkv_grad, a, b), r.w_qkv[n, :])
-        hidden = jnp.concatenate([rows(r.upstream, k).at[:, n][...] for k in (a, b)], axis=0)
-        r.gain_sum[0:1, n] += jnp.sum(made * hidden.astype(WIDE), axis=0, keepdims=True)
-        return made
-
-    input_sum = SumExpert(at, r, r.pair3, r.line3, r.mine1, r.s_sems.at[2])
-    input_sum.start(hidden_one_tile)
-
-    branch_copies.wait_recv()
-    branch_copies.wait_send()
-    attended.finish()
-    gain_rows = jnp.concatenate(
-        [
-            jnp.zeros((32, D), WIDE), r.gain_sum[0:1, :] / r.gains[0:1, :], gain_two_grad, jnp.zeros((94, D), WIDE),
-        ],
-        axis=0,
-    )
     for m in range(4):
         here = slice(256 * m, 256 * (m + 1))
-        grads = lead_dot(r.upstream[:, here], r.qkv_grad[...]).astype(LOW)
+        grads = lead_dot(r.upstream[:, here], r.qkv_grad[...])
+        gains = jnp.sum(grads * r.w_qkv[here, :].astype(WIDE), axis=-1, keepdims=True)
+        gains = gains / r.router[here, 32:33].astype(WIDE)
+        grads = grads.astype(LOW)
         out_grads = lead_dot(r.attended_all[:, here], r.branch_part[...]).astype(LOW)
-        others = [jnp.transpose(gain_rows[:, 256 * m + 128 * t : 256 * m + 128 * (t + 1)]) for t in range(2)]
-        others = (router_grad[here] + jnp.concatenate(others, axis=0)).astype(LOW)
         for x in range(4):
             part = slice(64 * x, 64 * (x + 1))
             r.dense[m, x, 0:64] = grads[part, 0:128]
             r.dense[m, x, 64:128] = grads[part, 128:256]
             r.dense[m, x, 128:192] = out_grads[part]
-            r.dense[m, x, 192:256] = others[part]
+            others = r.dense[m, x, 192:256].astype(WIDE)
+            r.dense[m, x, 192:256] = jnp.where(lanes((64, 128)) == 32, gains[part], others).astype(LOW)
     dense_sum = SumXY(
         at, [r.dense.at[:, :, pl.ds(128 * n, 128)] for n in range(2)], (r.dense1, r.dense2, r.dense3, r.dense4),
         r.f_sems, 128,
     )
     dense_sum.step1()
-    sums(3, "step3")
-    sums(2, "step4")
+
+    def hidden_one_tile(a, b, n):
+        return tail_dot(two_blocks(r.qkv_grad, a, b), r.w_qkv[n, :])
+
+    input_sum = SumExpert(at, partial, r.partial, r.pair3, r.line3, r.mine1, r.s_sems.at[2])
+    for n in range(4):
+        input_sum.across(hidden_one_tile, n)
+    wide("step3", 0, 1)
     dense_sum.step2()
+    for n in range(4):
+        input_sum.along(hidden_one_tile, n)
+    branch_copies.wait_send()
+    wide("step3", 2)
+    wide("step4", 0)
+    dense_sum.step3()
+    wide("step3", 3)
+    wide("step4", 1)
+    dense_sum.step4()
+    wide("step4", 2, 3)
+
+    def own_shard(ref, e):
+        return ref.at[e, at.y, at.x]
 
     def stores(e):
-        high = pl.ds(pl.multiple_of(e * 64, 64), 64)
-        low = pl.ds(pl.multiple_of(e * 32, 32), 32)
+        arrays = ((r.gate, r.gate_out), (r.up, r.up_out), (r.down, r.down_out))
         return [
-            pltpu.make_async_copy(r.wide_a.at[high, 0:512], r.gate_out.at[e], r.store.at[e, 0]),
-            pltpu.make_async_copy(r.wide_a.at[high, 512:1024], r.up_out.at[e], r.store.at[e, 1]),
-            pltpu.make_async_copy(r.wide_b.at[low], r.down_out.at[e], r.store.at[e, 2]),
+            pltpu.make_async_copy(own_shard(ref, e), out.at[e], r.store.at[e, n])
+            for n, (ref, out) in enumerate(arrays)
         ]
 
     def finish_expert(e, _):
         wide_sum, half_sum = expert_sums(r, at, e)
         gate, up = wide_sum.step5()
         left, right = half_sum.step5()
-        high = pl.ds(pl.multiple_of(e * 64, 64), 64)
-        r.wide_a[high, 0:512] = gate
-        r.wide_a[high, 512:1024] = up
-        low = pl.ds(pl.multiple_of(e * 32, 32), 32)
-        r.wide_b[low, 0:512] = left
-        r.wide_b[low, 512:1024] = right
+        own_shard(r.gate, e)[...], own_shard(r.up, e)[...] = gate.astype(LOW), up.astype(LOW)
+        down = own_shard(r.down, e)
+        down[:, 0:512], down[:, 512:1024] = left.astype(LOW), right.astype(LOW)
         for copy in stores(e):
             copy.start()
         return 0
 
-    lax.fori_loop(0, 3, finish_expert, 0)
-    sums(3, "step4")
-    dense_sum.step3()
-    r.branch[...] = (r.residual[...] + output_sum.total()).astype(LOW)
+    output_sum.arrived()
+
+    def strip_out(t, _):
+        here = pl.ds(pl.multiple_of(t * 32, 32), 32)
+        r.branch[here, :] = (r.residual[here, :] + output_sum.total(here)).astype(LOW)
+        return 0
+
+    lax.fori_loop(0, 4, strip_out, 0)
     output_store = pltpu.make_async_copy(r.branch, r.output, r.load.at[0])
     output_store.start()
-    finish_expert(3, 0)
-    dense_sum.step4()
-
-    hidden_grad = input_sum.total()
-    inputs = r.tokens[...].astype(WIDE)
-    inverse = lax.rsqrt(jnp.mean(inputs * inputs, axis=-1, keepdims=True) + EPSILON)
-    scaled = hidden_grad * r.gains[0:1, :]
-    mean = jnp.mean(scaled * inputs, axis=-1, keepdims=True)
-    r.residual_grad[...] = (
-        r.residual_grad[...] + scaled * inverse - inputs * (inverse * inverse * inverse * mean)
-    )
-    input_store = pltpu.make_async_copy(r.residual_grad, r.input_grad, r.load.at[1])
-    input_store.start()
     for n, total in enumerate(dense_sum.step5()):
         r.dense_total[n] = total.reshape(2, 8, 8, 128)
     last_copies = Shares(
         at, lambda b: r.dense_total.at[:, :, b], r.dense_back.at[at.j], r.dense_back.at[0:7], r.l_sems
     )
     r.dense_back[pl.ds(at.j, 1)] = r.dense_total[:, :, pl.ds(at.j, 1)].reshape(1, 2, 2, 8, 128)
+    lax.fori_loop(0, 4, finish_expert, 0)
+
+    input_sum.arrived()
+
+    def strip_in(t, _):
+        here = pl.ds(pl.multiple_of(t * 32, 32), 32)
+        _, input_grad = norm_back(r.tokens[here, :].astype(WIDE), input_sum.total(here), r.gains[0:1, :])
+        r.residual_grad[here, :] += input_grad
+        return 0
+
+    lax.fori_loop(0, 4, strip_in, 0)
+    input_store = pltpu.make_async_copy(r.residual_grad, r.input_grad, r.load.at[1])
+    input_store.start()
     last_copies.wait_recv()
     low_lanes = lanes((8, 128)) < 64
     others = jnp.zeros((8, 128), WIDE)
@@ -920,8 +969,8 @@
 
 OUTS = dict(
     output=far(TOK, D, kind=LOW), input_grad=far(TOK, D), query_out=wide(8, D), key_out=wide(8, 512),
-    value_out=wide(8, 512), out_out=wide(8, D), others_out=wide(8, 128), gate_out=far(4, 64, 512),
-    up_out=far(4, 64, 512), down_out=far(4, 32, D), made_far=far(4 * SLOTS, D, kind=LOW),
+    value_out=wide(8, 512), out_out=wide(8, D), others_out=wide(8, 128), gate_out=far(4, 64, 512, kind=LOW),
+    up_out=far(4, 64, 512, kind=LOW), down_out=far(4, 32, D, kind=LOW), made_far=far(4 * SLOTS, D, kind=LOW),
     hidden_far=far(SEQ, D, kind=LOW), out_far=far(D, D, kind=LOW),
 )
 SCRATCH = dict(
@@ -931,11 +980,10 @@
     pack=wide(8, 24, 128), near=wide(8, 24, 128), stage=low(192, 128),
     out_mine=wide(8, D), out_other=wide(8, D), out_rows=low(64, 512),
     gate=low(4, 4, 4, 64, 512), up=low(4, 4, 4, 64, 512), down=low(4, 4, 4, 32, D),
-    shares=wide(TOK, 128), shares_row=wide(32, SEQ), order_row=wide(32, SEQ), places=low(SEQ, 4 * SLOTS),
-    rows=low(SLOTS, D), route_grad=low(SLOTS, D), made=low(SLOTS, D), slot_grad=low(4 * SLOTS, D),
-    gate_grad=wide(8, 8, 128), gate_back=wide(8, 8, 128), wide_a=wide(SLOTS, D), wide_b=wide(SLOTS, D),
-    product=low(SLOTS, 512), gate_low=low(SLOTS, 512), up_low=low(SLOTS, 512), share=wide(SLOTS, 1),
-    gate_dot=wide(SLOTS, 1), hidden_own=low(TOK, D),
+    shares=wide(TOK, 128), order_row=wide(32, SEQ), places=low(SEQ, 4 * SLOTS),
+    rows=low(4 * SLOTS, D), low_grad=low(4 * SLOTS, D), made=low(SLOTS, D), slot_grad=low(4 * SLOTS, D),
+    gate_grad=wide(8, 8, 128), gate_back=wide(8, 8, 128),
+    product=low(SLOTS, 512),
     wide1=low(4, 2, 2, 2, 64, 512), wide2=low(4, 2, 2, 4, 64, 512), wide3=low(4, 2, 2, 32, 512),
     wide4=low(4, 2, 2, 64, 512), half1=low(4, 2, 2, 2, 32, 512), half2=low(4, 2, 2, 4, 32, 512),
     half3=low(4, 2, 2, 16, 512), half4=low(4, 2, 2, 32, 512), dense=low(4, 4, 256, 128),
@@ -945,7 +993,7 @@
     pair2=low(4, TOK, D), line2=low(3, TOK, D), mine2=wide(TOK, D), pair3=low(4, TOK, D), line3=low(3, TOK, D),
     residual_grad=wide(TOK, D), branch=low(TOK, D), branch_part=low(SEQ, 128), attended_grad=low(TOK, D),
     attended_back=low(SEQ, 128), attended_all=low(SEQ, D), key_grad=wide(SEQ, 128), value_grad=wide(SEQ, 128),
-    qkv_grad=low(SEQ, 256), gain_sum=wide(8, D),
+    qkv_grad=low(SEQ, 256), extra=wide(8, 128),
     x_sems=DMA((5,)), n_sems=DMA((5,)), g_sems=DMA((5,)), h_sems=DMA((5,)), t_sems=DMA((5,)), p_sems=DMA((2,)),
     c_sems=DMA((2,)), b_sems=DMA((2,)), d_sems=DMA((2,)), l_sems=DMA((2,)), w_sems=DMA((2, 4)),
     o_sems=DMA((2, 4)), a_sems=DMA((2,)), q_sems=DMA((6,)), e_sems=DMA((4, 2, 4, 2)), f_sems=DMA((4, 2)),
@@ -968,7 +1016,8 @@
         r = SimpleNamespace(**dict(zip(names, refs)))
         r.hidden_one, r.w_out_all = r.slot_grad.at[0:SEQ], r.places.at[:, 0:D]
         r.attended_head = r.qkv_grad.at[:, 128:256]
-        r.extra_all = r.key_grad
+        r.extra_all, r.corner = r.key_grad, r.value_grad.at[0:128]
+        r.share_parts, r.hidden_own = r.qkv_grad.at[:, 0:128], r.attended_grad
         back(r, front(r))
 
     outs = pl.pallas_call(
@@ -986,53 +1035,65 @@
 
 
 def hand_on(*refs):
-    come, go = refs[-2:]
-    loads = [pltpu.make_async_copy(refs[n], refs[18 + n], come.at[n]) for n in range(9)]
-    stores = [pltpu.make_async_copy(refs[18 + n], refs[9 + n], go.at[n]) for n in range(9)]
+    others, sources, router, gains = refs[0], refs[1:10], refs[10], refs[11:13]
+    targets, between, (come, go) = refs[13:22], refs[22:31], refs[31:33]
+    narrow = refs[33:36]
+    loads = [
+        pltpu.make_async_copy(sources[n], narrow[n - 6] if n > 5 else between[n], come.at[n]) for n in range(9)
+    ]
+    stores = [pltpu.make_async_copy(between[n], targets[n], go.at[n]) for n in range(9)]
     for copy in loads:
         copy.start()
-    for load, store in zip(loads, stores):
+    router[...] = others[:, 0:32]
+    turned = jnp.transpose(jnp.concatenate([others[...], jnp.zeros((120, 128), WIDE)], axis=0))
+    for n in range(2):
+        gains[n][...] = turned[32 + n : 33 + n, 0:8]
+    for n, (load, store) in enumerate(zip(loads, stores)):
         load.wait()
+        if n > 5:
+            between[n][...] = narrow[n - 6][...].astype(WIDE)
         store.start()
     for copy in stores:
         copy.wait()
 
 
-def handed_on(*arrays):
+def handed_on(others, *arrays):
+    near, away = pl.BlockSpec(memory_space=pltpu.VMEM), pl.BlockSpec(memory_space=pl.ANY)
+    small = [jax.ShapeDtypeStruct(shape, WIDE) for shape in ((8, 32), (1, 8), (1, 8))]
+    kinds = [LOW] + [WIDE] * 8
     return pl.pallas_call(
         hand_on,
-        out_shape=[jax.ShapeDtypeStruct(a.shape, a.dtype) for a in arrays],
-        in_specs=[pl.BlockSpec(memory_space=pl.ANY)] * 9,
-        out_specs=[pl.BlockSpec(memory_space=pl.ANY)] * 9,
-        scratch_shapes=[pltpu.VMEM(a.shape, a.dtype) for a in arrays] + [DMA((9,)), DMA((9,))],
+        out_shape=small + [jax.ShapeDtypeStruct(a.shape, kind) for a, kind in zip(arrays, kinds)],
+        in_specs=[near] + [away] * 9,
+        out_specs=[near] * 3 + [away] * 9,
+        scratch_shapes=[pltpu.VMEM(a.shape, kind) for a, kind in zip(arrays, kinds)]
+        + [DMA((9,)), DMA((9,))]
+        + [pltpu.VMEM(a.shape, LOW) for a in arrays[6:]],
         name="hand_on",
-    )(*arrays)
+    )(others, *arrays)
 
 
 def shards(
     tokens, segments, routes, gain_attn, gain_ffn, w_query, w_key, w_value, w_out, w_router, w_gate, w_up,
     w_down, cotangent,
 ):
-    extra = jnp.concatenate(
-        [w_router, gain_attn[:, None], gain_ffn[:, None], jnp.zeros((8, 94), LOW)], axis=1
-    ).astype(WIDE)
     angle = np.arange(SEQ, dtype=np.float32)[:, None] * (
         np.float32(10000.0) ** (-np.arange(32, dtype=np.float32) / np.float32(32))
     )
     waves = np.concatenate([np.cos(angle), np.cos(angle), -np.sin(angle), np.sin(angle)], axis=1)
     made = layer(
         tokens=tokens, routes=routes.T, w_query=w_query, w_key=w_key, w_value=w_value, w_out=w_out,
-        extra=extra, seg_row=segments, table=jnp.asarray(waves.astype(np.float32)), cotangent=cotangent,
+        w_router=w_router, gain_attn=gain_attn.reshape(1, 8), gain_ffn=gain_ffn.reshape(1, 8),
+        seg_row=segments, table=jnp.asarray(waves.astype(np.float32)), cotangent=cotangent,
         gate_in=w_gate.reshape(4, 4, 4, 64, 512), up_in=w_up.reshape(4, 4, 4, 64, 512),
         down_in=w_down.reshape(4, 4, 4, 32, D),
     )
-    others = made["others_out"]
-    output, input_grad, query, key, value, out, gate, up, down = handed_on(
-        made["output"], made["input_grad"], made["query_out"], made["key_out"], made["value_out"],
-        made["out_out"], made["gate_out"], made["up_out"], made["down_out"],
+    router, gain_one, gain_two, output, input_grad, query, key, value, out, gate, up, down = handed_on(
+        made["others_out"], made["output"], made["input_grad"], made["query_out"], made["key_out"],
+        made["value_out"], made["out_out"], made["gate_out"], made["up_out"], made["down_out"],
     )
     return (
-        output, input_grad, others[:, 32], others[:, 33], query, key, value, out, others[:, 0:32], gate, up, down,
+        output, input_grad, gain_one.reshape(8), gain_two.reshape(8), query, key, value, out, router, gate, up, down,
     )
 
 

time: 181 us -> 162 us (0.90)
  Pallas kernels: 175 us -> 161 us
  local copies, waits for them, and re-layouts: 4.31 us -> 0 us
    pallas_call x1, Pallas kernels: 172 us -> 157 us  [layer(): pl.pallas_call(kernel, out_shape=[jax.ShapeDtypeStruct(OUTS[n].shape, OUT...]
where the time goes in v3:
time: 162 us
  Pallas kernels  161 us (99%)
    pallas_call x1, Pallas kernels, layer(): pl.pallas_call(kernel, out_shape=[jax.ShapeDtypeStruct(OUTS[n].shape, OUT...  157 us
    pallas_call x1, Pallas kernels, handed_on(): pl.pallas_call(hand_on, out_shape=small + [jax.ShapeDtypeStruct(a.shape,...  3.91 us

profile of v3, /device:TPU:1, one launch (start us, length us, event | category | flops | bytes accessed | tf_op | source)
XLA Modules:
  0.0 161.5 jit_solution(15433081765046127541)
XLA Ops:
  0.6 156.8 %layer.1 = (bf16[128,1024]{1,0:T(8,128)(2,1)}, f32[128,1024]{1,0:T(8,128)}, f32[8,1024]{1,0:T(8,128)}, f32[8,512]{1,0:T(8,128)}, f32[8,512]{1,0:T(8,128)}, /*ind...) custom-call(bf16[128,1024]{1,0:T(8,128)(2,1)} %refs_0_.1, ...), custom_call_target="tpu_custom_call" | custom-call | tf_op jit(solution)/shard_map/layer/pallas_call | solution.py:1023
  157.4 3.9 %hand_on.1 = (f32[8,32]{1,0:T(8,128)}, f32[1,8]{1,0:T(1,128)}, f32[1,8]{1,0:T(1,128)}, bf16[128,1024]{1,0:T(8,128)(2,1)}, f32[128,1024]{1,0:T(8,128)}, /*index=5...) custom-call(f32[8,128]{1,0:T(8,128)} %get-tuple-element.34.refs_0_, ...), custom_call_target="tpu_custom_call" | custom-call | tf_op jit(solution)/shard_map/hand_on/pallas_call | solution.py:1064

commit v4 on v3

--- a/solution.py
+++ b/solution.py
@@ -14,7 +14,8 @@
 EPSILON = 1e-06
 SCALE = 64 ** (-0.5)
 TOK, SEQ, D, SLOTS = 128, 1024, 1024, 384
-Z_STEPS = (2, 1, 3)
+Z_STEPS = (1, 3, 2)
+EARLY = 1
 
 
 def dot(one, two):
@@ -86,15 +87,24 @@
             send(self.source, mine, self.sems.at[0], self.sems.at[1 + k], z_peer(at, step))
         send(self.source, mine, self.sems.at[0], self.sems.at[4], at.sibling)
 
-    def forward(self):
+    def block(self, k):
+        return plus(self.at.z, 4 - Z_STEPS[k], 4)
+
+    def forward(self, *which):
         at = self.at
-        for k, step in enumerate(Z_STEPS):
-            block = rows(self.target, plus(at.z, 4 - step, 4) * 2 + at.c)
+        for k in which or range(3):
+            block = rows(self.target, self.block(k) * 2 + at.c)
             got(block, self.sems.at[1 + k], at)
-            send(block, block, self.sems.at[0], self.sems.at[4], at.sibling)
-
-    def finish(self):
-        got(self.target.at[0 : 4 * TOK], self.sems.at[4], self.at)
+            send(block, block, self.sems.at[0], self.sems.at[5 + k], at.sibling)
+
+    def chip(self, k):
+        got(self.target.at[0:TOK], self.sems.at[5 + k], self.at)
+        return self.at.z if k < 0 else self.block(k)
+
+    def finish(self, arrived=False):
+        for k in range(-1, 3):
+            if not arrived:
+                self.chip(k)
         gone(self.target.at[0 : 7 * TOK], self.sems.at[0], self.at)
 
 
@@ -207,7 +217,7 @@
     for k in range(8):
         named = named + jnp.where(r.routes[k : k + 1, :] == expert, 1.0, 0.0)
     rows(r.named, at.j)[...] = jnp.transpose(named).astype(LOW)
-    rows(r.hidden_one, at.j)[...] = r.tokens[...]
+    rows(r.x_all, at.j)[...] = r.tokens[...]
     for b in range(8):
         here = slice(TOK * b, TOK * (b + 1))
         across = jnp.broadcast_to(r.seg_row[:, here].astype(WIDE), (TOK, TOK))
@@ -216,7 +226,7 @@
     ready()
     pair = send(r.out_mine, r.out_other, r.q_sems.at[0], r.q_sems.at[1], at.sibling)
     first = Shares(at, lambda b: r.pack.at[b], r.near.at[at.j], r.near.at[0:7], r.p_sems)
-    tokens = Gather(at, r.tokens, r.hidden_one, r.x_sems)
+    tokens = Gather(at, r.tokens, r.x_all, r.x_sems)
     tokens.start()
     pair.wait_recv()
     mine, other = r.out_mine[...], r.out_other[...]
@@ -238,12 +248,14 @@
     first.wait_recv()
     for b in range(8):
         r.stage[16 * b : 16 * (b + 1)] = r.near[b, 0:16].astype(LOW)
-    r.stage[128:192] = jnp.concatenate([r.near[b, 16:24] for b in range(8)], axis=0).astype(LOW)
+    extras = [jnp.concatenate([r.near[b, 16:24] for b in some], axis=0) for some in (range(4), range(4, 8))]
+    extras = jnp.where(lanes((32, 128)) < 64, extras[0], pltpu.roll(extras[1], 64, axis=1))
+    r.stage[128:160] = extras.astype(LOW)
     second = Spread(
-        at, r.stage, r.dense.at[at.y, at.x, 0:192], lambda y: r.dense.at[y, :, 0:192], r.dense.at[0, 0:3, 0:192],
+        at, r.stage, r.dense.at[at.y, at.x, 0:160], lambda y: r.dense.at[y, :, 0:160], r.dense.at[0, 0:3, 0:160],
         r.w_sems,
     )
-    r.dense[at.y, at.x, 0:192] = r.stage[...]
+    r.dense[at.y, at.x, 0:160] = r.stage[...]
     half = pl.ds(pl.multiple_of(at.c * 512, 512), 512)
     out_half = r.w_out_all.at[pl.ds(pl.multiple_of(at.i * 64, 64), 64), half]
     got(r.out_rows.at[0:48], r.q_sems.at[3], at)
@@ -252,31 +264,28 @@
         r.w_out_all.at[0:192, half], r.o_sems,
     )
     out_half[...] = r.out_rows[...]
-    tokens.forward()
-    rows(r.upstream, at.j)[...] = r.cotangent[...]
-    upstream = Gather(at, r.cotangent, r.upstream, r.g_sems)
-    upstream.start()
+    tokens.forward(0, 1)
     second.wait_recv()
 
     def unpack(i, _):
-        part = r.dense[lax.div(i, 4), lax.rem(i, 4), 0:192].astype(WIDE)
+        part = r.dense[lax.div(i, 4), lax.rem(i, 4), 0:160].astype(WIDE)
         here = pl.ds(pl.multiple_of(i * 64, 64), 64)
         heads = part[0:128].reshape(8, 16, 128)
         r.w_qkv[here, 0:128] = heads[:, 0:8, :].reshape(64, 128).astype(LOW)
         r.w_qkv[here, 128:256] = heads[:, 8:16, :].reshape(64, 128).astype(LOW)
-        r.extra_all[here, :] = part[128:192]
+        extras = part[128:160]
+        r.extra_all[here, :] = jnp.concatenate([extras, pltpu.roll(extras, 64, axis=1)], axis=0)
         return 0
 
     lax.fori_loop(0, 16, unpack, 0)
     r.gains[...] = extra_rows(r)
     r.router[...] = r.extra_all[...].astype(LOW)
-    tokens.finish()
 
     low_lanes = lanes((256, 128)) < 64
 
-    def project(b, _):
+    def project(b):
         here = pl.ds(pl.multiple_of(b * 256, 256), 256)
-        x = r.hidden_one[here, :].astype(WIDE)
+        x = r.x_all[here, :].astype(WIDE)
         inverse = lax.rsqrt(jnp.mean(x * x, axis=-1, keepdims=True) + EPSILON)
         hidden = (x * inverse * r.gains[0:1, :]).astype(LOW)
         r.hidden_one[here, :] = hidden
@@ -289,9 +298,15 @@
         turned = pltpu.roll(pair, 64, axis=1)
         r.keys[here, :] = jnp.where(low_lanes, pair, turned).astype(LOW)
         r.values[here, :] = jnp.where(low_lanes, turned, pair).astype(LOW)
-        return 0
-
-    lax.fori_loop(0, 4, project, 0)
+
+    for k in range(-1, 2):
+        project(tokens.chip(k))
+    tokens.forward(2)
+    rows(r.upstream, at.j)[...] = r.cotangent[...]
+    upstream = Gather(at, r.cotangent, r.upstream, r.g_sems)
+    upstream.start()
+    project(tokens.chip(2))
+    tokens.finish(arrived=True)
     marks.forward()
     hidden_save = pltpu.make_async_copy(r.hidden_one, r.hidden_far, r.load.at[3])
     hidden_save.start()
@@ -369,8 +384,12 @@
     for copy in loads:
         copy.wait()
     lax.fori_loop(0, 4, lambda e, _: pick_upstream(r, at, e), 0)
-    hidden.forward()
-    hidden.finish()
+    hidden.forward(0, 1)
+    for k in range(-1, 2):
+        share_tokens(r, at, hidden.chip(k))
+    hidden.forward(2)
+    share_tokens(r, at, hidden.chip(2))
+    hidden.finish(arrived=True)
     attended.start()
     return attended
 
@@ -530,24 +549,19 @@
     lax.fori_loop(0, 8, block, jnp.zeros((1, 128), WIDE))
 
 
-def share_tokens(r, at):
-    def block(b, _):
-        here = pl.ds(pl.multiple_of(b * 256, 256), 256)
-        named = r.named[here, :].astype(WIDE) > 0.0
-        logits = jnp.where(named, dot(r.hidden_two[here, :], r.router[...]), -1e30)
-        powers = jnp.where(named, jnp.exp(logits - jnp.max(logits, axis=-1, keepdims=True)), 0.0)
-        shares = powers / jnp.sum(powers, axis=-1, keepdims=True)
-        high, middle, lowest = three_parts(shares)
-        parts = high + pltpu.roll(middle, 32, axis=1) + pltpu.roll(lowest, 64, axis=1)
-        r.share_parts[here, :] = parts.astype(LOW)
-
-        @pl.when(b == at.z)
-        def _():
-            r.shares[...] = jnp.where(at.c == 0, shares[0:TOK], shares[TOK:])
-
-        return 0
-
-    lax.fori_loop(0, 4, block, 0)
+def share_tokens(r, at, b):
+    here = pl.ds(pl.multiple_of(b * 256, 256), 256)
+    named = r.named[here, :].astype(WIDE) > 0.0
+    logits = jnp.where(named, dot(r.hidden_two[here, :], r.router[...]), -1e30)
+    powers = jnp.where(named, jnp.exp(logits - jnp.max(logits, axis=-1, keepdims=True)), 0.0)
+    shares = powers / jnp.sum(powers, axis=-1, keepdims=True)
+    high, middle, lowest = three_parts(shares)
+    parts = high + pltpu.roll(middle, 32, axis=1) + pltpu.roll(lowest, 64, axis=1)
+    r.share_parts[here, :] = parts.astype(LOW)
+
+    @pl.when(b == at.z)
+    def _():
+        r.shares[...] = jnp.where(at.c == 0, shares[0:TOK], shares[TOK:])
 
 
 def three_parts(values):
@@ -605,9 +619,13 @@
         r.low_grad[here, part] = (product_grad * up_pre * (sigmoid + silu * (1.0 - sigmoid))).astype(LOW)
         r.low_grad[here, later] = (product_grad * silu).astype(LOW)
     for n in quarters:
-        r.made[:, n] = dot(r.product[...], r.down[e, :, :, :, n].reshape(512, 256)).astype(LOW)
-    keep = pltpu.make_async_copy(r.made, r.made_far.at[here], r.load.at[3])
-    keep.start()
+        made = dot(r.product[...], r.down[e, :, :, :, n].reshape(512, 256)).astype(LOW)
+        r.partial[3:6, :, n] = made.reshape(3, TOK, 256)
+    keep = [
+        pltpu.make_async_copy(r.partial.at[3 + k], rows(r.made_far, 3 * e + k), r.keep.at[k]) for k in range(3)
+    ]
+    for copy in keep:
+        copy.start()
     for n in quarters:
         down_grad = lead_dot(r.product[...], r.slot_grad[here, n])
         r.down[e, :, :, :, n] = down_grad.astype(LOW).reshape(4, 4, 32, 256)
@@ -617,18 +635,15 @@
     gate_row = gate_rows[0:1] + gate_rows[1:2] + gate_rows[2:3]
     for b in range(8):
         r.gate_grad[b, pl.ds(e, 1), :] = gate_row[:, TOK * b : TOK * (b + 1)]
-    keep.wait()
-
-
-def slot_grads(r, m):
-    def one(e, _):
-        here = pl.ds(pl.multiple_of(e * SLOTS, SLOTS), SLOTS)
-        gate, up = r.gate[e, m].reshape(256, 512), r.up[e, m].reshape(256, 512)
-        slot_grad = tail_dot(r.low_grad[here, 0:512], gate) + tail_dot(r.low_grad[here, 512:1024], up)
-        r.slot_grad[here, 256 * m : 256 * (m + 1)] = slot_grad.astype(LOW)
-        return 0
-
-    lax.fori_loop(0, 4, one, 0)
+    for copy in keep:
+        copy.wait()
+
+
+def slot_grads(r, e, m):
+    here = pl.ds(pl.multiple_of(e * SLOTS, SLOTS), SLOTS)
+    gate, up = r.gate[e, m].reshape(256, 512), r.up[e, m].reshape(256, 512)
+    slot_grad = tail_dot(r.low_grad[here, 0:512], gate) + tail_dot(r.low_grad[here, 512:1024], up)
+    r.slot_grad[here, 256 * m : 256 * (m + 1)] = slot_grad.astype(LOW)
 
 
 def gate_up_grads(r, e):
@@ -651,24 +666,48 @@
     r.wide_ways = (r.wide1, r.wide2, r.wide3, r.wide4)
     r.half_ways = (r.half1, r.half2, r.half3, r.half4)
     r.gate_grad[...] = jnp.zeros((8, 8, 128), WIDE)
-    share_tokens(r, at)
 
     def wide(name, *experts):
-        for e in experts:
+        if len(experts) == 1:
+            getattr(expert_sums(r, at, experts[0])[0], name)()
+            return
+
+        def one(e, _):
             getattr(expert_sums(r, at, e)[0], name)()
+            return 0
+
+        lax.fori_loop(experts[0], experts[-1] + 1, one, 0)
 
     def half(name, *experts):
-        for e in experts:
+        if len(experts) == 1:
+            getattr(expert_sums(r, at, experts[0])[1], name)()
+            return
+
+        def one(e, _):
             getattr(expert_sums(r, at, e)[1], name)()
+            return 0
+
+        lax.fori_loop(experts[0], experts[-1] + 1, one, 0)
 
     def one(e, _):
         expert(r, at, e)
         half("step1", e)
 
+        @pl.when(e < EARLY)
+        def _():
+            for m in range(4):
+                slot_grads(r, e, m)
+            gate_up_grads(r, e)
+            wide("step1", e)
+
         @pl.when(e > 0)
         def _():
             half("step2", e - 1)
 
+        @pl.when((e > 0) & (e <= EARLY))
+        def _():
+            wide("step2", e - 1)
+
         return 0
 
     lax.fori_loop(0, 4, one, 0)
@@ -687,7 +726,8 @@
 
     hidden_sum = SumExpert(at, partial, r.partial, r.pair1, r.line1, r.mine1, r.s_sems.at[0])
     for n in range(4):
-        slot_grads(r, n)
+        for e in range(EARLY, 4):
+            slot_grads(r, e, n)
         hidden_sum.across(slot_sums, n)
         if n > 0:
             hidden_sum.along(slot_sums, n - 1)
@@ -707,9 +747,12 @@
         wide("step1", e)
         return 0
 
-    lax.fori_loop(0, 4, two, 0)
+    lax.fori_loop(EARLY, 4, two, 0)
+    hidden_load = pltpu.make_async_copy(r.hidden_far, r.rows.at[0:SEQ], r.load.at[1])
+    hidden_load.start()
     half("step3", 1, 2, 3)
     attended.forward()
+    wide("step3", 0)
     gate_copies.wait_recv()
     gate_grad = jnp.concatenate(
         [r.gate_back[b][0:4] for b in range(8)] + [jnp.zeros((96, 128), WIDE)], axis=0
@@ -731,6 +774,7 @@
     )
     for n in range(4):
         output_sum.across(slot_sums, n)
+    wide("step2", 1)
     hidden_sum.arrived()
 
     def norm_back(values, hidden_grad, gain):
@@ -764,7 +808,8 @@
     rows(r.attended_back, at.j)[...] = columns(r.attended_grad, at.j)[...]
     hidden_sum.sent_all()
 
-    wide("step2", 0)
+    wide("step4", 0)
+    wide("step2", 2, 3)
     half("step4", 0, 1)
     for n in range(4):
         output_sum.along(slot_sums, n)
@@ -809,8 +854,8 @@
         query_grad = jnp.where(low_lanes, heads[0], heads[1]) * SCALE
         cosine, sine = angles(r, here, (256, 128))
         r.qkv_grad[here, 0:128] = turn(query_grad, cosine, -sine).astype(LOW)
-        if b > 0:
-            wide("step2", b)
+        if b == 3:
+            wide("step3", 1)
     low_lanes = lanes((TOK, 128)) < 64
 
     def finish_keys(b, _):
@@ -825,16 +870,13 @@
 
     lax.fori_loop(0, 8, finish_keys, 0)
 
-    output_sum.sent_all()
-    hidden_load = pltpu.make_async_copy(r.hidden_far, r.upstream, r.load.at[1])
-    hidden_load.start()
 
     branch_copies.wait_recv()
     attended.finish()
     hidden_load.wait()
     for m in range(4):
         here = slice(256 * m, 256 * (m + 1))
-        grads = lead_dot(r.upstream[:, here], r.qkv_grad[...])
+        grads = lead_dot(r.rows[0:SEQ, here], r.qkv_grad[...])
         gains = jnp.sum(grads * r.w_qkv[here, :].astype(WIDE), axis=-1, keepdims=True)
         gains = gains / r.router[here, 32:33].astype(WIDE)
         grads = grads.astype(LOW)
@@ -858,18 +900,14 @@
     input_sum = SumExpert(at, partial, r.partial, r.pair3, r.line3, r.mine1, r.s_sems.at[2])
     for n in range(4):
         input_sum.across(hidden_one_tile, n)
-    wide("step3", 0, 1)
-    dense_sum.step2()
     for n in range(4):
         input_sum.along(hidden_one_tile, n)
     branch_copies.wait_send()
-    wide("step3", 2)
-    wide("step4", 0)
+    wide("step3", 2, 3)
+    dense_sum.step2()
+    wide("step4", 1, 2, 3)
     dense_sum.step3()
-    wide("step3", 3)
-    wide("step4", 1)
     dense_sum.step4()
-    wide("step4", 2, 3)
 
     def own_shard(ref, e):
         return ref.at[e, at.y, at.x]
@@ -936,6 +974,7 @@
         r.value_out[:, head] = jnp.where(low_lanes, pltpu.roll(even, 64, axis=1), odd)
     r.others_out[...] = others
 
+    output_sum.sent_all()
     input_sum.sent_all()
     for copy in (gate_copies, grad_copies, last_copies):
         copy.wait_send()
@@ -977,11 +1016,11 @@
     w_qkv=low(D, 256), router=low(D, 128), gains=wide(8, D), queries=low(SEQ, 128), keys=low(SEQ, 128),
     values=low(SEQ, 128), log_total=wide(SEQ, 128), attended=low(TOK, D), residual=wide(TOK, D),
     hidden_two=low(SEQ, D), upstream=low(SEQ, D), named=low(SEQ, 128),
-    pack=wide(8, 24, 128), near=wide(8, 24, 128), stage=low(192, 128),
+    pack=wide(8, 24, 128), near=wide(8, 24, 128), stage=low(160, 128),
     out_mine=wide(8, D), out_other=wide(8, D), out_rows=low(64, 512),
     gate=low(4, 4, 4, 64, 512), up=low(4, 4, 4, 64, 512), down=low(4, 4, 4, 32, D),
     shares=wide(TOK, 128), order_row=wide(32, SEQ), places=low(SEQ, 4 * SLOTS),
-    rows=low(4 * SLOTS, D), low_grad=low(4 * SLOTS, D), made=low(SLOTS, D), slot_grad=low(4 * SLOTS, D),
+    rows=low(4 * SLOTS, D), low_grad=low(4 * SLOTS, D), slot_grad=low(4 * SLOTS, D),
     gate_grad=wide(8, 8, 128), gate_back=wide(8, 8, 128),
     product=low(SLOTS, 512),
     wide1=low(4, 2, 2, 2, 64, 512), wide2=low(4, 2, 2, 4, 64, 512), wide3=low(4, 2, 2, 32, 512),
@@ -994,10 +1033,10 @@
     residual_grad=wide(TOK, D), branch=low(TOK, D), branch_part=low(SEQ, 128), attended_grad=low(TOK, D),
     attended_back=low(SEQ, 128), attended_all=low(SEQ, D), key_grad=wide(SEQ, 128), value_grad=wide(SEQ, 128),
     qkv_grad=low(SEQ, 256), extra=wide(8, 128),
-    x_sems=DMA((5,)), n_sems=DMA((5,)), g_sems=DMA((5,)), h_sems=DMA((5,)), t_sems=DMA((5,)), p_sems=DMA((2,)),
+    x_sems=DMA((8,)), n_sems=DMA((8,)), g_sems=DMA((8,)), h_sems=DMA((8,)), t_sems=DMA((8,)), p_sems=DMA((2,)),
     c_sems=DMA((2,)), b_sems=DMA((2,)), d_sems=DMA((2,)), l_sems=DMA((2,)), w_sems=DMA((2, 4)),
     o_sems=DMA((2, 4)), a_sems=DMA((2,)), q_sems=DMA((6,)), e_sems=DMA((4, 2, 4, 2)), f_sems=DMA((4, 2)),
-    s_sems=DMA((3, 6)), load=DMA((5,)), store=DMA((4, 3)),
+    s_sems=DMA((3, 6)), load=DMA((5,)), keep=DMA((3,)), store=DMA((4, 3)),
 )
 
 
@@ -1014,6 +1053,7 @@
 
     def kernel(*refs):
         r = SimpleNamespace(**dict(zip(names, refs)))
+        r.x_all = r.rows.at[0:SEQ]
         r.hidden_one, r.w_out_all = r.slot_grad.at[0:SEQ], r.places.at[:, 0:D]
         r.attended_head = r.qkv_grad.at[:, 128:256]
         r.extra_all, r.corner = r.key_grad, r.value_grad.at[0:128]

time: 162 us -> 158 us (0.975)
  Pallas kernels: 161 us -> 157 us
    pallas_call x1, Pallas kernels: 157 us -> 153 us  [layer(): pl.pallas_call(kernel, out_shape=[jax.ShapeDtypeStruct(OUTS[n].shape, OUT...]
where the time goes in v4:
time: 158 us
  Pallas kernels  157 us (99%)
    pallas_call x1, Pallas kernels, layer(): pl.pallas_call(kernel, out_shape=[jax.ShapeDtypeStruct(OUTS[n].shape, OUT...  153 us
    pallas_call x1, Pallas kernels, handed_on(): pl.pallas_call(hand_on, out_shape=small + [jax.ShapeDtypeStruct(a.shape,...  3.91 us

profile of v4, /device:TPU:1, one launch (start us, length us, event | category | flops | bytes accessed | tf_op | source)
XLA Modules:
  0.0 157.8 jit_solution(1492664063727078961)
XLA Ops:
  0.6 153.1 %layer.1 = (bf16[128,1024]{1,0:T(8,128)(2,1)}, f32[128,1024]{1,0:T(8,128)}, f32[8,1024]{1,0:T(8,128)}, f32[8,512]{1,0:T(8,128)}, f32[8,512]{1,0:T(8,128)}, /*ind...) custom-call(bf16[128,1024]{1,0:T(8,128)(2,1)} %refs_0_.1, ...), custom_call_target="tpu_custom_call" | custom-call | tf_op jit(solution)/shard_map/layer/pallas_call | solution.py:1063
  153.7 3.9 %hand_on.1 = (f32[8,32]{1,0:T(8,128)}, f32[1,8]{1,0:T(1,128)}, f32[1,8]{1,0:T(1,128)}, bf16[128,1024]{1,0:T(8,128)(2,1)}, f32[128,1024]{1,0:T(8,128)}, /*index=5...) custom-call(f32[8,128]{1,0:T(8,128)} %get-tuple-element.34.refs_0_, ...), custom_call_target="tpu_custom_call" | custom-call | tf_op jit(solution)/shard_map/hand_on/pallas_call | solution.py:1104
